TPU v7x, 256 devices: a whole 4x4x8 slice. The times are simulated.
256 devices in a mesh: seq: 32 (over x, y, core), chan: 8 (over z).
Axes of the slice: x: 4, y: 4, z: 8, core: 2. Of those that a mesh axis runs over, the one named last changes fastest.
Arguments:
- query_act: bfloat16 [16384, 1024], P('seq', 'chan'), may hold values from -6 to 6
- key_act: bfloat16 [16384, 1024], P('seq', 'chan'), may hold values from -6 to 6
- value_act: bfloat16 [16384, 1024], P('seq', 'chan'), may hold values from -6 to 6
- out_grad: bfloat16 [16384, 1024], P('seq', 'chan'), may hold values from -6 to 6
- filter_in: float32 [16, 64], replicated, may hold values from -1.5 to 1.5
- filter_mid: float32 [64, 64], replicated, may hold values from -0.75 to 0.75
- filter_out: float32 [64, 1024], P(None, 'chan'), may hold values from -0.75 to 0.75
- decay_rate: float32 [1024], P('chan'), may hold values from 1.5258789e-05 to 0.0333333333
- skip_gain: float32 [1024], P('chan'), may hold values from -4 to 4
Outputs:
- output: bfloat16 [16384, 1024], P('seq', 'chan')
- grad_query: bfloat16 [16384, 1024], P('seq', 'chan')
- grad_key: bfloat16 [16384, 1024], P('seq', 'chan')
- grad_value: bfloat16 [16384, 1024], P('seq', 'chan')
- grad_filter_in: float32 [16, 64], replicated
- grad_filter_mid: float32 [64, 64], replicated
- grad_filter_out: float32 [64, 1024], P(None, 'chan')
- grad_decay: float32 [1024], P('chan')
- grad_skip: float32 [1024], P('chan')
All inputs are finite; a program needn't handle non-finite values.
Results may differ from a plain program's by a relative error of at most 0.0014.
Values sent between devices are 32-bit elements; how exact they have to be, the bound alone decides.
No kernel may reach another device: no remote copies, remote signals or barrier semaphores. Data moves between devices by JAX's collectives and lax.ppermute only.
A program may use at most 128 MiB of HBM per device.

v0:
```python
import math

import jax
import jax.numpy as jnp
from jax import lax
from jax.sharding import PartitionSpec as P

HIGHEST = lax.Precision.HIGHEST


def from_partner(x, axis, distance):
    return lax.ppermute(x, axis, [(i, i ^ 1 << distance) for i in range(lax.axis_size(axis))])


def positional_features(positions, seq_total):
    ramp_col = positions.astype(jnp.float32) / seq_total
    sine_cols = []
    cosine_cols = []
    for level_id in range(7):
        factor = max(1, seq_total // 4 // 4 ** (6 - level_id))
        turns = factor * (positions % (seq_total // factor))
        phase = turns.astype(jnp.float32) * (2.0 * math.pi / seq_total)
        sine_cols.append(jnp.sin(phase))
        cosine_cols.append(jnp.cos(phase))
    return jnp.stack([ramp_col] + sine_cols + cosine_cols + [jnp.ones_like(ramp_col)], axis=1)


def filter_values(filter_in, filter_mid, filter_out, decay_rate, positions, seq_total):
    feature_rows = positional_features(positions, seq_total)
    hidden = jnp.sin(
        jnp.dot(feature_rows, filter_in, precision=HIGHEST, preferred_element_type=jnp.float32)
    )
    hidden = jnp.sin(
        jnp.dot(hidden, filter_mid, precision=HIGHEST, preferred_element_type=jnp.float32)
    )
    shaped = jnp.dot(hidden, filter_out, precision=HIGHEST, preferred_element_type=jnp.float32)
    time_col = positions.astype(jnp.float32)[:, None]
    window = (
        jnp.exp(-decay_rate[None, :] * time_col) * jnp.sqrt(decay_rate + 1.0 / seq_total)[None, :]
    )
    return shaped * window


def dft_table(length_n, sign_v):
    index_row = jnp.arange(length_n, dtype=jnp.int32)
    turns = index_row[:, None] * index_row[None, :] % length_n
    phase = turns.astype(jnp.float32) * (sign_v * 2.0 * math.pi / length_n)
    return (jnp.cos(phase), jnp.sin(phase))


def complex_apply(form, table_re, table_im, real_part, imag_part):

    def product_of(table, field):
        return jnp.einsum(form, table, field, precision=HIGHEST, preferred_element_type=jnp.float32)

    return (
        product_of(table_re, real_part) - product_of(table_im, imag_part),
        product_of(table_re, imag_part) + product_of(table_im, real_part),
    )


def rotate(real_part, imag_part, cosine, sine):
    return (real_part * cosine - imag_part * sine, real_part * sine + imag_part * cosine)


def reverse_bits(seq_place, axis_len):
    level_count = axis_len.bit_length() - 1
    flipped = jnp.zeros((), jnp.int32)
    for level_id in range(level_count):
        flipped = flipped + seq_place // 2**level_id % 2 * 2 ** (level_count - 1 - level_id)
    return flipped


def swap_forward(real_part, imag_part, seq_place, axis_len):
    level_count = axis_len.bit_length() - 1
    for level_id in range(level_count - 1, -1, -1):
        half_span = 2**level_id
        partner = from_partner(jnp.stack([real_part, imag_part]), "seq", level_id)
        is_upper = seq_place // half_span % 2 == 1
        phase = (seq_place % half_span).astype(jnp.float32) * (-math.pi / half_span)
        diff_re, diff_im = rotate(
            partner[0] - real_part, partner[1] - imag_part, jnp.cos(phase), jnp.sin(phase)
        )
        real_part = jnp.where(is_upper, diff_re, real_part + partner[0])
        imag_part = jnp.where(is_upper, diff_im, imag_part + partner[1])
    return (real_part, imag_part)


def swap_inverse(real_part, imag_part, seq_place, axis_len):
    level_count = axis_len.bit_length() - 1
    for level_id in range(level_count):
        half_span = 2**level_id
        partner = from_partner(jnp.stack([real_part, imag_part]), "seq", level_id)
        is_upper = seq_place // half_span % 2 == 1
        phase = (seq_place % half_span).astype(jnp.float32) * (math.pi / half_span)
        cosine = jnp.cos(phase)
        sine = jnp.sin(phase)
        other_re, other_im = rotate(partner[0], partner[1], cosine, sine)
        self_re, self_im = rotate(real_part, imag_part, cosine, sine)
        real_part = jnp.where(is_upper, partner[0] - self_re, real_part + other_re)
        imag_part = jnp.where(is_upper, partner[1] - self_im, imag_part + other_im)
    return (real_part, imag_part)


def freq_twiddle(local_len, freq_index, seq_total, sign_v):
    row_ids = jnp.arange(local_len, dtype=jnp.int32)
    freq_ids = 2 * freq_index + jnp.arange(2, dtype=jnp.int32)
    turns = freq_ids[:, None] * row_ids[None, :] % (2 * seq_total)
    phase = turns.astype(jnp.float32) * (sign_v * math.pi / seq_total)
    return (jnp.cos(phase)[None, :, :, None], jnp.sin(phase)[None, :, :, None])


def local_forward(real_part, imag_part, freq_index, seq_total):
    local_len = real_part.shape[2]
    cosine, sine = freq_twiddle(local_len, freq_index, seq_total, -1.0)
    real_part, imag_part = rotate(real_part, imag_part, cosine, sine)
    table_re, table_im = dft_table(local_len, -1.0)
    return complex_apply("kr,nerc->nekc", table_re, table_im, real_part, imag_part)


def local_inverse(real_part, imag_part, freq_index, seq_total):
    local_len = real_part.shape[2]
    table_re, table_im = dft_table(local_len, 1.0)
    real_part, imag_part = complex_apply("kr,nerc->nekc", table_re, table_im, real_part, imag_part)
    cosine, sine = freq_twiddle(local_len, freq_index, seq_total, 1.0)
    return rotate(real_part, imag_part, cosine, sine)


def combine_halves(real_part, imag_part, seq_place, axis_len, seq_total):
    phase = seq_place.astype(jnp.float32) * (math.pi / axis_len)
    cosine = jnp.cos(phase)
    sine = jnp.sin(phase)
    out_re = real_part[:, 0] + real_part[:, 1] * cosine - imag_part[:, 1] * sine
    out_im = imag_part[:, 0] + real_part[:, 1] * sine + imag_part[:, 1] * cosine
    scale_n = 0.5 / seq_total
    return (out_re * scale_n, out_im * scale_n)


def spectra_products(spec_re, spec_im):
    gated_re, gated_im = (spec_re[0], spec_im[0])
    incoming_re, incoming_im = (spec_re[1], spec_im[1])
    filt_sre, filt_sim = (spec_re[2], spec_im[2])
    prod_re = gated_re * filt_sre - gated_im * filt_sim
    prod_im = gated_re * filt_sim + gated_im * filt_sre
    corr_re = filt_sre * incoming_re + filt_sim * incoming_im
    corr_im = filt_sre * incoming_im - filt_sim * incoming_re
    first_re = prod_re - corr_im
    first_im = prod_im + corr_re
    second_re = incoming_re * gated_re + incoming_im * gated_im
    second_im = incoming_im * gated_re - incoming_re * gated_im
    return (jnp.stack([first_re, second_re]), jnp.stack([first_im, second_im]))


def body(
    query_act,
    key_act,
    value_act,
    out_grad,
    filter_in,
    filter_mid,
    filter_out,
    decay_rate,
    skip_gain,
):
    axis_len = lax.axis_size("seq")
    seq_place = lax.axis_index("seq")
    local_len = query_act.shape[0]
    seq_total = axis_len * local_len
    positions = seq_place * local_len + jnp.arange(local_len, dtype=jnp.int32)
    query_wide = query_act.astype(jnp.float32)
    key_wide = key_act.astype(jnp.float32)
    value_wide = value_act.astype(jnp.float32)
    grad_wide = out_grad.astype(jnp.float32)
    gated = key_wide * value_wide
    incoming = grad_wide * query_wide

    def make_filter(w_first, w_second, w_third, rates):
        return filter_values(w_first, w_second, w_third, rates, positions, seq_total)

    filter_vals, pullback = jax.vjp(make_filter, filter_in, filter_mid, filter_out, decay_rate)
    freq_index = reverse_bits(seq_place, axis_len)
    fields = jnp.stack([gated, incoming, filter_vals])
    phase = seq_place.astype(jnp.float32) * (math.pi / axis_len)
    real_part = jnp.stack([fields, fields * jnp.cos(phase)], axis=1)
    imag_part = jnp.stack([jnp.zeros_like(fields), -fields * jnp.sin(phase)], axis=1)
    real_part, imag_part = swap_forward(real_part, imag_part, seq_place, axis_len)
    spec_re, spec_im = local_forward(real_part, imag_part, freq_index, seq_total)
    inv_re, inv_im = spectra_products(spec_re, spec_im)
    inv_re, inv_im = local_inverse(inv_re, inv_im, freq_index, seq_total)
    inv_re, inv_im = swap_inverse(inv_re, inv_im, seq_place, axis_len)
    field_re, field_im = combine_halves(inv_re, inv_im, seq_place, axis_len, seq_total)
    conv_field = field_re[0]
    back_field = field_im[0]
    grad_first, grad_second, grad_third, grad_rates = pullback(field_re[1])
    mixed_field = conv_field + skip_gain[None, :] * gated
    output = (query_wide * mixed_field).astype(jnp.bfloat16)
    grad_query = (grad_wide * mixed_field).astype(jnp.bfloat16)
    dgated = back_field + skip_gain[None, :] * incoming
    grad_key = (dgated * value_wide).astype(jnp.bfloat16)
    grad_value = (dgated * key_wide).astype(jnp.bfloat16)
    grad_skip = jnp.sum(incoming * gated, axis=0)
    grad_first, grad_second = lax.psum((grad_first, grad_second), ("seq", "chan"))
    grad_third, grad_rates, grad_skip = lax.psum((grad_third, grad_rates, grad_skip), "seq")
    return (
        output,
        grad_query,
        grad_key,
        grad_value,
        grad_first,
        grad_second,
        grad_third,
        grad_rates,
        grad_skip,
    )


def solution(mesh):
    placed = (
        P("seq", "chan"),
        P("seq", "chan"),
        P("seq", "chan"),
        P("seq", "chan"),
        P(),
        P(),
        P(None, "chan"),
        P("chan"),
        P("chan"),
    )
    return jax.shard_map(
        body,
        mesh=mesh,
        in_specs=placed,
        out_specs=(
            P("seq", "chan"),
            P("seq", "chan"),
            P("seq", "chan"),
            P("seq", "chan"),
            P(),
            P(),
            P(None, "chan"),
            P("chan"),
            P("chan"),
        ),
        check_vma=False,
    )
```

profile of v0, /device:TPU:32, one launch (start us, length us, event | category | flops | bytes accessed | tf_op | source)
XLA Modules:
  0.0 794.4 jit_solution(16584058516358421628)
XLA Ops:
  1.9 0.7 fusion.136
  2.7 2.0 fusion.137
  4.7 2.1 fusion.138
  6.8 0.6 fusion.139
  8.0 0.7 copy-done.9
  8.7 0.3 copy-done.8
  9.0 0.7 copy-done.7
  10.0 3.1 collective-permute-start
  13.2 68.3 %collective-permute-done = f32[2,3,2,512,128]{4,3,2,1,0:T(8,128)} collective-permute-done((f32[2,3,2,512,128]{4,3,2,1,0:T(8,128)S(1)}, f32[2,3,2,512,128]{4,3,2,1,0:T(8,128)}, u32[]{:S(2)}, u32[]{:S(2)}) %collective-permute-start) | collective-permute-done | bytes 3145760 | tf_op jit(solution)/shard_map/ppermute | solution.py:12
  81.5 3.1 add_select_fusion.9
  84.6 1.8 pad_maximum_fusion.1
  86.5 1.5 collective-permute-start.1
  88.1 67.6 %collective-permute-done.1 = f32[2,3,2,512,128]{4,3,2,1,0:T(8,128)} collective-permute-done((f32[2,3,2,512,128]{4,3,2,1,0:T(8,128)}, f32[2,3,2,512,128]{4,3,2,1,0:T(8,128)}, u32[]{:S(2)}, u32[]{:S(2)}) %collective-permute-start.1) | collective-permute-done | bytes 3145760 | tf_op jit(solution)/shard_map/ppermute | solution.py:12
  155.8 2.5 add_select_fusion.8
  158.6 0.9 copy-done.1
  159.5 0.5 copy-done.2
  160.0 3.2 collective-permute-start.2
  163.3 66.3 %collective-permute-done.2 = f32[2,3,2,512,128]{4,3,2,1,0:T(8,128)} collective-permute-done((f32[2,3,2,512,128]{4,3,2,1,0:T(8,128)S(1)}, f32[2,3,2,512,128]{4,3,2,1,0:T(8,128)}, u32[]{:S(2)}, u32[]{:S(2)}) %collective-permute-start.2) | collective-permute-done | bytes 3145760 | tf_op jit(solution)/shard_map/ppermute | solution.py:12
  229.6 3.5 add_select_fusion.6
  233.1 1.8 pad_maximum_fusion.3
  235.0 1.6 collective-permute-start.3
  236.7 65.7 %collective-permute-done.3 = f32[2,3,2,512,128]{4,3,2,1,0:T(8,128)} collective-permute-done((f32[2,3,2,512,128]{4,3,2,1,0:T(8,128)}, f32[2,3,2,512,128]{4,3,2,1,0:T(8,128)}, u32[]{:S(2)}, u32[]{:S(2)}) %collective-permute-start.3) | collective-permute-done | bytes 3145760 | tf_op jit(solution)/shard_map/ppermute | solution.py:12
  302.4 2.5 add_select_fusion.4
  305.2 0.9 copy-done.3
  306.1 0.5 copy-done.4
  306.6 0.4 collective-permute-start.4
  307.3 5.5 collective-permute-done.4
  312.9 3.3 add_select_fusion.2
  316.2 9.0 %fusion.25 = f32[3,2,128,512]{3,2,1,0:T(8,128)S(1)} fusion(f32[3,2,512,128]{3,2,1,0:T(8,128)S(1)} %get-tuple-element.19, f32[3,2,512,128]{3,2,1,0:T(8,128)S(1)} %get-tuple-element.18, f32[2,512]{1,0:T(2,128)S(1)} %get-tuple-element.65, f32[2,512]{1,0:T(2,128)S(1)} %get-tuple-element.66), kind=kOutput, calls=%fused_computation.86 | convolution fusion | flops 2420768768 | bytes 4726784 | tf_op jit(solution)/shard_map/kr,nerc->nekc/dot_general | solution.py:54
  325.3 9.2 %fusion.23 = f32[3,2,128,512]{3,2,1,0:T(8,128)S(1)} fusion(f32[3,2,512,128]{3,2,1,0:T(8,128)S(1)} %get-tuple-element.19, f32[3,2,512,128]{3,2,1,0:T(8,128)S(1)} %get-tuple-element.18, f32[2,512]{1,0:T(2,128)S(1)} %get-tuple-element.65, f32[2,512]{1,0:T(2,128)S(1)} %get-tuple-element.66), kind=kOutput, calls=%fused_computation.84 | convolution fusion | flops 2420768768 | bytes 4726784 | tf_op jit(solution)/shard_map/kr,nerc->nekc/dot_general | solution.py:54
  334.5 9.2 %subtract_bitcast_fusion = f32[3,2,512,128]{2,3,1,0:T(8,128)S(1)} fusion(f32[3,2,128,512]{3,2,1,0:T(8,128)S(1)} %fusion.25, f32[3,2,512,128]{3,2,1,0:T(8,128)S(1)} %get-tuple-element.19, f32[3,2,512,128]{3,2,1,0:T(8,128)S(1)} %get-tuple-element.18, f32[2,512]{1,0:T(2,128)S(1)} %get-tuple-element.65, f32[2,512]{1,0:T(2,128)S(1)} %get-tuple-element.66), kind=kOutput, calls=%fused_computation.26 | convolution fusion | flops 2421161984 | bytes 6299648 | tf_op jit(solution)/shard_map/kr,nerc->nekc/dot_general | solution.py:54
  343.7 9.4 %add_bitcast_fusion = f32[3,2,512,128]{2,3,1,0:T(8,128)S(1)} fusion(f32[3,2,128,512]{3,2,1,0:T(8,128)S(1)} %fusion.23, f32[3,2,512,128]{3,2,1,0:T(8,128)S(1)} %get-tuple-element.19, f32[3,2,512,128]{3,2,1,0:T(8,128)S(1)} %get-tuple-element.18, f32[2,512]{1,0:T(2,128)S(1)} %get-tuple-element.65, f32[2,512]{1,0:T(2,128)S(1)} %get-tuple-element.66), kind=kOutput, calls=%fused_computation.25 | convolution fusion | flops 2421161984 | bytes 6299648 | tf_op jit(solution)/shard_map/kr,nerc->nekc/dot_general | solution.py:54
  353.4 0.4 subtract_subtract_fusion
  353.8 5.6 fusion.19
  359.4 5.8 fusion.21
  365.2 5.7 convolution_subtract_fusion
  370.9 6.2 multiply_subtract_fusion.1
  377.5 4.0 collective-permute-done.5
  381.5 0.5 fusion.12
  382.0 1.5 pad_maximum_fusion.6
  383.5 1.6 collective-permute-start.6
  385.2 46.2 %collective-permute-done.6 = f32[2,2,2,512,128]{4,3,2,1,0:T(8,128)} collective-permute-done((f32[2,2,2,512,128]{4,3,2,1,0:T(8,128)}, f32[2,2,2,512,128]{4,3,2,1,0:T(8,128)}, u32[]{:S(2)}, u32[]{:S(2)}) %collective-permute-start.6) | collective-permute-done | bytes 2097184 | tf_op jit(solution)/shard_map/ppermute | solution.py:12
  431.4 2.2 add_select_fusion.16
  433.8 0.8 copy-done.5
  434.6 3.2 collective-permute-start.7
  437.9 45.1 %collective-permute-done.7 = f32[2,2,2,512,128]{4,3,2,1,0:T(8,128)} collective-permute-done((f32[2,2,2,512,128]{4,3,2,1,0:T(8,128)S(1)}, f32[2,2,2,512,128]{4,3,2,1,0:T(8,128)}, u32[]{:S(2)}, u32[]{:S(2)}) %collective-permute-start.7) | collective-permute-done | bytes 2097184 | tf_op jit(solution)/shard_map/ppermute | solution.py:12
  483.0 2.5 add_select_fusion.14
  485.5 1.5 pad_maximum_fusion.8
  487.0 1.5 collective-permute-start.8
  488.6 44.6 %collective-permute-done.8 = f32[2,2,2,512,128]{4,3,2,1,0:T(8,128)} collective-permute-done((f32[2,2,2,512,128]{4,3,2,1,0:T(8,128)}, f32[2,2,2,512,128]{4,3,2,1,0:T(8,128)}, u32[]{:S(2)}, u32[]{:S(2)}) %collective-permute-start.8) | collective-permute-done | bytes 2097184 | tf_op jit(solution)/shard_map/ppermute | solution.py:12
  533.2 2.2 add_select_fusion.12
  535.4 1.6 pad_maximum_fusion.9
  537.0 3.0 collective-permute-start.9
  540.2 43.5 %collective-permute-done.9 = f32[2,2,2,512,128]{4,3,2,1,0:T(8,128)S(1)} collective-permute-done((f32[2,2,2,512,128]{4,3,2,1,0:T(8,128)}, f32[2,2,2,512,128]{4,3,2,1,0:T(8,128)S(1)}, u32[]{:S(2)}, u32[]{:S(2)}) %collective-permute-start.9) | collective-permute-done | bytes 2097184 | tf_op jit(solution)/shard_map/ppermute | solution.py:12
  583.7 1.8 add_select_fusion.10
  585.8 0.6 copy-done.15
  586.5 0.4 fusion.71
  586.9 0.9 convolution_multiply_fusion.1
  587.8 0.3 fusion.141
  588.1 0.6 convolution_multiply_fusion
  588.9 1.1 multiply_reduce_fusion.1
  590.0 0.7 fusion.54
  590.7 78.0 %all-reduce.1 = (f32[16,64]{1,0:T(8,128)}, f32[64,64]{1,0:T(8,128)}) all-reduce(f32[16,64]{1,0:T(8,128)S(1)} %fusion.140, f32[64,64]{1,0:T(8,128)S(1)} %fusion.141), channel_id=1, replica_groups=mesh['seq'=32,'chan'=8] {'seq','chan'}, use_global_device_ids=true, to_apply=%region_0.1 | all-reduce | flops 5120 | bytes 40960 | tf_op jit(solution)/shard_map/psum | solution.py:202
  668.7 125.5 %all-reduce.2 = (f32[64,128]{1,0:T(8,128)}, f32[128]{0:T(128)}, f32[128]{0:T(128)}) all-reduce(f32[64,128]{1,0:T(8,128)S(1)} %fusion.71, f32[128]{0:T(128)S(1)} %fusion.97, f32[128]{0:T(128)S(1)} %get-tuple-element.52), channel_id=1, replica_groups=mesh['seq'=32,'chan'=8] {'seq'}, use_global_device_ids=true, to_apply=%region_2.3 | all-reduce | flops 8448 | bytes 67584 | tf_op jit(solution)/shard_map/psum | solution.py:203
  (74 shorter events, 3.8 us)
Async XLA Ops:
  0.6 6.2 copy-start
  0.7 6.9 copy-start.16
  0.7 6.9 copy-start.10
  0.7 6.9 copy-start.20
  0.7 6.9 copy-start.18
  4.7 2.1 copy-start.12
  6.8 1.0 copy-start.14
  7.8 0.9 copy-start.9
  7.8 1.1 copy-start.8
  8.7 0.9 copy-start.7
  10.0 71.5 %collective-permute-start = (f32[2,3,2,512,128]{4,3,2,1,0:T(8,128)S(1)}, f32[2,3,2,512,128]{4,3,2,1,0:T(8,128)}, u32[]{:S(2)}, u32[]{:S(2)}) collective-permute-start(f32[2,3,2,512,128]{4,3,2,1,0:T(8,128)S(1)} %pad_maximum_fusion), channel_id=1, source_target_pairs={{0,128},{8,136},{16,144},{24,152},{32,160},{40,168},{48,176},{56,1... | collective-permute-start | bytes 9437192 | tf_op jit(solution)/shard_map/ppermute | solution.py:12
  86.5 69.3 %collective-permute-start.1 = (f32[2,3,2,512,128]{4,3,2,1,0:T(8,128)}, f32[2,3,2,512,128]{4,3,2,1,0:T(8,128)}, u32[]{:S(2)}, u32[]{:S(2)}) collective-permute-start(f32[2,3,2,512,128]{4,3,2,1,0:T(8,128)} %pad_maximum_fusion.1), channel_id=1, source_target_pairs={{0,64},{8,72},{16,80},{24,88},{32,96},{40,104},{48,112},{56,120},{... | collective-permute-start | bytes 9437192 | tf_op jit(solution)/shard_map/ppermute | solution.py:12
  158.3 1.2 copy-start.1
  158.3 1.7 copy-start.2
  160.0 69.7 %collective-permute-start.2 = (f32[2,3,2,512,128]{4,3,2,1,0:T(8,128)S(1)}, f32[2,3,2,512,128]{4,3,2,1,0:T(8,128)}, u32[]{:S(2)}, u32[]{:S(2)}) collective-permute-start(f32[2,3,2,512,128]{4,3,2,1,0:T(8,128)S(1)} %pad_maximum_fusion.2), channel_id=1, source_target_pairs={{0,32},{8,40},{16,48},{24,56},{32,0},{40,8},{48,16},{56,24},{64,96... | collective-permute-start | bytes 9437192 | tf_op jit(solution)/shard_map/ppermute | solution.py:12
  235.0 67.4 %collective-permute-start.3 = (f32[2,3,2,512,128]{4,3,2,1,0:T(8,128)}, f32[2,3,2,512,128]{4,3,2,1,0:T(8,128)}, u32[]{:S(2)}, u32[]{:S(2)}) collective-permute-start(f32[2,3,2,512,128]{4,3,2,1,0:T(8,128)} %pad_maximum_fusion.3), channel_id=1, source_target_pairs={{0,16},{8,24},{16,0},{24,8},{32,48},{40,56},{48,32},{56,40},{64,80... | collective-permute-start | bytes 9437192 | tf_op jit(solution)/shard_map/ppermute | solution.py:12
  305.0 1.2 copy-start.3
  305.0 1.7 copy-start.4
  306.6 6.2 collective-permute-start.4
  377.2 4.2 collective-permute-start.5
  383.5 48.0 %collective-permute-start.6 = (f32[2,2,2,512,128]{4,3,2,1,0:T(8,128)}, f32[2,2,2,512,128]{4,3,2,1,0:T(8,128)}, u32[]{:S(2)}, u32[]{:S(2)}) collective-permute-start(f32[2,2,2,512,128]{4,3,2,1,0:T(8,128)} %pad_maximum_fusion.6), channel_id=1, source_target_pairs={{0,16},{8,24},{16,0},{24,8},{32,48},{40,56},{48,32},{56,40},{64,80... | collective-permute-start | bytes 6291464 | tf_op jit(solution)/shard_map/ppermute | solution.py:12
  433.6 1.0 copy-start.5
  434.6 48.5 %collective-permute-start.7 = (f32[2,2,2,512,128]{4,3,2,1,0:T(8,128)S(1)}, f32[2,2,2,512,128]{4,3,2,1,0:T(8,128)}, u32[]{:S(2)}, u32[]{:S(2)}) collective-permute-start(f32[2,2,2,512,128]{4,3,2,1,0:T(8,128)S(1)} %pad_maximum_fusion.7), channel_id=1, source_target_pairs={{0,32},{8,40},{16,48},{24,56},{32,0},{40,8},{48,16},{56,24},{64,96... | collective-permute-start | bytes 6291464 | tf_op jit(solution)/shard_map/ppermute | solution.py:12
  487.0 46.2 %collective-permute-start.8 = (f32[2,2,2,512,128]{4,3,2,1,0:T(8,128)}, f32[2,2,2,512,128]{4,3,2,1,0:T(8,128)}, u32[]{:S(2)}, u32[]{:S(2)}) collective-permute-start(f32[2,2,2,512,128]{4,3,2,1,0:T(8,128)} %pad_maximum_fusion.8), channel_id=1, source_target_pairs={{0,64},{8,72},{16,80},{24,88},{32,96},{40,104},{48,112},{56,120},{... | collective-permute-start | bytes 6291464 | tf_op jit(solution)/shard_map/ppermute | solution.py:12
  535.4 1.7 copy-start.6
  537.0 46.7 %collective-permute-start.9 = (f32[2,2,2,512,128]{4,3,2,1,0:T(8,128)}, f32[2,2,2,512,128]{4,3,2,1,0:T(8,128)S(1)}, u32[]{:S(2)}, u32[]{:S(2)}) collective-permute-start(f32[2,2,2,512,128]{4,3,2,1,0:T(8,128)} %pad_maximum_fusion.9), channel_id=1, source_target_pairs={{0,128},{8,136},{16,144},{24,152},{32,160},{40,168},{48,176},{56,1... | collective-permute-start | bytes 6291464 | tf_op jit(solution)/shard_map/ppermute | solution.py:12
  585.6 0.9 copy-start.15
  585.6 1.3 copy-start.22
  585.6 2.2 copy-start.13
  585.6 2.4 copy-start.23
  585.6 2.4 copy-start.24
  585.8 3.1 copy-start.11
  585.8 3.1 copy-start.17
  585.8 3.1 copy-start.19
  585.8 3.1 copy-start.21
  585.8 3.1 copy-start.25
  588.9 1.8 copy-start.26
where the time goes:
time: 802 us; the launch traced here: 794 us
  waiting for transfers between devices  457 us (57%)
  blocking collectives  203 us (25%)
  matrix products  67.2 us (8%)
  other arithmetic  38.2 us (5%)
  starting transfers between devices  19.3 us (2%)
    ppermute x10, waiting for transfers between devices, from_partner(): lax.ppermute(x, axis, [(i, i ^ 1 << distance) for i in range(lax.axis_siz...  457 us
    psum x1, blocking collectives, body(): lax.psum((grad_third, grad_rates, grad_skip), 'seq')  125 us
    psum x1, blocking collectives, body(): lax.psum((grad_first, grad_second), ('seq', 'chan'))  78 us
    dot_general x8, matrix products, product_of(): jnp.einsum(form, table, field, precision=HIGHEST, preferred_element_type=...  60.2 us
    ppermute x10, starting transfers between devices, from_partner(): lax.ppermute(x, axis, [(i, i ^ 1 << distance) for i in range(lax.axis_siz...  19.3 us
  transfers between devices with their start and end apart: 10, of which 10 were waited for; matrix products, arithmetic and copies ran while one was open for 0% of the time, Pallas kernels for 0%

commit v1 on v0

v1 whole, which is shorter than its diff:
```python
import functools
import math

import jax
import jax.numpy as jnp
import ml_dtypes
import numpy as np
from jax import lax
from jax.experimental import pallas as pl
from jax.experimental.pallas import tpu as pltpu
from jax.sharding import PartitionSpec as P

F32 = jnp.float32
BF16 = jnp.bfloat16
LENGTH = 16384
SEQ = 32
ROWS = 512
SIDE = 128
OWN = 4
ORDER = 64
STEP = 2048
PIECE = 256
MIB = 1 << 20


def split_table(table):
    high = table.astype(ml_dtypes.bfloat16)
    low = (table - high.astype(np.float64)).astype(ml_dtypes.bfloat16)
    return high, low


@functools.cache
def time_rows():
    p = np.arange(SIDE)
    return 4 * (p % SEQ) + p // SEQ


@functools.cache
def feature_table():
    t = (time_rows()[:, None] * SIDE + np.arange(SIDE)[None, :]).reshape(-1)
    rows = [t / LENGTH]
    angles = []
    for i in range(7):
        factor = max(1, LENGTH // 4 // 4 ** (6 - i))
        angles.append((factor * t % LENGTH) * (2.0 * math.pi / LENGTH))
    rows += [np.sin(a) for a in angles] + [np.cos(a) for a in angles] + [np.ones(LENGTH)]
    high, low = split_table(np.stack(rows).astype(np.float64))
    return np.concatenate([high, low])


@functools.cache
def transform_tables():
    idx = np.arange(SIDE)
    n1 = time_rows()
    first = np.exp(-2j * np.pi * ((n1[None, :] * idx[:, None] % SIDE) / SIDE + n1[None, :] / (4 * SIDE)))
    twiddle = np.exp(-2j * np.pi * idx[None, :] * (4 * idx[:, None] + 1) / (4 * LENGTH))
    second = np.exp(-2j * np.pi * (idx[:, None] * idx[None, :] % SIDE) / SIDE)
    high, low = split_table(np.concatenate([first.real, first.imag]))
    first_fwd = np.concatenate([high, high, low], axis=1)
    high, low = split_table(np.block([[second.real, second.imag], [-second.imag, second.real]]))
    second_fwd = np.concatenate([high, high, low])
    high, low = split_table(np.block([[second.real, -second.imag], [second.imag, second.real]]))
    second_inv = np.concatenate([high, high, low])
    high, low = split_table(np.concatenate([first.real.T, first.imag.T], axis=1) / LENGTH)
    first_inv = np.concatenate([high, high, low], axis=1)
    twiddle = np.concatenate([twiddle.real, twiddle.imag], axis=1).astype(np.float32)
    return first_fwd, second_fwd, twiddle, second_inv, first_inv


@functools.cache
def turn_polynomials():
    nodes = 0.5 * np.cos(np.pi * (np.arange(400) + 0.5) / 800)
    squares = nodes * nodes

    def fit(values, weight, count):
        basis = np.stack([squares**k for k in range(count)], axis=1)
        return np.linalg.lstsq(basis * weight[:, None], values, rcond=None)[0]

    sine = fit(np.sin(2 * np.pi * nodes), nodes, 6)
    cosine = fit(np.cos(2 * np.pi * nodes), np.ones_like(nodes), 7)
    return [float(c) for c in sine], [float(c) for c in cosine]


def sine_cosine(turns):
    sine, cosine = turn_polynomials()
    part = turns - jnp.round(turns)
    square = part * part
    s = jnp.full_like(square, sine[-1])
    for c in sine[-2::-1]:
        s = s * square + c
    c_out = jnp.full_like(square, cosine[-1])
    for c in cosine[-2::-1]:
        c_out = c_out * square + c
    return s * part, c_out


def halves(x):
    high = x.astype(BF16)
    return high, (x - high.astype(F32)).astype(BF16)


def dot(a, b):
    return jnp.dot(a, b, preferred_element_type=F32)


def dot_nt(a, b, precision=None):
    return lax.dot_general(a, b, (((1,), (1,)), ((), ())), precision=precision, preferred_element_type=F32)


def dot_tn(a, b, precision=None):
    return lax.dot_general(a, b, (((0,), (0,)), ((), ())), precision=precision, preferred_element_type=F32)


def data_left(x, axis):
    high, low = halves(x)
    return jnp.concatenate([high, low, high], axis=axis)


def weight_left(x, axis):
    high, low = halves(x)
    return jnp.concatenate([high, high, low], axis=axis)


def own_channels(place):
    row = lax.broadcasted_iota(jnp.int32, (8, SIDE), 0)
    lane = lax.broadcasted_iota(jnp.int32, (8, SIDE), 1)
    return jnp.where((row < OWN) & (lane == place + SEQ * row), 1.0, 0.0).astype(F32)


def position_grid():
    row = lax.broadcasted_iota(jnp.int32, (SIDE, SIDE), 0)
    lane = lax.broadcasted_iota(jnp.int32, (SIDE, SIDE), 1)
    return (ROWS * (row % SEQ) + SIDE * (row // SEQ) + lane).astype(F32)


def spec(shape, index=None):
    if index is None:
        zeros = (0,) * len(shape)
        return pl.BlockSpec(shape, lambda i: zeros)
    return pl.BlockSpec(shape, index)


def out(shape, dtype=F32):
    return jax.ShapeDtypeStruct(shape, dtype)


def call(kernel, grid, in_specs, out_specs, out_shape, scratch=(), limit=32, flops=1, nbytes=1, interpret=False):
    return pl.pallas_call(
        kernel,
        grid=(grid,),
        in_specs=in_specs,
        out_specs=out_specs,
        out_shape=out_shape,
        scratch_shapes=scratch,
        compiler_params=pltpu.CompilerParams(vmem_limit_bytes=limit * MIB),
        cost_estimate=pl.CostEstimate(flops=flops, bytes_accessed=nbytes, transcendentals=0),
        interpret=interpret,
    )


def send_kernel(query, key, value, grad, sent):
    for h in range(ROWS // SIDE):
        rows = pl.ds(SIDE * h, SIDE)
        gated = key[rows, :].astype(F32) * value[rows, :].astype(F32)
        incoming = grad[rows, :].astype(F32) * query[rows, :].astype(F32)
        for offset, block in ((0, gated.T), (OWN, incoming.T)):
            for c in range(OWN):
                sent[pl.ds(8 * h + offset + c, SEQ, stride=SEQ), :] = block[SEQ * c : SEQ * (c + 1), :]


def receive_kernel(query, key, value, grad, skip, field, output, grad_query, grad_key, grad_value):
    for h in range(ROWS // SIDE):
        rows = pl.ds(SIDE * h, SIDE)
        query_wide = query[rows, :].astype(F32)
        key_wide = key[rows, :].astype(F32)
        value_wide = value[rows, :].astype(F32)
        grad_wide = grad[rows, :].astype(F32)
        conv, back = (
            jnp.concatenate([field[pl.ds(8 * h + offset + c, SEQ, stride=SEQ), :] for c in range(OWN)]).T
            for offset in (0, OWN)
        )
        mixed = conv + skip[...] * (key_wide * value_wide)
        output[rows, :] = (query_wide * mixed).astype(BF16)
        grad_query[rows, :] = (grad_wide * mixed).astype(BF16)
        dgated = back + skip[...] * (grad_wide * query_wide)
        grad_key[rows, :] = (dgated * value_wide).astype(BF16)
        grad_value[rows, :] = (dgated * key_wide).astype(BF16)


def forward_rows(fields, first_fwd, second_fwd, twiddle):
    cos, sin = twiddle[:, :SIDE], twiddle[:, SIDE:]
    turned = []
    for pair in range(0, len(fields), 2):
        stage = dot(first_fwd[...], data_left(jnp.concatenate(fields[pair : pair + 2], axis=1), 0))
        for k in range(2):
            re = stage[:SIDE, SIDE * k : SIDE * (k + 1)]
            im = stage[SIDE:, SIDE * k : SIDE * (k + 1)]
            turned.append(data_left(jnp.concatenate([re * cos - im * sin, re * sin + im * cos], axis=1), 1))
    return dot(jnp.concatenate(turned), second_fwd[...])


def inverse_rows(spectra, first_inv, second_inv, twiddle):
    cos, sin = twiddle[:, :SIDE], twiddle[:, SIDE:]
    stage = dot(jnp.concatenate([data_left(s, 1) for s in spectra]), second_inv[...])
    turned = []
    for k in range(len(spectra)):
        re = stage[SIDE * k : SIDE * (k + 1), :SIDE]
        im = stage[SIDE * k : SIDE * (k + 1), SIDE:]
        turned.append(jnp.concatenate([re * cos + im * sin, im * cos - re * sin]))
    fields = []
    for pair in range(0, len(spectra), 2):
        both = dot(first_inv[...], data_left(jnp.concatenate(turned[pair : pair + 2], axis=1), 0))
        fields += [both[:, :SIDE], both[:, SIDE:]]
    return fields


def filter_kernel(place, features, filter_in, filter_mid, filter_out, decay, first_fwd, second_fwd, twiddle,
                  h1_high, h1_low, cos1, h2_high, h2_low, cos2, spectrum, filt, window, shaped):
    step = pl.program_id(0)
    own = own_channels(place())
    turn = 1.0 / (2.0 * math.pi)
    in_high, in_low = halves(filter_in[...].T * turn)
    weight1 = jnp.concatenate([in_high, in_low, in_high], axis=1)
    weight2 = weight_left(filter_mid[...].T * turn, 1)
    weight3 = weight_left(dot_nt(own, filter_out[...], lax.Precision.HIGHEST), 1)
    pieces = [pl.ds(PIECE * k, PIECE) for k in range(STEP // PIECE)]
    for piece in pieces:
        feature = features[:, piece]
        rows = jnp.concatenate([feature[:16], feature[:16], feature[16:]])
        sine, cosine = sine_cosine(dot(weight1, rows))
        cos1[:, piece] = cosine
        h1_high[:, piece], h1_low[:, piece] = halves(sine)
    for piece in pieces:
        high = h1_high[:, piece]
        sine, cosine = sine_cosine(dot(weight2, jnp.concatenate([high, h1_low[:, piece], high])))
        cos2[:, piece] = cosine
        h2_high[:, piece], h2_low[:, piece] = halves(sine)
    for k, piece in enumerate(pieces):
        high = h2_high[:, piece]
        values = dot(weight3, jnp.concatenate([high, h2_low[:, piece], high]))
        for m in range(PIECE // SIDE):
            row = 8 * (step * (STEP // SIDE) + k * (PIECE // SIDE) + m)
            shaped[pl.ds(pl.multiple_of(row, 8), 8), :] = values[:, SIDE * m : SIDE * (m + 1)]

    @pl.when(step == LENGTH // STEP - 1)
    def _():
        time = position_grid()
        rates = jnp.sum(own * decay[...], axis=1, keepdims=True)
        fields = []
        for c in range(OWN):
            rate = rates[c : c + 1, :]
            window_c = jnp.exp(-rate * time) * jnp.sqrt(rate + 1.0 / LENGTH)
            field = shaped[pl.ds(c, SIDE, stride=8), :] * window_c
            window[pl.ds(SIDE * c, SIDE), :] = window_c
            filt[pl.ds(SIDE * c, SIDE), :] = field
            fields.append(field)
        spectrum[...] = forward_rows(fields, first_fwd, second_fwd, twiddle)


def convolve_kernel(place, field, spectrum, filt, window, decay, first_fwd, second_fwd, twiddle, second_inv, first_inv,
                    sent, dshaped, sums):
    fields = []
    for c in range(OWN):
        for offset in (0, OWN):
            fields.append(
                jnp.concatenate([field[pl.ds(8 * h + offset + c, SEQ, stride=SEQ), :] for h in range(ROWS // SIDE)])
            )
    spectra = forward_rows(fields, first_fwd, second_fwd, twiddle)
    products = []
    for c in range(OWN):
        gated, incoming = (spectra[SIDE * k : SIDE * (k + 1)] for k in (2 * c, 2 * c + 1))
        kernel = spectrum[pl.ds(SIDE * c, SIDE), :]
        gated_re, gated_im = gated[:, :SIDE], gated[:, SIDE:]
        incoming_re, incoming_im = incoming[:, :SIDE], incoming[:, SIDE:]
        kernel_re, kernel_im = kernel[:, :SIDE], kernel[:, SIDE:]
        products.append((
            jnp.concatenate([kernel_re * gated_re - kernel_im * gated_im,
                             kernel_re * gated_im + kernel_im * gated_re], axis=1),
            jnp.concatenate([kernel_re * incoming_re + kernel_im * incoming_im,
                             kernel_re * incoming_im - kernel_im * incoming_re], axis=1),
            jnp.concatenate([gated_re * incoming_re + gated_im * incoming_im,
                             gated_re * incoming_im - gated_im * incoming_re], axis=1),
        ))
    results = inverse_rows([p for c in range(OWN) for p in products[c][:2]] + [products[c][2] for c in range(OWN)],
                           first_inv, second_inv, twiddle)
    time = position_grid()
    rates = jnp.sum(own_channels(place()) * decay[...], axis=1, keepdims=True)
    for c in range(OWN):
        for offset, result in ((0, results[2 * c]), (OWN, results[2 * c + 1])):
            for h in range(ROWS // SIDE):
                sent[pl.ds(8 * h + offset + c, SEQ, stride=SEQ), :] = result[SEQ * h : SEQ * (h + 1), :]
        dfilt = results[2 * OWN + c]
        dshaped[pl.ds(c, SIDE, stride=8), :] = dfilt * window[pl.ds(SIDE * c, SIDE), :]
        dshaped[pl.ds(c + OWN, SIDE, stride=8), :] = jnp.zeros((SIDE, SIDE), F32)
        slope = 0.5 / (rates[c : c + 1, :] + 1.0 / LENGTH) - time
        sums[pl.ds(c, 1), :] = jnp.sum(dfilt * filt[pl.ds(SIDE * c, SIDE), :] * slope, axis=0, keepdims=True)
        sums[pl.ds(c + OWN, 1), :] = jnp.sum(fields[2 * c] * fields[2 * c + 1], axis=0, keepdims=True)


def backward_kernel(place, features, h1_high, h1_low, cos1, h2_high, h2_low, cos2, dshaped, sums, filter_mid, filter_out,
                    grads, grad_mid, grad_in, grad_out, d2_high, d2_low, d1_high, d1_low):
    step = pl.program_id(0)
    own = own_channels(place())
    weight3 = weight_left(dot_nt(filter_out[...], own, lax.Precision.HIGHEST), 1)
    weight2 = weight_left(filter_mid[...], 1)

    @pl.when(step == 0)
    def _():
        grad_mid[...] = jnp.zeros_like(grad_mid)
        grad_in[...] = jnp.zeros_like(grad_in)
        grad_out[...] = jnp.zeros_like(grad_out)

    pieces = [pl.ds(PIECE * k, PIECE) for k in range(STEP // PIECE)]
    shaped_high, shaped_low = halves(jnp.concatenate([dshaped[pl.ds(8 * m, 8), :] for m in range(STEP // SIDE)], axis=1))
    for k, piece in enumerate(pieces):
        part = slice(PIECE * k, PIECE * (k + 1))
        rows = jnp.concatenate([shaped_high[:, part], shaped_low[:, part], shaped_high[:, part]])
        d2_high[:, piece], d2_low[:, piece] = halves(dot(weight3, rows) * cos2[:, piece])
    for piece in pieces:
        high = d2_high[:, piece]
        d1_high[:, piece], d1_low[:, piece] = halves(
            dot(weight2, jnp.concatenate([high, d2_low[:, piece], high])) * cos1[:, piece]
        )
    grad_mid[...] += dot_nt(jnp.concatenate([h1_high[...], h1_low[...]]), jnp.concatenate([d2_high[...], d2_low[...]]))
    grad_in[...] += dot_nt(features[...], jnp.concatenate([d1_high[...], d1_low[...]]))
    grad_out[...] += dot_nt(jnp.concatenate([shaped_high, shaped_low]), jnp.concatenate([h2_high[...], h2_low[...]]))

    @pl.when(step == LENGTH // STEP - 1)
    def _():
        def joined(x, half):
            return x[:half, :ORDER] + (x[:half, ORDER:] + x[half:, :ORDER])

        mid = joined(grad_mid, 64)
        first = joined(grad_in, 16)
        third = joined(grad_out, 8)
        grads[pl.ds(0, 32), :] = jnp.concatenate([mid[:32], mid[32:]], axis=1)
        grads[pl.ds(32, 8), :] = jnp.concatenate([first[:8], first[8:]], axis=1)
        grads[pl.ds(40, 64), :] = dot_tn(third, own, lax.Precision.HIGHEST)
        totals = jnp.sum(sums[...], axis=1, keepdims=True)
        grads[pl.ds(104, 8), :] = jnp.concatenate([
            jnp.sum(own[:OWN] * totals[:OWN], axis=0, keepdims=True),
            jnp.sum(own[:OWN] * totals[OWN:], axis=0, keepdims=True),
            jnp.zeros((6, SIDE), F32),
        ])


def finish_kernel(mine, other, grad_in, grad_mid, grad_out, grad_decay, grad_skip):
    total = mine[...] + other[...]
    grad_mid[pl.ds(0, 32), :] = total[:32, :ORDER]
    grad_mid[pl.ds(32, 32), :] = total[:32, ORDER:]
    grad_in[pl.ds(0, 8), :] = total[32:40, :ORDER]
    grad_in[pl.ds(8, 8), :] = total[32:40, ORDER:]
    grad_out[...] = total[40:104]
    grad_decay[...] = total[104:105]
    grad_skip[...] = total[105:106]


def seq_place():
    return lax.axis_index("seq")


def run_send(query, key, value, grad, **kw):
    block = spec((ROWS, SIDE))
    return call(send_kernel, 1, [block] * 4, spec((1024, SIDE)), out((1024, SIDE)), **kw)(query, key, value, grad)


def run_filter(filter_in, filter_mid, filter_out, decay, place=seq_place, **kw):
    first_fwd, second_fwd, twiddle, _, _ = transform_tables()
    wide = lambda i: (0, i)
    hidden = spec((ORDER, STEP), wide)
    half, full = out((ORDER, LENGTH), BF16), out((ORDER, LENGTH))
    return call(
        functools.partial(filter_kernel, place),
        LENGTH // STEP,
        [spec((32, STEP), wide), spec((16, ORDER)), spec((ORDER, ORDER)), spec((ORDER, SIDE)), spec((1, SIDE)),
         spec((256, 384)), spec((768, 256)), spec((SIDE, 256))],
        [hidden] * 6 + [spec((512, 256)), spec((512, SIDE)), spec((512, SIDE))],
        [half, half, full, half, half, full, out((512, 256)), out((512, SIDE)), out((512, SIDE))],
        scratch=[pltpu.VMEM((1024, SIDE), F32)],
        flops=8 * 10**9, nbytes=20 * MIB, **kw,
    )(feature_table(), filter_in, filter_mid, filter_out, decay, first_fwd, second_fwd, twiddle)


def run_convolve(field, spectrum, filt, window, decay, place=seq_place, **kw):
    first_fwd, second_fwd, twiddle, second_inv, first_inv = transform_tables()
    return call(
        functools.partial(convolve_kernel, place),
        1,
        [spec((1024, SIDE)), spec((512, 256)), spec((512, SIDE)), spec((512, SIDE)), spec((1, SIDE)),
         spec((256, 384)), spec((768, 256)), spec((SIDE, 256)), spec((768, 256)), spec((SIDE, 768))],
        [spec((1024, SIDE)), spec((1024, SIDE)), spec((8, SIDE))],
        [out((1024, SIDE)), out((1024, SIDE)), out((8, SIDE))],
        flops=4 * 10**9, nbytes=4 * MIB, **kw,
    )(field, spectrum, filt, window, decay, first_fwd, second_fwd, twiddle, second_inv, first_inv)


def run_backward(hidden, dshaped, sums, filter_mid, filter_out, place=seq_place, **kw):
    wide = lambda i: (0, i)
    block = spec((ORDER, STEP), wide)
    return call(
        functools.partial(backward_kernel, place),
        LENGTH // STEP,
        [spec((32, STEP), wide)] + [block] * 6 + [spec((STEP // 16, SIDE), lambda i: (i, 0)), spec((8, SIDE)),
         spec((ORDER, ORDER)), spec((ORDER, SIDE))],
        spec((112, SIDE)),
        out((112, SIDE)),
        scratch=[pltpu.VMEM((SIDE, SIDE), F32), pltpu.VMEM((32, SIDE), F32), pltpu.VMEM((16, SIDE), F32)]
        + [pltpu.VMEM((ORDER, STEP), BF16)] * 4,
        flops=8 * 10**9, nbytes=20 * MIB, **kw,
    )(feature_table(), *hidden, dshaped, sums, filter_mid, filter_out)


def run_receive(query, key, value, grad, skip, field, **kw):
    block = spec((ROWS, SIDE))
    return call(receive_kernel, 1, [block] * 4 + [spec((1, SIDE)), spec((1024, SIDE))], [block] * 4,
                [out((ROWS, SIDE), BF16)] * 4, **kw)(query, key, value, grad, skip, field)


def run_finish(mine, other, **kw):
    shapes = [(16, ORDER), (ORDER, ORDER), (ORDER, SIDE), (1, SIDE), (1, SIDE)]
    return call(finish_kernel, 1, [spec((112, SIDE))] * 2, [spec(s) for s in shapes], [out(s) for s in shapes], **kw)(
        mine, other
    )


def exchanged(x, axis, distance):
    return lax.ppermute(x, axis, [(i, i ^ distance) for i in range(lax.axis_size(axis))])


def group_sum(x, axis, distances):
    values = [x] + [exchanged(x, axis, d) for d in distances]
    while len(values) > 1:
        values = [a + b for a, b in zip(values[::2], values[1::2])]
    return values[0]


def body(query, key, value, grad, filter_in, filter_mid, filter_out, decay_rate, skip_gain):
    decay = decay_rate.reshape(1, SIDE)
    skip = skip_gain.reshape(1, SIDE)
    sent = run_send(query, key, value, grad).reshape(SEQ, SEQ, SIDE)
    field = lax.all_to_all(sent, "seq", 0, 0, tiled=True).reshape(1024, SIDE)
    *hidden, spectrum, filt, window = run_filter(filter_in, filter_mid, filter_out, decay)
    sent, dshaped, sums = run_convolve(field, spectrum, filt, window, decay)
    field = lax.all_to_all(sent.reshape(SEQ, SEQ, SIDE), "seq", 0, 0, tiled=True).reshape(1024, SIDE)
    grads = run_backward(hidden, dshaped, sums, filter_mid, filter_out)
    output, grad_query, grad_key, grad_value = run_receive(query, key, value, grad, skip, field)
    shared = group_sum(grads[:40], "chan", range(1, 8))
    grads = jnp.concatenate([shared, grads[40:]])
    grads = group_sum(grads, "seq", (8, 16, 24))
    grads = group_sum(grads, "seq", (2, 4, 6))
    first, second, third, rates, gains = run_finish(grads, exchanged(grads, "seq", 1))
    return (output, grad_query, grad_key, grad_value, first, second, third, rates.reshape(SIDE), gains.reshape(SIDE))


def solution(mesh):
    wide = P("seq", "chan")
    return jax.shard_map(
        body,
        mesh=mesh,
        in_specs=(wide, wide, wide, wide, P(), P(), P(None, "chan"), P("chan"), P("chan")),
        out_specs=(wide, wide, wide, wide, P(), P(), P(None, "chan"), P("chan"), P("chan")),
        check_vma=False,
    )
```

time: 802 us -> 107 us (0.13)
  waiting for transfers between devices: 457 us -> 15.4 us
  blocking collectives: 203 us -> 0 us
  matrix products: 67.2 us -> 0 us
  other arithmetic: 38.2 us -> 0.06 us
  Pallas kernels: 0 us -> 31.3 us
  starting transfers between devices: 19.3 us -> 38.6 us
  local copies, waits for them, and re-layouts: 6.34 us -> 19.4 us
    ppermute x10 -> x14, waiting for transfers between devices: 457 us -> 15.4 us  [exchanged(): lax.ppermute(x, axis, [(i, i ^ distance) for i in range(lax.axis_size(axi...]
    psum x2 -> x0, blocking collectives: 203 us -> none  [the longest x1 125 us: body(): lax.psum((grad_third, grad_rates, grad_skip), 'seq')]
    dot_general x16 -> x0, matrix products: 67.2 us -> none  [the longest x8 60.2 us: product_of(): jnp.einsum(form, table, field, precision=HIGHEST, preferred_element_type=...]
    pallas_call x0 -> x6, Pallas kernels: none -> 31.3 us  [the longest x1 14 us: run_filter(): call(functools.partial(filter_kernel, place), LENGTH // STEP, [spec((32,...]
    select_n x10 -> x0, other arithmetic: 24.1 us -> none  [the longest x5 15.1 us: swap_forward(): real_part = jnp.where(is_upper, diff_re, real_part + partner[0])]
    all_to_all x0 -> x2, starting transfers between devices: none -> 14.9 us  [the longest x1 7.61 us: body(): lax.all_to_all(sent.reshape(SEQ, SEQ, SIDE), 'seq', 0, 0, tiled=True)]
    unnamed x54 -> x70, local copies, waits for them, and re-layouts: 6.16 us -> 19.4 us
    another operation x14 -> x0, other arithmetic: 9.52 us -> none  [the longest x5 4.82 us: swap_inverse(): partner = from_partner(jnp.stack([real_part, imag_part]), 'seq', level_id)]
  transfers between devices with their start and end apart: 10 -> 16, of which waited for: 10 -> 6; matrix products, arithmetic and copies ran while one was open for 0% -> 0% of each run, Pallas kernels for 0% -> 14%
where the time goes in v1:
time: 107 us; the launch traced here: 106 us
  starting transfers between devices  38.6 us (36%)
  Pallas kernels  31.3 us (29%)
  local copies, waits for them, and re-layouts  19.4 us (18%)
  waiting for transfers between devices  15.4 us (14%)
    ppermute x14, starting transfers between devices, exchanged(): lax.ppermute(x, axis, [(i, i ^ distance) for i in range(lax.axis_size(axi...  23.7 us
    unnamed x70, local copies, waits for them, and re-layouts  19.4 us
    ppermute x14, waiting for transfers between devices, exchanged(): lax.ppermute(x, axis, [(i, i ^ distance) for i in range(lax.axis_size(axi...  15.4 us
    pallas_call x1, Pallas kernels, run_filter(): call(functools.partial(filter_kernel, place), LENGTH // STEP, [spec((32,...  14 us
    pallas_call x1, Pallas kernels, run_backward(): call(functools.partial(backward_kernel, place), LENGTH // STEP, [spec((32...  10.4 us
    all_to_all x1, starting transfers between devices, body(): lax.all_to_all(sent.reshape(SEQ, SEQ, SIDE), 'seq', 0, 0, tiled=True)  7.61 us
    all_to_all x1, starting transfers between devices, body(): field = lax.all_to_all(sent, 'seq', 0, 0, tiled=True).reshape(1024, SIDE)  7.32 us
    pallas_call x1, Pallas kernels, run_convolve(): call(functools.partial(convolve_kernel, place), 1, [spec((1024, SIDE)), s...  3.9 us
  transfers between devices with their start and end apart: 16, of which 6 were waited for; matrix products, arithmetic and copies ran while one was open for 0% of the time, Pallas kernels for 14%

profile of v1, /device:TPU:32, one launch (start us, length us, event | category | flops | bytes accessed | tf_op | source)
XLA Modules:
  0.0 105.9 jit_solution(4093195071515591356)
XLA Ops:
  0.6 0.0 copy-start
  0.7 0.9 copy-done
  1.6 0.9 copy-done.2
  2.5 0.9 copy-done.4
  3.4 0.9 copy-done.6
  4.3 0.0 copy-start.13
  4.3 0.0 copy-start.14
  4.3 0.0 copy-start.16
  4.3 0.0 copy-start.18
  4.3 1.2 %shard_map.214 = f32[1024,128]{1,0:T(8,128)} custom-call(bf16[512,128]{1,0:T(8,128)(2,1)S(1)} %copy-done, bf16[512,128]{1,0:T(8,128)(2,1)S(1)} %copy-done.2, bf16[512,128]{1,0:T(8,128)(2,1)S(1)} %copy-done.4, bf16[512,128]{1,0:T(8,128)(2,1)S(1)} %copy-done.6), custom_call_target="tpu_custom_call" | custom-call | flops 1 | bytes 1 | tf_op jit(solution)/shard_map/pallas_call | solution.py:364
  5.5 7.3 %all-to-all-start = ((f32[32,32,128]{2,1,0:T(8,128)}), f32[32,32,128]{2,1,0:T(8,128)S(1)}, u32[]{:S(2)}, u32[]{:S(2)}) async-start(f32[32,32,128]{2,1,0:T(8,128)} %bitcast.1), calls=%async_computation | async-start | bytes 1048576 | tf_op jit(solution)/shard_map/all_to_all | solution.py:441
  13.0 0.0 copy-start.15
  13.0 0.0 copy-start.17
  13.0 14.0 %shard_map.215 = (bf16[64,16384]{1,0:T(8,128)(2,1)S(1)}, bf16[64,16384]{1,0:T(8,128)(2,1)S(1)}, f32[64,16384]{1,0:T(8,128)S(1)}, bf16[64,16384]{1,0:T(8,128)(2,1...) custom-call(bf16[32,16384]{1,0:T(8,128)(2,1)S(1)} %copy-done.13, ...), custom_call_target="tpu_custom_call" | custom-call | flops 8000000000 | bytes 20971520 | tf_op jit(solution)/shard_map/pallas_call | solution.py:372
  27.0 2.0 %copy-done.19 = f32[64,16384]{1,0:T(8,128)} copy-done((f32[64,16384]{1,0:T(8,128)}, f32[64,16384]{1,0:T(8,128)S(1)}, u32[]{:S(2)}) %copy-start.19) | copy-done | bytes 4194328
  29.0 2.0 %copy-done.21 = f32[64,16384]{1,0:T(8,128)} copy-done((f32[64,16384]{1,0:T(8,128)}, f32[64,16384]{1,0:T(8,128)S(1)}, u32[]{:S(2)}) %copy-start.21) | copy-done | bytes 4194328
  31.0 1.3 %copy-done.23 = bf16[64,16384]{1,0:T(8,128)(2,1)} copy-done((bf16[64,16384]{1,0:T(8,128)(2,1)}, bf16[64,16384]{1,0:T(8,128)(2,1)S(1)}, u32[]{:S(2)}) %copy-start.23) | copy-done | bytes 2097176
  32.3 1.4 %copy-done.25 = bf16[64,16384]{1,0:T(8,128)(2,1)} copy-done((bf16[64,16384]{1,0:T(8,128)(2,1)}, bf16[64,16384]{1,0:T(8,128)(2,1)S(1)}, u32[]{:S(2)}) %copy-start.25) | copy-done | bytes 2097176
  33.7 1.3 %copy-done.27 = bf16[64,16384]{1,0:T(8,128)(2,1)} copy-done((bf16[64,16384]{1,0:T(8,128)(2,1)}, bf16[64,16384]{1,0:T(8,128)(2,1)S(1)}, u32[]{:S(2)}) %copy-start.27) | copy-done | bytes 2097176
  35.0 1.3 %copy-done.29 = bf16[64,16384]{1,0:T(8,128)(2,1)} copy-done((bf16[64,16384]{1,0:T(8,128)(2,1)}, bf16[64,16384]{1,0:T(8,128)(2,1)S(1)}, u32[]{:S(2)}) %copy-start.29) | copy-done | bytes 2097176
  36.3 0.7 copy-done.31
  37.0 0.7 copy-done.33
  37.7 0.9 copy-done.32
  38.7 0.9 copy-done.34
  39.7 3.9 %shard_map.216 = (f32[1024,128]{1,0:T(8,128)}, f32[1024,128]{1,0:T(8,128)S(1)}, f32[8,128]{1,0:T(8,128)S(1)}) custom-call(f32[1024,128]{1,0:T(8,128)S(1)} %bitcast.9, f32[512,256]{1,0:T(8,128)S(1)} %get-tuple-element.30.spectrum, f32[512,128]{1,0:T(8,128)S(1)} %copy-done.32, f32[512,128]{1,0:T(8,128)S(1)} %copy-done.34, f32[1,128]{1,0:T(1,128)S(1)} %bitcast.12, ...), custom_call_target="tpu_custom_call" | custom-call | flops 4000000000 | bytes 4194304 | tf_op jit(solution)/shard_map/pallas_call | solution.py:386
  43.6 0.1 copy-done.24
  43.7 0.8 copy-done.26
  44.5 0.6 copy-done.28
  45.1 1.6 %copy-done.30 = bf16[64,16384]{1,0:T(8,128)(2,1)S(1)} copy-done((bf16[64,16384]{1,0:T(8,128)(2,1)S(1)}, bf16[64,16384]{1,0:T(8,128)(2,1)}, u32[]{:S(2)}) %copy-start.30) | copy-done | bytes 2097176
  46.7 10.4 %shard_map.218 = f32[112,128]{1,0:T(8,128)S(1)} custom-call(bf16[32,16384]{1,0:T(8,128)(2,1)S(1)} %copy-done.13, bf16[64,16384]{1,0:T(8,128)(2,1)S(1)} %copy-done.24, bf16[64,16384]{1,0:T(8,128)(2,1)S(1)} %copy-done.26, f32[64,16384]{1,0:T(8,128)S(1)} %copy-done.20, bf16[64,16384]{1,0:T(8,128)(2,1)S(1)} %copy-done.28, bf16[64,16384]{1,0:T(8,128)(2,1)S(1)} %copy-done.30, ...), custom_call_target="tpu_custom_call" | custom-call | flops 8000000000 | bytes 20971520 | tf_op jit(solution)/shard_map/pallas_call | solution.py:400
  57.0 0.0 copy-start.1
  57.1 0.0 copy-start.3
  57.1 0.0 copy-start.5
  57.1 0.0 copy-start.7
  57.1 0.0 copy-start.8
  57.1 5.5 %collective-permute-start.5 = (f32[40,128]{1,0:T(8,128)S(1)}, f32[40,128]{1,0:T(8,128)S(1)}, u32[]{:S(2)}, u32[]{:S(2)}) collective-permute-start(f32[40,128]{1,0:T(8,128)S(1)} %slice.8), channel_id=1, source_target_pairs={{0,6},{1,7},{2,4},{3,5},{4,2},{5,3},{6,0},{7,1},{8,14},{9,15},{10,... | collective-permute-start | bytes 61448 | tf_op jit(solution)/shard_map/ppermute | solution.py:427
  62.6 0.5 collective-permute-start.4
  63.1 4.9 %collective-permute-start.3 = (f32[40,128]{1,0:T(8,128)S(1)}, f32[40,128]{1,0:T(8,128)S(1)}, u32[]{:S(2)}, u32[]{:S(2)}) collective-permute-start(f32[40,128]{1,0:T(8,128)S(1)} %slice.8), channel_id=1, source_target_pairs={{0,4},{1,5},{2,6},{3,7},{4,0},{5,1},{6,2},{7,3},{8,12},{9,13},{10,... | collective-permute-start | bytes 61448 | tf_op jit(solution)/shard_map/ppermute | solution.py:427
  68.1 1.0 collective-permute-start.2
  69.1 2.4 %collective-permute-start.1 = (f32[40,128]{1,0:T(8,128)S(1)}, f32[40,128]{1,0:T(8,128)S(1)}, u32[]{:S(2)}, u32[]{:S(2)}) collective-permute-start(f32[40,128]{1,0:T(8,128)S(1)} %slice.8), channel_id=1, source_target_pairs={{0,2},{1,3},{2,0},{3,1},{4,6},{5,7},{6,4},{7,5},{8,10},{9,11},{10,... | collective-permute-start | bytes 61448 | tf_op jit(solution)/shard_map/ppermute | solution.py:427
  71.5 0.0 collective-permute-done.5
  71.5 0.5 collective-permute-start.6
  72.0 0.0 collective-permute-done.4
  72.0 0.0 collective-permute-start
  72.0 0.0 collective-permute-done.3
  72.0 0.1 collective-permute-done.2
  72.1 1.7 %collective-permute-done.1 = f32[40,128]{1,0:T(8,128)S(1)} collective-permute-done((f32[40,128]{1,0:T(8,128)S(1)}, f32[40,128]{1,0:T(8,128)S(1)}, u32[]{:S(2)}, u32[]{:S(2)}) %collective-permute-start.1) | collective-permute-done | bytes 20512 | tf_op jit(solution)/shard_map/ppermute | solution.py:427
  73.8 4.5 %collective-permute-done.6 = f32[40,128]{1,0:T(8,128)S(1)} collective-permute-done((f32[40,128]{1,0:T(8,128)S(1)}, f32[40,128]{1,0:T(8,128)S(1)}, u32[]{:S(2)}, u32[]{:S(2)}) %collective-permute-start.6) | collective-permute-done | bytes 20512 | tf_op jit(solution)/shard_map/ppermute | solution.py:427
  78.3 0.0 collective-permute-done
  78.3 3.4 %collective-permute-start.8 = (f32[112,128]{1,0:T(8,128)S(1)}, f32[112,128]{1,0:T(8,128)S(1)}, u32[]{:S(2)}, u32[]{:S(2)}) collective-permute-start(f32[112,128]{1,0:T(8,128)S(1)} %pad_maximum_fusion), channel_id=1, source_target_pairs={{0,128},{8,136},{16,144},{24,152},{32,160},{40,168},{48,176},{56,1... | collective-permute-start | bytes 172040 | tf_op jit(solution)/shard_map/ppermute | solution.py:427
  81.7 1.2 %collective-permute-start.9 = (f32[112,128]{1,0:T(8,128)S(1)}, f32[112,128]{1,0:T(8,128)S(1)}, u32[]{:S(2)}, u32[]{:S(2)}) collective-permute-start(f32[112,128]{1,0:T(8,128)S(1)} %pad_maximum_fusion), channel_id=1, source_target_pairs={{0,192},{8,200},{16,208},{24,216},{32,224},{40,232},{48,240},{56,2... | collective-permute-start | bytes 172040 | tf_op jit(solution)/shard_map/ppermute | solution.py:427
  82.8 0.0 collective-permute-start.7
  82.8 7.6 %all-to-all-start.1 = ((f32[32,32,128]{2,1,0:T(8,128)}), f32[32,32,128]{2,1,0:T(8,128)S(1)}, u32[]{:S(2)}, u32[]{:S(2)}) async-start(f32[32,32,128]{2,1,0:T(8,128)} %bitcast.4), calls=%async_computation.1 | async-start | bytes 1048576 | tf_op jit(solution)/shard_map/all_to_all | solution.py:444
  90.5 0.0 collective-permute-done.8
  90.5 0.0 collective-permute-done.7
  90.5 3.1 %collective-permute-start.12 = (f32[112,128]{1,0:T(8,128)S(1)}, f32[112,128]{1,0:T(8,128)S(1)}, u32[]{:S(2)}, u32[]{:S(2)}) collective-permute-start(f32[112,128]{1,0:T(8,128)S(1)} %add_add_fusion.1), channel_id=1, source_target_pairs={{0,48},{8,56},{16,32},{24,40},{32,16},{40,24},{48,0},{56,8},{64,11... | collective-permute-start | bytes 172040 | tf_op jit(solution)/shard_map/ppermute | solution.py:427
  93.6 0.9 collective-permute-start.11
  94.5 0.2 collective-permute-start.10
  94.7 5.4 %collective-permute-done.12 = f32[112,128]{1,0:T(8,128)S(1)} collective-permute-done((f32[112,128]{1,0:T(8,128)S(1)}, f32[112,128]{1,0:T(8,128)S(1)}, u32[]{:S(2)}, u32[]{:S(2)}) %collective-permute-start.12) | collective-permute-done | bytes 57376 | tf_op jit(solution)/shard_map/ppermute | solution.py:427
  100.1 2.5 %collective-permute-done.11 = f32[112,128]{1,0:T(8,128)S(1)} collective-permute-done((f32[112,128]{1,0:T(8,128)S(1)}, f32[112,128]{1,0:T(8,128)S(1)}, u32[]{:S(2)}, u32[]{:S(2)}) %collective-permute-start.11) | collective-permute-done | bytes 57376 | tf_op jit(solution)/shard_map/ppermute | solution.py:427
  102.7 0.1 collective-permute-start.13
  102.8 1.2 %collective-permute-done.13.other = f32[112,128]{1,0:T(8,128)S(1)} collective-permute-done((f32[112,128]{1,0:T(8,128)S(1)}, f32[112,128]{1,0:T(8,128)S(1)}, u32[]{:S(2)}, u32[]{:S(2)}) %collective-permute-start.13) | collective-permute-done | bytes 57376 | tf_op jit(solution)/shard_map/ppermute | solution.py:427
  104.0 0.7 shard_map.219
  104.7 1.2 %shard_map.217 = (bf16[512,128]{1,0:T(8,128)(2,1)}, bf16[512,128]{1,0:T(8,128)(2,1)}, bf16[512,128]{1,0:T(8,128)(2,1)}, bf16[512,128]{1,0:T(8,128)(2,1)}) custom-call(bf16[512,128]{1,0:T(8,128)(2,1)S(1)} %copy-done.1, bf16[512,128]{1,0:T(8,128)(2,1)S(1)} %copy-done.3, bf16[512,128]{1,0:T(8,128)(2,1)S(1)} %copy-done.5, bf16[512,128]{1,0:T(8,128)(2,1)S(1)} %copy-done.7, ...), custom_call_target="tpu_custom_call" | custom-call | flops 1 | bytes 1 | tf_op jit(solution)/shard_map/pallas_call | solution.py:415
  (50 shorter events, 0.1 us)
Async XLA Ops:
  0.6 0.9 copy-start
  1.6 0.9 copy-start.2
  2.5 0.9 copy-start.4
  3.4 0.9 copy-start.6
  4.3 8.6 %copy-start.9 = (f32[64,64]{1,0:T(8,128)S(1)}, f32[64,64]{1,0:T(8,128)}, u32[]{:S(2)}) copy-start(f32[64,64]{1,0:T(8,128)} %filter_mid.3) | copy-start | bytes 49156
  4.3 8.6 %copy-start.10 = (f32[64,128]{1,0:T(8,128)S(1)}, f32[64,128]{1,0:T(8,128)}, u32[]{:S(2)}) copy-start(f32[64,128]{1,0:T(8,128)} %filter_out.3) | copy-start | bytes 98308
  4.3 8.6 %copy-start.11 = (f32[16,64]{1,0:T(8,128)S(1)}, f32[16,64]{1,0:T(8,128)}, u32[]{:S(2)}) copy-start(f32[16,64]{1,0:T(8,128)} %filter_in.1) | copy-start | bytes 12292
  4.3 8.6 %copy-start.12 = (f32[128]{0:T(128)S(1)}, f32[128]{0:T(128)}, u32[]{:S(2)}) copy-start(f32[128]{0:T(128)} %param.22) | copy-start | bytes 1540
  4.3 8.6 %copy-start.13 = (bf16[32,16384]{1,0:T(8,128)(2,1)S(1)}, bf16[32,16384]{1,0:T(8,128)(2,1)}, u32[]{:S(2)}) copy-start(bf16[32,16384]{1,0:T(8,128)(2,1)} %constant.12.clone.features) | copy-start | bytes 3145732
  4.3 8.6 %copy-start.14 = (bf16[768,256]{1,0:T(8,128)(2,1)S(1)}, bf16[768,256]{1,0:T(8,128)(2,1)}, u32[]{:S(2)}) copy-start(bf16[768,256]{1,0:T(8,128)(2,1)} %constant.14.clone.second_fwd) | copy-start | bytes 1179652
  4.3 8.6 %copy-start.16 = (bf16[256,384]{1,0:T(8,128)(2,1)S(1)}, bf16[256,384]{1,0:T(8,128)(2,1)}, u32[]{:S(2)}) copy-start(bf16[256,384]{1,0:T(8,128)(2,1)} %constant.13.clone.first_fwd) | copy-start | bytes 589828
  4.3 8.6 %copy-start.18 = (f32[128,256]{1,0:T(8,128)S(1)}, f32[128,256]{1,0:T(8,128)}, u32[]{:S(2)}) copy-start(f32[128,256]{1,0:T(8,128)} %constant.15.clone.twiddle) | copy-start | bytes 393220
  5.5 32.2 %all-to-all-start = ((f32[32,32,128]{2,1,0:T(8,128)}), f32[32,32,128]{2,1,0:T(8,128)S(1)}, u32[]{:S(2)}, u32[]{:S(2)}) async-start(f32[32,32,128]{2,1,0:T(8,128)} %bitcast.1), calls=%async_computation | async-start | bytes 1048576 | tf_op jit(solution)/shard_map/all_to_all | solution.py:441
  13.0 24.8 %copy-start.15 = (bf16[768,256]{1,0:T(8,128)(2,1)S(1)}, bf16[768,256]{1,0:T(8,128)(2,1)}, u32[]{:S(2)}) copy-start(bf16[768,256]{1,0:T(8,128)(2,1)} %constant.16.clone.second_inv) | copy-start | bytes 1179652
  13.0 24.8 %copy-start.17 = (bf16[128,768]{1,0:T(8,128)(2,1)S(1)}, bf16[128,768]{1,0:T(8,128)(2,1)}, u32[]{:S(2)}) copy-start(bf16[128,768]{1,0:T(8,128)(2,1)} %constant.17.clone.first_inv) | copy-start | bytes 589828
  27.0 2.0 %copy-start.19 = (f32[64,16384]{1,0:T(8,128)}, f32[64,16384]{1,0:T(8,128)S(1)}, u32[]{:S(2)}) copy-start(f32[64,16384]{1,0:T(8,128)S(1)} %get-tuple-element.40.cos1) | copy-start | bytes 12582916
  29.0 2.0 %copy-start.21 = (f32[64,16384]{1,0:T(8,128)}, f32[64,16384]{1,0:T(8,128)S(1)}, u32[]{:S(2)}) copy-start(f32[64,16384]{1,0:T(8,128)S(1)} %get-tuple-element.43.cos2) | copy-start | bytes 12582916
  31.0 1.3 %copy-start.23 = (bf16[64,16384]{1,0:T(8,128)(2,1)}, bf16[64,16384]{1,0:T(8,128)(2,1)S(1)}, u32[]{:S(2)}) copy-start(bf16[64,16384]{1,0:T(8,128)(2,1)S(1)} %get-tuple-element.38.h1_high) | copy-start | bytes 6291460
  32.3 1.4 %copy-start.25 = (bf16[64,16384]{1,0:T(8,128)(2,1)}, bf16[64,16384]{1,0:T(8,128)(2,1)S(1)}, u32[]{:S(2)}) copy-start(bf16[64,16384]{1,0:T(8,128)(2,1)S(1)} %get-tuple-element.39.h1_low) | copy-start | bytes 6291460
  33.7 1.3 %copy-start.27 = (bf16[64,16384]{1,0:T(8,128)(2,1)}, bf16[64,16384]{1,0:T(8,128)(2,1)S(1)}, u32[]{:S(2)}) copy-start(bf16[64,16384]{1,0:T(8,128)(2,1)S(1)} %get-tuple-element.41.h2_high) | copy-start | bytes 6291460
  35.0 1.3 %copy-start.29 = (bf16[64,16384]{1,0:T(8,128)(2,1)}, bf16[64,16384]{1,0:T(8,128)(2,1)S(1)}, u32[]{:S(2)}) copy-start(bf16[64,16384]{1,0:T(8,128)(2,1)S(1)} %get-tuple-element.42.h2_low) | copy-start | bytes 6291460
  36.3 0.7 copy-start.31
  37.0 0.7 copy-start.33
  37.7 1.0 copy-start.32
  38.7 0.9 copy-start.34
  39.6 3.9 %copy-start.20 = (f32[64,16384]{1,0:T(8,128)S(1)}, f32[64,16384]{1,0:T(8,128)}, u32[]{:S(2)}) copy-start(f32[64,16384]{1,0:T(8,128)} %copy-done.19) | copy-start | bytes 12582916
  39.6 3.9 %copy-start.22 = (f32[64,16384]{1,0:T(8,128)S(1)}, f32[64,16384]{1,0:T(8,128)}, u32[]{:S(2)}) copy-start(f32[64,16384]{1,0:T(8,128)} %copy-done.21) | copy-start | bytes 12582916
  39.6 4.1 %copy-start.24 = (bf16[64,16384]{1,0:T(8,128)(2,1)S(1)}, bf16[64,16384]{1,0:T(8,128)(2,1)}, u32[]{:S(2)}) copy-start(bf16[64,16384]{1,0:T(8,128)(2,1)} %copy-done.23) | copy-start | bytes 6291460
  39.6 4.8 %copy-start.26 = (bf16[64,16384]{1,0:T(8,128)(2,1)S(1)}, bf16[64,16384]{1,0:T(8,128)(2,1)}, u32[]{:S(2)}) copy-start(bf16[64,16384]{1,0:T(8,128)(2,1)} %copy-done.25) | copy-start | bytes 6291460
  39.7 5.4 %copy-start.28 = (bf16[64,16384]{1,0:T(8,128)(2,1)S(1)}, bf16[64,16384]{1,0:T(8,128)(2,1)}, u32[]{:S(2)}) copy-start(bf16[64,16384]{1,0:T(8,128)(2,1)} %copy-done.27) | copy-start | bytes 6291460
  45.1 1.6 %copy-start.30 = (bf16[64,16384]{1,0:T(8,128)(2,1)S(1)}, bf16[64,16384]{1,0:T(8,128)(2,1)}, u32[]{:S(2)}) copy-start(bf16[64,16384]{1,0:T(8,128)(2,1)} %copy-done.29) | copy-start | bytes 6291460
  57.0 47.7 %copy-start.1 = (bf16[512,128]{1,0:T(8,128)(2,1)S(1)}, bf16[512,128]{1,0:T(8,128)(2,1)}, u32[]{:S(2)}) copy-start(bf16[512,128]{1,0:T(8,128)(2,1)} %query.3) | copy-start | bytes 393220
  57.1 47.6 %copy-start.3 = (bf16[512,128]{1,0:T(8,128)(2,1)S(1)}, bf16[512,128]{1,0:T(8,128)(2,1)}, u32[]{:S(2)}) copy-start(bf16[512,128]{1,0:T(8,128)(2,1)} %key.3) | copy-start | bytes 393220
  57.1 47.6 %copy-start.5 = (bf16[512,128]{1,0:T(8,128)(2,1)S(1)}, bf16[512,128]{1,0:T(8,128)(2,1)}, u32[]{:S(2)}) copy-start(bf16[512,128]{1,0:T(8,128)(2,1)} %value.3) | copy-start | bytes 393220
  57.1 47.6 %copy-start.7 = (bf16[512,128]{1,0:T(8,128)(2,1)S(1)}, bf16[512,128]{1,0:T(8,128)(2,1)}, u32[]{:S(2)}) copy-start(bf16[512,128]{1,0:T(8,128)(2,1)} %grad.3) | copy-start | bytes 393220
  57.1 47.6 %copy-start.8 = (f32[128]{0:T(128)S(1)}, f32[128]{0:T(128)}, u32[]{:S(2)}) copy-start(f32[128]{0:T(128)} %param.23) | copy-start | bytes 1540
  57.1 14.4 %collective-permute-start.5 = (f32[40,128]{1,0:T(8,128)S(1)}, f32[40,128]{1,0:T(8,128)S(1)}, u32[]{:S(2)}, u32[]{:S(2)}) collective-permute-start(f32[40,128]{1,0:T(8,128)S(1)} %slice.8), channel_id=1, source_target_pairs={{0,6},{1,7},{2,4},{3,5},{4,2},{5,3},{6,0},{7,1},{8,14},{9,15},{10,... | collective-permute-start | bytes 61448 | tf_op jit(solution)/shard_map/ppermute | solution.py:427
  62.6 9.4 %collective-permute-start.4 = (f32[40,128]{1,0:T(8,128)S(1)}, f32[40,128]{1,0:T(8,128)S(1)}, u32[]{:S(2)}, u32[]{:S(2)}) collective-permute-start(f32[40,128]{1,0:T(8,128)S(1)} %slice.8), channel_id=1, source_target_pairs={{0,5},{1,4},{2,7},{3,6},{4,1},{5,0},{6,3},{7,2},{8,13},{9,12},{10,... | collective-permute-start | bytes 61448 | tf_op jit(solution)/shard_map/ppermute | solution.py:427
  63.1 8.9 %collective-permute-start.3 = (f32[40,128]{1,0:T(8,128)S(1)}, f32[40,128]{1,0:T(8,128)S(1)}, u32[]{:S(2)}, u32[]{:S(2)}) collective-permute-start(f32[40,128]{1,0:T(8,128)S(1)} %slice.8), channel_id=1, source_target_pairs={{0,4},{1,5},{2,6},{3,7},{4,0},{5,1},{6,2},{7,3},{8,12},{9,13},{10,... | collective-permute-start | bytes 61448 | tf_op jit(solution)/shard_map/ppermute | solution.py:427
  68.1 4.0 %collective-permute-start.2 = (f32[40,128]{1,0:T(8,128)S(1)}, f32[40,128]{1,0:T(8,128)S(1)}, u32[]{:S(2)}, u32[]{:S(2)}) collective-permute-start(f32[40,128]{1,0:T(8,128)S(1)} %slice.8), channel_id=1, source_target_pairs={{0,3},{1,2},{2,1},{3,0},{4,7},{5,6},{6,5},{7,4},{8,11},{9,10},{10,... | collective-permute-start | bytes 61448 | tf_op jit(solution)/shard_map/ppermute | solution.py:427
  69.1 4.7 %collective-permute-start.1 = (f32[40,128]{1,0:T(8,128)S(1)}, f32[40,128]{1,0:T(8,128)S(1)}, u32[]{:S(2)}, u32[]{:S(2)}) collective-permute-start(f32[40,128]{1,0:T(8,128)S(1)} %slice.8), channel_id=1, source_target_pairs={{0,2},{1,3},{2,0},{3,1},{4,6},{5,7},{6,4},{7,5},{8,10},{9,11},{10,... | collective-permute-start | bytes 61448 | tf_op jit(solution)/shard_map/ppermute | solution.py:427
  71.5 6.8 %collective-permute-start.6 = (f32[40,128]{1,0:T(8,128)S(1)}, f32[40,128]{1,0:T(8,128)S(1)}, u32[]{:S(2)}, u32[]{:S(2)}) collective-permute-start(f32[40,128]{1,0:T(8,128)S(1)} %slice.8), channel_id=1, source_target_pairs={{0,7},{1,6},{2,5},{3,4},{4,3},{5,2},{6,1},{7,0},{8,15},{9,14},{10,... | collective-permute-start | bytes 61448 | tf_op jit(solution)/shard_map/ppermute | solution.py:427
  72.0 6.2 %collective-permute-start = (f32[40,128]{1,0:T(8,128)S(1)}, f32[40,128]{1,0:T(8,128)S(1)}, u32[]{:S(2)}, u32[]{:S(2)}) collective-permute-start(f32[40,128]{1,0:T(8,128)S(1)} %slice.8), channel_id=1, source_target_pairs={{0,1},{1,0},{2,3},{3,2},{4,5},{5,4},{6,7},{7,6},{8,9},{9,8},{10,11... | collective-permute-start | bytes 61448 | tf_op jit(solution)/shard_map/ppermute | solution.py:427
  78.3 12.2 %collective-permute-start.8 = (f32[112,128]{1,0:T(8,128)S(1)}, f32[112,128]{1,0:T(8,128)S(1)}, u32[]{:S(2)}, u32[]{:S(2)}) collective-permute-start(f32[112,128]{1,0:T(8,128)S(1)} %pad_maximum_fusion), channel_id=1, source_target_pairs={{0,128},{8,136},{16,144},{24,152},{32,160},{40,168},{48,176},{56,1... | collective-permute-start | bytes 172040 | tf_op jit(solution)/shard_map/ppermute | solution.py:427
  81.7 8.8 %collective-permute-start.9 = (f32[112,128]{1,0:T(8,128)S(1)}, f32[112,128]{1,0:T(8,128)S(1)}, u32[]{:S(2)}, u32[]{:S(2)}) collective-permute-start(f32[112,128]{1,0:T(8,128)S(1)} %pad_maximum_fusion), channel_id=1, source_target_pairs={{0,192},{8,200},{16,208},{24,216},{32,224},{40,232},{48,240},{56,2... | collective-permute-start | bytes 172040 | tf_op jit(solution)/shard_map/ppermute | solution.py:427
  82.8 7.6 %collective-permute-start.7 = (f32[112,128]{1,0:T(8,128)S(1)}, f32[112,128]{1,0:T(8,128)S(1)}, u32[]{:S(2)}, u32[]{:S(2)}) collective-permute-start(f32[112,128]{1,0:T(8,128)S(1)} %pad_maximum_fusion), channel_id=1, source_target_pairs={{0,64},{8,72},{16,80},{24,88},{32,96},{40,104},{48,112},{56,120},{... | collective-permute-start | bytes 172040 | tf_op jit(solution)/shard_map/ppermute | solution.py:427
  82.8 21.8 %all-to-all-start.1 = ((f32[32,32,128]{2,1,0:T(8,128)}), f32[32,32,128]{2,1,0:T(8,128)S(1)}, u32[]{:S(2)}, u32[]{:S(2)}) async-start(f32[32,32,128]{2,1,0:T(8,128)} %bitcast.4), calls=%async_computation.1 | async-start | bytes 1048576 | tf_op jit(solution)/shard_map/all_to_all | solution.py:444
  90.5 9.6 %collective-permute-start.12 = (f32[112,128]{1,0:T(8,128)S(1)}, f32[112,128]{1,0:T(8,128)S(1)}, u32[]{:S(2)}, u32[]{:S(2)}) collective-permute-start(f32[112,128]{1,0:T(8,128)S(1)} %add_add_fusion.1), channel_id=1, source_target_pairs={{0,48},{8,56},{16,32},{24,40},{32,16},{40,24},{48,0},{56,8},{64,11... | collective-permute-start | bytes 172040 | tf_op jit(solution)/shard_map/ppermute | solution.py:427
  93.6 9.0 %collective-permute-start.11 = (f32[112,128]{1,0:T(8,128)S(1)}, f32[112,128]{1,0:T(8,128)S(1)}, u32[]{:S(2)}, u32[]{:S(2)}) collective-permute-start(f32[112,128]{1,0:T(8,128)S(1)} %add_add_fusion.1), channel_id=1, source_target_pairs={{0,32},{8,40},{16,48},{24,56},{32,0},{40,8},{48,16},{56,24},{64,96... | collective-permute-start | bytes 172040 | tf_op jit(solution)/shard_map/ppermute | solution.py:427
  94.5 8.2 %collective-permute-start.10 = (f32[112,128]{1,0:T(8,128)S(1)}, f32[112,128]{1,0:T(8,128)S(1)}, u32[]{:S(2)}, u32[]{:S(2)}) collective-permute-start(f32[112,128]{1,0:T(8,128)S(1)} %add_add_fusion.1), channel_id=1, source_target_pairs={{0,16},{8,24},{16,0},{24,8},{32,48},{40,56},{48,32},{56,40},{64,80... | collective-permute-start | bytes 172040 | tf_op jit(solution)/shard_map/ppermute | solution.py:427
  102.7 1.3 %collective-permute-start.13 = (f32[112,128]{1,0:T(8,128)S(1)}, f32[112,128]{1,0:T(8,128)S(1)}, u32[]{:S(2)}, u32[]{:S(2)}) collective-permute-start(f32[112,128]{1,0:T(8,128)S(1)} %add_add_fusion.mine), channel_id=1, source_target_pairs={{0,8},{8,0},{16,24},{24,16},{32,40},{40,32},{48,56},{56,48},{64,72... | collective-permute-start | bytes 172040 | tf_op jit(solution)/shard_map/ppermute | solution.py:427

commit v2 on v1

--- a/solution.py
+++ b/solution.py
@@ -20,6 +20,7 @@
 ORDER = 64
 STEP = 2048
 PIECE = 256
+HALF = LENGTH // 2
 MIB = 1 << 20
 
 
@@ -124,7 +125,9 @@
 def own_channels(place):
     row = lax.broadcasted_iota(jnp.int32, (8, SIDE), 0)
     lane = lax.broadcasted_iota(jnp.int32, (8, SIDE), 1)
-    return jnp.where((row < OWN) & (lane == place + SEQ * row), 1.0, 0.0).astype(F32)
+    other = place + 1 - 2 * (place % 2)
+    channel = jnp.where(row < OWN, place + SEQ * row, other + SEQ * (row - OWN))
+    return jnp.where(lane == channel, 1.0, 0.0).astype(F32)
 
 
 def position_grid():
@@ -144,7 +147,7 @@
     return jax.ShapeDtypeStruct(shape, dtype)
 
 
-def call(kernel, grid, in_specs, out_specs, out_shape, scratch=(), limit=32, flops=1, nbytes=1, interpret=False):
+def call(kernel, grid, in_specs, out_specs, out_shape, scratch=(), limit=16, flops=1, nbytes=1, interpret=False):
     return pl.pallas_call(
         kernel,
         grid=(grid,),
@@ -158,12 +161,16 @@
     )
 
 
-def send_kernel(query, key, value, grad, sent):
-    for h in range(ROWS // SIDE):
-        rows = pl.ds(SIDE * h, SIDE)
-        gated = key[rows, :].astype(F32) * value[rows, :].astype(F32)
-        incoming = grad[rows, :].astype(F32) * query[rows, :].astype(F32)
-        for offset, block in ((0, gated.T), (OWN, incoming.T)):
+def send_kernel(query, key, value, grad, sent, held, sems):
+    copies = [pltpu.make_async_copy(x, held.at[k], sems.at[k]) for k, x in enumerate((key, value, grad, query))]
+    for copy in copies:
+        copy.start()
+    for offset, first, second in ((0, 0, 1), (OWN, 2, 3)):
+        copies[first].wait()
+        copies[second].wait()
+        for h in range(ROWS // SIDE):
+            rows = pl.ds(SIDE * h, SIDE)
+            block = (held[first, rows, :].astype(F32) * held[second, rows, :].astype(F32)).T
             for c in range(OWN):
                 sent[pl.ds(8 * h + offset + c, SEQ, stride=SEQ), :] = block[SEQ * c : SEQ * (c + 1), :]
 
@@ -214,8 +221,8 @@
     return fields
 
 
-def filter_kernel(place, features, filter_in, filter_mid, filter_out, decay, first_fwd, second_fwd, twiddle,
-                  h1_high, h1_low, cos1, h2_high, h2_low, cos2, spectrum, filt, window, shaped):
+def filter_kernel(place, features, filter_in, filter_mid, filter_out,
+                  h1_high, h1_low, cos1, h2_high, h2_low, cos2, mine, theirs, shaped):
     step = pl.program_id(0)
     own = own_channels(place())
     turn = 1.0 / (2.0 * math.pi)
@@ -242,23 +249,32 @@
             row = 8 * (step * (STEP // SIDE) + k * (PIECE // SIDE) + m)
             shaped[pl.ds(pl.multiple_of(row, 8), 8), :] = values[:, SIDE * m : SIDE * (m + 1)]
 
-    @pl.when(step == LENGTH // STEP - 1)
+    @pl.when(step == HALF // STEP - 1)
     def _():
-        time = position_grid()
-        rates = jnp.sum(own * decay[...], axis=1, keepdims=True)
-        fields = []
         for c in range(OWN):
-            rate = rates[c : c + 1, :]
-            window_c = jnp.exp(-rate * time) * jnp.sqrt(rate + 1.0 / LENGTH)
-            field = shaped[pl.ds(c, SIDE, stride=8), :] * window_c
-            window[pl.ds(SIDE * c, SIDE), :] = window_c
-            filt[pl.ds(SIDE * c, SIDE), :] = field
-            fields.append(field)
-        spectrum[...] = forward_rows(fields, first_fwd, second_fwd, twiddle)
+            mine[pl.ds(64 * c, 64), :] = shaped[pl.ds(c, 64, stride=8), :]
+            theirs[pl.ds(64 * c, 64), :] = shaped[pl.ds(c + OWN, 64, stride=8), :]
+
+
+def spectrum_kernel(place, mine, other, decay, first_fwd, second_fwd, twiddle, spectrum, filt, window):
+    me = place()
+    time = position_grid()
+    rates = jnp.sum(own_channels(me) * decay[...], axis=1, keepdims=True)
+    lower = me % 2 == 0
+    fields = []
+    for c in range(OWN):
+        rate = rates[c : c + 1, :]
+        window_c = jnp.exp(-rate * time) * jnp.sqrt(rate + 1.0 / LENGTH)
+        here, there = mine[pl.ds(64 * c, 64), :], other[pl.ds(64 * c, 64), :]
+        field = jnp.concatenate([jnp.where(lower, here, there), jnp.where(lower, there, here)]) * window_c
+        window[pl.ds(SIDE * c, SIDE), :] = window_c
+        filt[pl.ds(SIDE * c, SIDE), :] = field
+        fields.append(field)
+    spectrum[...] = forward_rows(fields, first_fwd, second_fwd, twiddle)
 
 
 def convolve_kernel(place, field, spectrum, filt, window, decay, first_fwd, second_fwd, twiddle, second_inv, first_inv,
-                    sent, dshaped, sums):
+                    sent, mine, theirs, sums):
     fields = []
     for c in range(OWN):
         for offset in (0, OWN):
@@ -284,20 +300,26 @@
     results = inverse_rows([p for c in range(OWN) for p in products[c][:2]] + [products[c][2] for c in range(OWN)],
                            first_inv, second_inv, twiddle)
     time = position_grid()
-    rates = jnp.sum(own_channels(place()) * decay[...], axis=1, keepdims=True)
+    me = place()
+    lower = me % 2 == 0
+    rates = jnp.sum(own_channels(me) * decay[...], axis=1, keepdims=True)
+    zeros = jnp.zeros((64, SIDE), F32)
     for c in range(OWN):
         for offset, result in ((0, results[2 * c]), (OWN, results[2 * c + 1])):
             for h in range(ROWS // SIDE):
                 sent[pl.ds(8 * h + offset + c, SEQ, stride=SEQ), :] = result[SEQ * h : SEQ * (h + 1), :]
         dfilt = results[2 * OWN + c]
-        dshaped[pl.ds(c, SIDE, stride=8), :] = dfilt * window[pl.ds(SIDE * c, SIDE), :]
-        dshaped[pl.ds(c + OWN, SIDE, stride=8), :] = jnp.zeros((SIDE, SIDE), F32)
+        dshaped = dfilt * window[pl.ds(SIDE * c, SIDE), :]
+        mine[pl.ds(c, 64, stride=8), :] = jnp.where(lower, dshaped[:64], dshaped[64:])
+        mine[pl.ds(c + OWN, 64, stride=8), :] = zeros
+        theirs[pl.ds(c, 64, stride=8), :] = zeros
+        theirs[pl.ds(c + OWN, 64, stride=8), :] = jnp.where(lower, dshaped[64:], dshaped[:64])
         slope = 0.5 / (rates[c : c + 1, :] + 1.0 / LENGTH) - time
         sums[pl.ds(c, 1), :] = jnp.sum(dfilt * filt[pl.ds(SIDE * c, SIDE), :] * slope, axis=0, keepdims=True)
         sums[pl.ds(c + OWN, 1), :] = jnp.sum(fields[2 * c] * fields[2 * c + 1], axis=0, keepdims=True)
 
 
-def backward_kernel(place, features, h1_high, h1_low, cos1, h2_high, h2_low, cos2, dshaped, sums, filter_mid, filter_out,
+def backward_kernel(place, features, h1_high, h1_low, cos1, h2_high, h2_low, cos2, mine, other, sums, filter_mid, filter_out,
                     grads, grad_mid, grad_in, grad_out, d2_high, d2_low, d1_high, d1_low):
     step = pl.program_id(0)
     own = own_channels(place())
@@ -311,7 +333,9 @@
         grad_out[...] = jnp.zeros_like(grad_out)
 
     pieces = [pl.ds(PIECE * k, PIECE) for k in range(STEP // PIECE)]
-    shaped_high, shaped_low = halves(jnp.concatenate([dshaped[pl.ds(8 * m, 8), :] for m in range(STEP // SIDE)], axis=1))
+    shaped_high, shaped_low = halves(
+        jnp.concatenate([mine[pl.ds(8 * m, 8), :] + other[pl.ds(8 * m, 8), :] for m in range(STEP // SIDE)], axis=1)
+    )
     for k, piece in enumerate(pieces):
         part = slice(PIECE * k, PIECE * (k + 1))
         rows = jnp.concatenate([shaped_high[:, part], shaped_low[:, part], shaped_high[:, part]])
@@ -325,7 +349,7 @@
     grad_in[...] += dot_nt(features[...], jnp.concatenate([d1_high[...], d1_low[...]]))
     grad_out[...] += dot_nt(jnp.concatenate([shaped_high, shaped_low]), jnp.concatenate([h2_high[...], h2_low[...]]))
 
-    @pl.when(step == LENGTH // STEP - 1)
+    @pl.when(step == HALF // STEP - 1)
     def _():
         def joined(x, half):
             return x[:half, :ORDER] + (x[:half, ORDER:] + x[half:, :ORDER])
@@ -360,25 +384,37 @@
 
 
 def run_send(query, key, value, grad, **kw):
-    block = spec((ROWS, SIDE))
-    return call(send_kernel, 1, [block] * 4, spec((1024, SIDE)), out((1024, SIDE)), **kw)(query, key, value, grad)
-
-
-def run_filter(filter_in, filter_mid, filter_out, decay, place=seq_place, **kw):
-    first_fwd, second_fwd, twiddle, _, _ = transform_tables()
+    return call(
+        send_kernel, 1, [pl.BlockSpec(memory_space=pltpu.HBM)] * 4, spec((1024, SIDE)), out((1024, SIDE)),
+        scratch=[pltpu.VMEM((4, ROWS, SIDE), BF16), pltpu.SemaphoreType.DMA((4,))], **kw,
+    )(query, key, value, grad)
+
+
+def run_filter(features, filter_in, filter_mid, filter_out, place=seq_place, **kw):
     wide = lambda i: (0, i)
     hidden = spec((ORDER, STEP), wide)
-    half, full = out((ORDER, LENGTH), BF16), out((ORDER, LENGTH))
+    half, full = out((ORDER, HALF), BF16), out((ORDER, HALF))
     return call(
         functools.partial(filter_kernel, place),
-        LENGTH // STEP,
-        [spec((32, STEP), wide), spec((16, ORDER)), spec((ORDER, ORDER)), spec((ORDER, SIDE)), spec((1, SIDE)),
-         spec((256, 384)), spec((768, 256)), spec((SIDE, 256))],
-        [hidden] * 6 + [spec((512, 256)), spec((512, SIDE)), spec((512, SIDE))],
-        [half, half, full, half, half, full, out((512, 256)), out((512, SIDE)), out((512, SIDE))],
-        scratch=[pltpu.VMEM((1024, SIDE), F32)],
-        flops=8 * 10**9, nbytes=20 * MIB, **kw,
-    )(feature_table(), filter_in, filter_mid, filter_out, decay, first_fwd, second_fwd, twiddle)
+        HALF // STEP,
+        [spec((32, STEP), wide), spec((16, ORDER)), spec((ORDER, ORDER)), spec((ORDER, SIDE))],
+        [hidden] * 6 + [spec((256, SIDE))] * 2,
+        [half, half, full, half, half, full, out((256, SIDE)), out((256, SIDE))],
+        scratch=[pltpu.VMEM((512, SIDE), F32)],
+        flops=4 * 10**9, nbytes=10 * MIB, **kw,
+    )(features, filter_in, filter_mid, filter_out)
+
+
+def run_spectrum(mine, other, decay, place=seq_place, **kw):
+    first_fwd, second_fwd, twiddle, _, _ = transform_tables()
+    return call(
+        functools.partial(spectrum_kernel, place),
+        1,
+        [spec((256, SIDE))] * 2 + [spec((1, SIDE)), spec((256, 384)), spec((768, 256)), spec((SIDE, 256))],
+        [spec((512, 256)), spec((512, SIDE)), spec((512, SIDE))],
+        [out((512, 256)), out((512, SIDE)), out((512, SIDE))],
+        flops=10**9, nbytes=MIB, **kw,
+    )(mine, other, decay, first_fwd, second_fwd, twiddle)
 
 
 def run_convolve(field, spectrum, filt, window, decay, place=seq_place, **kw):
@@ -388,26 +424,26 @@
         1,
         [spec((1024, SIDE)), spec((512, 256)), spec((512, SIDE)), spec((512, SIDE)), spec((1, SIDE)),
          spec((256, 384)), spec((768, 256)), spec((SIDE, 256)), spec((768, 256)), spec((SIDE, 768))],
-        [spec((1024, SIDE)), spec((1024, SIDE)), spec((8, SIDE))],
-        [out((1024, SIDE)), out((1024, SIDE)), out((8, SIDE))],
+        [spec((1024, SIDE)), spec((512, SIDE)), spec((512, SIDE)), spec((8, SIDE))],
+        [out((1024, SIDE)), out((512, SIDE)), out((512, SIDE)), out((8, SIDE))],
         flops=4 * 10**9, nbytes=4 * MIB, **kw,
     )(field, spectrum, filt, window, decay, first_fwd, second_fwd, twiddle, second_inv, first_inv)
 
 
-def run_backward(hidden, dshaped, sums, filter_mid, filter_out, place=seq_place, **kw):
+def run_backward(features, hidden, mine, other, sums, filter_mid, filter_out, place=seq_place, **kw):
     wide = lambda i: (0, i)
     block = spec((ORDER, STEP), wide)
+    deep = spec((STEP // 16, SIDE), lambda i: (i, 0))
     return call(
         functools.partial(backward_kernel, place),
-        LENGTH // STEP,
-        [spec((32, STEP), wide)] + [block] * 6 + [spec((STEP // 16, SIDE), lambda i: (i, 0)), spec((8, SIDE)),
-         spec((ORDER, ORDER)), spec((ORDER, SIDE))],
+        HALF // STEP,
+        [spec((32, STEP), wide)] + [block] * 6 + [deep, deep, spec((8, SIDE)), spec((ORDER, ORDER)), spec((ORDER, SIDE))],
         spec((112, SIDE)),
         out((112, SIDE)),
         scratch=[pltpu.VMEM((SIDE, SIDE), F32), pltpu.VMEM((32, SIDE), F32), pltpu.VMEM((16, SIDE), F32)]
         + [pltpu.VMEM((ORDER, STEP), BF16)] * 4,
-        flops=8 * 10**9, nbytes=20 * MIB, **kw,
-    )(feature_table(), *hidden, dshaped, sums, filter_mid, filter_out)
+        flops=4 * 10**9, nbytes=10 * MIB, **kw,
+    )(features, *hidden, mine, other, sums, filter_mid, filter_out)
 
 
 def run_receive(query, key, value, grad, skip, field, **kw):
@@ -437,14 +473,16 @@
 def body(query, key, value, grad, filter_in, filter_mid, filter_out, decay_rate, skip_gain):
     decay = decay_rate.reshape(1, SIDE)
     skip = skip_gain.reshape(1, SIDE)
+    features = lax.dynamic_slice_in_dim(jnp.asarray(feature_table()), HALF * (lax.axis_index("seq") % 2), HALF, axis=1)
     sent = run_send(query, key, value, grad).reshape(SEQ, SEQ, SIDE)
     field = lax.all_to_all(sent, "seq", 0, 0, tiled=True).reshape(1024, SIDE)
-    *hidden, spectrum, filt, window = run_filter(filter_in, filter_mid, filter_out, decay)
-    sent, dshaped, sums = run_convolve(field, spectrum, filt, window, decay)
+    *hidden, mine, theirs = run_filter(features, filter_in, filter_mid, filter_out)
+    spectrum, filt, window = run_spectrum(mine, exchanged(theirs, "seq", 1), decay)
+    sent, mine, theirs, sums = run_convolve(field, spectrum, filt, window, decay)
     field = lax.all_to_all(sent.reshape(SEQ, SEQ, SIDE), "seq", 0, 0, tiled=True).reshape(1024, SIDE)
-    grads = run_backward(hidden, dshaped, sums, filter_mid, filter_out)
+    grads = run_backward(features, hidden, mine, exchanged(theirs, "seq", 1), sums, filter_mid, filter_out)
     output, grad_query, grad_key, grad_value = run_receive(query, key, value, grad, skip, field)
-    shared = group_sum(grads[:40], "chan", range(1, 8))
+    shared = group_sum(group_sum(grads[:40], "chan", (1,)), "chan", (2, 6, 5))
     grads = jnp.concatenate([shared, grads[40:]])
     grads = group_sum(grads, "seq", (8, 16, 24))
     grads = group_sum(grads, "seq", (2, 4, 6))

time: 107 us -> 86.3 us (0.81)
  the two profiles are of different devices: /device:TPU:32 before, /device:TPU:1 now
where the time goes in v2:
time: 86.3 us; the launch traced here: 85.9 us
  starting transfers between devices  37.6 us (44%)
  Pallas kernels  20.7 us (24%)
  waiting for transfers between devices  16.1 us (19%)
  local copies, waits for them, and re-layouts  10.4 us (12%)
  between operations  1.05 us (1%)
    ppermute x13, starting transfers between devices, exchanged(): lax.ppermute(x, axis, [(i, i ^ distance) for i in range(lax.axis_size(axi...  18 us
    ppermute x13, waiting for transfers between devices, exchanged(): lax.ppermute(x, axis, [(i, i ^ distance) for i in range(lax.axis_size(axi...  16.1 us
    all_to_all x1, starting transfers between devices, body(): lax.all_to_all(sent.reshape(SEQ, SEQ, SIDE), 'seq', 0, 0, tiled=True)  11.1 us
    unnamed x62, local copies, waits for them, and re-layouts  10.4 us
    all_to_all x1, starting transfers between devices, body(): field = lax.all_to_all(sent, 'seq', 0, 0, tiled=True).reshape(1024, SIDE)  8.6 us
    pallas_call x1, Pallas kernels, run_filter(): call(functools.partial(filter_kernel, place), HALF // STEP, [spec((32, ST...  6.67 us
    pallas_call x1, Pallas kernels, run_backward(): call(functools.partial(backward_kernel, place), HALF // STEP, [spec((32,...  5.47 us
    pallas_call x1, Pallas kernels, run_convolve(): call(functools.partial(convolve_kernel, place), 1, [spec((1024, SIDE)), s...  3.9 us
  transfers between devices with their start and end apart: 15, of which 7 were waited for; matrix products, arithmetic and copies ran while one was open for 0% of the time, Pallas kernels for 10%

profile of v2, /device:TPU:1, one launch (start us, length us, event | category | flops | bytes accessed | tf_op | source)
XLA Modules:
  0.0 85.9 jit_solution(2022081474856125855)
XLA Ops:
  0.6 0.0 copy-start
  0.7 0.9 %copy-done = bf16[512,128]{1,0:T(8,128)(2,1)S(1)} copy-done((bf16[512,128]{1,0:T(8,128)(2,1)S(1)}, bf16[512,128]{1,0:T(8,128)(2,1)}, u32[]{:S(2)}) %copy-start) | copy-done | bytes 131096
  1.6 0.9 %copy-done.2 = bf16[512,128]{1,0:T(8,128)(2,1)S(1)} copy-done((bf16[512,128]{1,0:T(8,128)(2,1)S(1)}, bf16[512,128]{1,0:T(8,128)(2,1)}, u32[]{:S(2)}) %copy-start.2) | copy-done | bytes 131096
  2.5 0.9 %copy-done.4 = bf16[512,128]{1,0:T(8,128)(2,1)S(1)} copy-done((bf16[512,128]{1,0:T(8,128)(2,1)S(1)}, bf16[512,128]{1,0:T(8,128)(2,1)}, u32[]{:S(2)}) %copy-start.4) | copy-done | bytes 131096
  3.4 0.9 %copy-done.6 = bf16[512,128]{1,0:T(8,128)(2,1)S(1)} copy-done((bf16[512,128]{1,0:T(8,128)(2,1)S(1)}, bf16[512,128]{1,0:T(8,128)(2,1)}, u32[]{:S(2)}) %copy-start.6) | copy-done | bytes 131096
  4.3 2.0 %shard_map.214 = f32[1024,128]{1,0:T(8,128)} custom-call(bf16[512,128]{1,0:T(8,128)(2,1)S(1)} %copy-done, bf16[512,128]{1,0:T(8,128)(2,1)S(1)} %copy-done.2, bf16[512,128]{1,0:T(8,128)(2,1)S(1)} %copy-done.4, bf16[512,128]{1,0:T(8,128)(2,1)S(1)} %copy-done.6), custom_call_target="tpu_custom_call" | custom-call | flops 1 | bytes 1 | tf_op jit(solution)/shard_map/pallas_call | solution.py:387
  6.3 8.6 %all-to-all-start = ((f32[32,32,128]{2,1,0:T(8,128)}), f32[32,32,128]{2,1,0:T(8,128)S(1)}, u32[]{:S(2)}, u32[]{:S(2)}) async-start(f32[32,32,128]{2,1,0:T(8,128)} %bitcast.1), calls=%async_computation | async-start | bytes 1048576 | tf_op jit(solution)/shard_map/all_to_all | solution.py:478
  14.9 0.0 copy-done.30
  15.0 0.0 copy-start.12
  15.0 0.0 copy-start.13
  15.0 0.0 copy-start.15
  15.0 0.0 copy-start.17
  15.1 6.7 %shard_map.215 = (bf16[64,8192]{1,0:T(8,128)(2,1)S(1)}, bf16[64,8192]{1,0:T(8,128)(2,1)S(1)}, f32[64,8192]{1,0:T(8,128)S(1)}, bf16[64,8192]{1,0:T(8,128)(2,1)S(1...) custom-call(bf16[32,8192]{1,0:T(8,128)(2,1)S(1)} %constant_dynamic-s, ...), custom_call_target="tpu_custom_call" | custom-call | flops 4000000000 | bytes 10485760 | tf_op jit(solution)/shard_map/pallas_call | solution.py:397
  21.7 1.3 %copy-done.18 = f32[64,8192]{1,0:T(8,128)} copy-done((f32[64,8192]{1,0:T(8,128)}, f32[64,8192]{1,0:T(8,128)S(1)}, u32[]{:S(2)}) %copy-start.18) | copy-done | bytes 2097176
  23.1 1.3 %copy-done.20 = f32[64,8192]{1,0:T(8,128)} copy-done((f32[64,8192]{1,0:T(8,128)}, f32[64,8192]{1,0:T(8,128)S(1)}, u32[]{:S(2)}) %copy-start.20) | copy-done | bytes 2097176
  24.4 1.0 %copy-done.22 = bf16[64,8192]{1,0:T(8,128)(2,1)} copy-done((bf16[64,8192]{1,0:T(8,128)(2,1)}, bf16[64,8192]{1,0:T(8,128)(2,1)S(1)}, u32[]{:S(2)}) %copy-start.22) | copy-done | bytes 1048600
  25.4 1.0 %copy-done.24 = bf16[64,8192]{1,0:T(8,128)(2,1)} copy-done((bf16[64,8192]{1,0:T(8,128)(2,1)}, bf16[64,8192]{1,0:T(8,128)(2,1)S(1)}, u32[]{:S(2)}) %copy-start.24) | copy-done | bytes 1048600
  26.4 1.0 %copy-done.26 = bf16[64,8192]{1,0:T(8,128)(2,1)} copy-done((bf16[64,8192]{1,0:T(8,128)(2,1)}, bf16[64,8192]{1,0:T(8,128)(2,1)S(1)}, u32[]{:S(2)}) %copy-start.26) | copy-done | bytes 1048600
  27.4 1.0 %copy-done.28 = bf16[64,8192]{1,0:T(8,128)(2,1)} copy-done((bf16[64,8192]{1,0:T(8,128)(2,1)}, bf16[64,8192]{1,0:T(8,128)(2,1)S(1)}, u32[]{:S(2)}) %copy-start.28) | copy-done | bytes 1048600
  28.4 0.2 collective-permute-start
  28.6 1.1 %collective-permute-done.other = f32[256,128]{1,0:T(8,128)S(1)} collective-permute-done((f32[256,128]{1,0:T(8,128)S(1)}, f32[256,128]{1,0:T(8,128)S(1)}, u32[]{:S(2)}, u32[]{:S(2)}) %collective-permute-start) | collective-permute-done | bytes 131104 | tf_op jit(solution)/shard_map/ppermute | solution.py:463
  29.8 0.0 copy-done.15
  29.8 0.0 copy-done.17
  29.8 0.8 shard_map.216
  30.6 0.0 all-to-all-done
  30.7 3.9 %shard_map.217 = (f32[1024,128]{1,0:T(8,128)}, f32[512,128]{1,0:T(8,128)S(1)}, f32[512,128]{1,0:T(8,128)S(1)}, f32[8,128]{1,0:T(8,128)S(1)}) custom-call(f32[1024,128]{1,0:T(8,128)S(1)} %bitcast.9, f32[512,256]{1,0:T(8,128)S(1)} %get-tuple-element.35.spectrum, f32[512,128]{1,0:T(8,128)S(1)} %get-tuple-element.36.filt, ...), custom_call_target="tpu_custom_call" | custom-call | flops 4000000000 | bytes 4194304 | tf_op jit(solution)/shard_map/pallas_call | solution.py:422
  34.6 0.2 collective-permute-start.1
  34.8 1.3 %collective-permute-done.1.other = f32[512,128]{1,0:T(8,128)S(1)} collective-permute-done((f32[512,128]{1,0:T(8,128)S(1)}, f32[512,128]{1,0:T(8,128)S(1)}, u32[]{:S(2)}, u32[]{:S(2)}) %collective-permute-start.1) | collective-permute-done | bytes 262176 | tf_op jit(solution)/shard_map/ppermute | solution.py:463
  36.1 0.0 copy-done.19
  36.2 5.5 %shard_map.219 = f32[112,128]{1,0:T(8,128)S(1)} custom-call(bf16[32,8192]{1,0:T(8,128)(2,1)S(1)} %constant_dynamic-slice_fusion.features, bf16[64,8192]{1,0:T(8,128)(2,1)S(1)} %copy-done.23, bf16[64,8192]{1,0:T(8,128)(2,1)S(1)} %copy-done.25, f32[64,8192]{1,0:T(8,128)S(1)} %copy-done.19, bf16[64,8192]{1,0:T(8,128)(2,1)S(1)} %copy-done.27, ...), custom_call_target="tpu_custom_call" | custom-call | flops 4000000000 | bytes 10485760 | tf_op jit(solution)/shard_map/pallas_call | solution.py:437
  41.6 0.0 copy-start.1
  41.7 0.0 copy-start.3
  41.7 0.0 copy-start.5
  41.7 0.0 copy-start.7
  41.7 0.0 copy-start.8
  41.7 1.7 %collective-permute-start.2 = (f32[40,128]{1,0:T(8,128)S(1)}, f32[40,128]{1,0:T(8,128)S(1)}, u32[]{:S(2)}, u32[]{:S(2)}) collective-permute-start(f32[40,128]{1,0:T(8,128)S(1)} %slice.8), channel_id=1, source_target_pairs={{0,1},{1,0},{2,3},{3,2},{4,5},{5,4},{6,7},{7,6},{8,9},{9,8},{10,11... | collective-permute-start | bytes 61448 | tf_op jit(solution)/shard_map/ppermute | solution.py:463
  43.4 1.2 %collective-permute-done.2 = f32[40,128]{1,0:T(8,128)S(1)} collective-permute-done((f32[40,128]{1,0:T(8,128)S(1)}, f32[40,128]{1,0:T(8,128)S(1)}, u32[]{:S(2)}, u32[]{:S(2)}) %collective-permute-start.2) | collective-permute-done | bytes 20512 | tf_op jit(solution)/shard_map/ppermute | solution.py:463
  44.6 6.3 %collective-permute-start.5 = (f32[40,128]{1,0:T(8,128)S(1)}, f32[40,128]{1,0:T(8,128)S(1)}, u32[]{:S(2)}, u32[]{:S(2)}) collective-permute-start(f32[40,128]{1,0:T(8,128)S(1)} %slice_add_fusion), channel_id=1, source_target_pairs={{0,5},{1,4},{2,7},{3,6},{4,1},{5,0},{6,3},{7,2},{8,13},{9,12},{10,... | collective-permute-start | bytes 61448 | tf_op jit(solution)/shard_map/ppermute | solution.py:463
  50.9 0.3 collective-permute-start.4
  51.2 0.9 %collective-permute-start.3 = (f32[40,128]{1,0:T(8,128)S(1)}, f32[40,128]{1,0:T(8,128)S(1)}, u32[]{:S(2)}, u32[]{:S(2)}) collective-permute-start(f32[40,128]{1,0:T(8,128)S(1)} %slice_add_fusion), channel_id=1, source_target_pairs={{0,2},{1,3},{2,0},{3,1},{4,6},{5,7},{6,4},{7,5},{8,10},{9,11},{10,... | collective-permute-start | bytes 61448 | tf_op jit(solution)/shard_map/ppermute | solution.py:463
  52.1 0.0 collective-permute-done.5
  52.1 3.5 %collective-permute-done.4 = f32[40,128]{1,0:T(8,128)S(1)} collective-permute-done((f32[40,128]{1,0:T(8,128)S(1)}, f32[40,128]{1,0:T(8,128)S(1)}, u32[]{:S(2)}, u32[]{:S(2)}) %collective-permute-start.4) | collective-permute-done | bytes 20512 | tf_op jit(solution)/shard_map/ppermute | solution.py:463
  55.7 0.0 collective-permute-done.3
  55.7 3.0 %collective-permute-start.7 = (f32[112,128]{1,0:T(8,128)S(1)}, f32[112,128]{1,0:T(8,128)S(1)}, u32[]{:S(2)}, u32[]{:S(2)}) collective-permute-start(f32[112,128]{1,0:T(8,128)S(1)} %pad_maximum_fusion), channel_id=1, source_target_pairs={{0,128},{8,136},{16,144},{24,152},{32,160},{40,168},{48,176},{56,1... | collective-permute-start | bytes 172040 | tf_op jit(solution)/shard_map/ppermute | solution.py:463
  58.7 0.9 %collective-permute-start.8 = (f32[112,128]{1,0:T(8,128)S(1)}, f32[112,128]{1,0:T(8,128)S(1)}, u32[]{:S(2)}, u32[]{:S(2)}) collective-permute-start(f32[112,128]{1,0:T(8,128)S(1)} %pad_maximum_fusion), channel_id=1, source_target_pairs={{0,192},{8,200},{16,208},{24,216},{32,224},{40,232},{48,240},{56,2... | collective-permute-start | bytes 172040 | tf_op jit(solution)/shard_map/ppermute | solution.py:463
  59.6 0.0 collective-permute-start.6
  59.6 11.1 %all-to-all-start.1 = ((f32[32,32,128]{2,1,0:T(8,128)}), f32[32,32,128]{2,1,0:T(8,128)S(1)}, u32[]{:S(2)}, u32[]{:S(2)}) async-start(f32[32,32,128]{2,1,0:T(8,128)} %bitcast.4), calls=%async_computation.1 | async-start | bytes 1048576 | tf_op jit(solution)/shard_map/all_to_all | solution.py:482
  70.6 0.0 collective-permute-done.7
  70.6 0.0 collective-permute-done.8
  70.6 0.0 collective-permute-done.6
  70.7 2.7 %collective-permute-start.11 = (f32[112,128]{1,0:T(8,128)S(1)}, f32[112,128]{1,0:T(8,128)S(1)}, u32[]{:S(2)}, u32[]{:S(2)}) collective-permute-start(f32[112,128]{1,0:T(8,128)S(1)} %add_add_fusion.1), channel_id=1, source_target_pairs={{0,48},{8,56},{16,32},{24,40},{32,16},{40,24},{48,0},{56,8},{64,11... | collective-permute-start | bytes 172040 | tf_op jit(solution)/shard_map/ppermute | solution.py:463
  73.4 0.6 collective-permute-start.10
  73.9 0.1 collective-permute-start.9
  74.0 5.8 %collective-permute-done.11 = f32[112,128]{1,0:T(8,128)S(1)} collective-permute-done((f32[112,128]{1,0:T(8,128)S(1)}, f32[112,128]{1,0:T(8,128)S(1)}, u32[]{:S(2)}, u32[]{:S(2)}) %collective-permute-start.11) | collective-permute-done | bytes 57376 | tf_op jit(solution)/shard_map/ppermute | solution.py:463
  79.9 2.2 %collective-permute-done.10 = f32[112,128]{1,0:T(8,128)S(1)} collective-permute-done((f32[112,128]{1,0:T(8,128)S(1)}, f32[112,128]{1,0:T(8,128)S(1)}, u32[]{:S(2)}, u32[]{:S(2)}) %collective-permute-start.10) | collective-permute-done | bytes 57376 | tf_op jit(solution)/shard_map/ppermute | solution.py:463
  82.1 0.0 collective-permute-done.9
  82.1 1.0 %collective-permute-start.12 = (f32[112,128]{1,0:T(8,128)S(1)}, f32[112,128]{1,0:T(8,128)S(1)}, u32[]{:S(2)}, u32[]{:S(2)}) collective-permute-start(f32[112,128]{1,0:T(8,128)S(1)} %add_add_fusion.mine), channel_id=1, source_target_pairs={{0,8},{8,0},{16,24},{24,16},{32,40},{40,32},{48,56},{56,48},{64,72... | collective-permute-start | bytes 172040 | tf_op jit(solution)/shard_map/ppermute | solution.py:463
  83.1 0.9 %collective-permute-done.12.other = f32[112,128]{1,0:T(8,128)S(1)} collective-permute-done((f32[112,128]{1,0:T(8,128)S(1)}, f32[112,128]{1,0:T(8,128)S(1)}, u32[]{:S(2)}, u32[]{:S(2)}) %collective-permute-start.12) | collective-permute-done | bytes 57376 | tf_op jit(solution)/shard_map/ppermute | solution.py:463
  84.0 0.7 shard_map.220
  84.7 0.0 all-to-all-done.1
  84.7 0.0 copy-done.5
  84.8 0.0 copy-done.7
  84.8 0.0 copy-done.8
  84.8 1.2 %shard_map.218 = (bf16[512,128]{1,0:T(8,128)(2,1)}, bf16[512,128]{1,0:T(8,128)(2,1)}, bf16[512,128]{1,0:T(8,128)(2,1)}, bf16[512,128]{1,0:T(8,128)(2,1)}) custom-call(bf16[512,128]{1,0:T(8,128)(2,1)S(1)} %copy-done.1, bf16[512,128]{1,0:T(8,128)(2,1)S(1)} %copy-done.3, bf16[512,128]{1,0:T(8,128)(2,1)S(1)} %copy-done.5, bf16[512,128]{1,0:T(8,128)(2,1)S(1)} %copy-done.7, ...), custom_call_target="tpu_custom_call" | custom-call | flops 1 | bytes 1 | tf_op jit(solution)/shard_map/pallas_call | solution.py:451
  (43 shorter events, 0.2 us)
Async XLA Ops:
  0.6 0.9 %copy-start = (bf16[512,128]{1,0:T(8,128)(2,1)S(1)}, bf16[512,128]{1,0:T(8,128)(2,1)}, u32[]{:S(2)}) copy-start(bf16[512,128]{1,0:T(8,128)(2,1)} %query.3) | copy-start | bytes 393220
  1.6 0.9 %copy-start.2 = (bf16[512,128]{1,0:T(8,128)(2,1)S(1)}, bf16[512,128]{1,0:T(8,128)(2,1)}, u32[]{:S(2)}) copy-start(bf16[512,128]{1,0:T(8,128)(2,1)} %key.3) | copy-start | bytes 393220
  2.5 0.9 %copy-start.4 = (bf16[512,128]{1,0:T(8,128)(2,1)S(1)}, bf16[512,128]{1,0:T(8,128)(2,1)}, u32[]{:S(2)}) copy-start(bf16[512,128]{1,0:T(8,128)(2,1)} %value.3) | copy-start | bytes 393220
  3.4 0.9 %copy-start.6 = (bf16[512,128]{1,0:T(8,128)(2,1)S(1)}, bf16[512,128]{1,0:T(8,128)(2,1)}, u32[]{:S(2)}) copy-start(bf16[512,128]{1,0:T(8,128)(2,1)} %grad.3) | copy-start | bytes 393220
  4.3 10.7 %copy-start.30 = (bf16[32,16384]{1,0:T(8,128)(2,1)S(1)}, bf16[32,16384]{1,0:T(8,128)(2,1)}, u32[]{:S(2)}) copy-start(bf16[32,16384]{1,0:T(8,128)(2,1)} %constant.36.clone) | copy-start | bytes 3145732
  4.3 10.7 %copy-start.9 = (f32[64,64]{1,0:T(8,128)S(1)}, f32[64,64]{1,0:T(8,128)}, u32[]{:S(2)}) copy-start(f32[64,64]{1,0:T(8,128)} %filter_mid.3) | copy-start | bytes 49156
  4.3 10.7 %copy-start.10 = (f32[64,128]{1,0:T(8,128)S(1)}, f32[64,128]{1,0:T(8,128)}, u32[]{:S(2)}) copy-start(f32[64,128]{1,0:T(8,128)} %filter_out.3) | copy-start | bytes 98308
  4.3 10.7 %copy-start.11 = (f32[16,64]{1,0:T(8,128)S(1)}, f32[16,64]{1,0:T(8,128)}, u32[]{:S(2)}) copy-start(f32[16,64]{1,0:T(8,128)} %filter_in.1) | copy-start | bytes 12292
  6.3 24.3 %all-to-all-start = ((f32[32,32,128]{2,1,0:T(8,128)}), f32[32,32,128]{2,1,0:T(8,128)S(1)}, u32[]{:S(2)}, u32[]{:S(2)}) async-start(f32[32,32,128]{2,1,0:T(8,128)} %bitcast.1), calls=%async_computation | async-start | bytes 1048576 | tf_op jit(solution)/shard_map/all_to_all | solution.py:478
  15.0 14.8 %copy-start.12 = (f32[128]{0:T(128)S(1)}, f32[128]{0:T(128)}, u32[]{:S(2)}) copy-start(f32[128]{0:T(128)} %param.22) | copy-start | bytes 1540
  15.0 14.7 %copy-start.13 = (bf16[768,256]{1,0:T(8,128)(2,1)S(1)}, bf16[768,256]{1,0:T(8,128)(2,1)}, u32[]{:S(2)}) copy-start(bf16[768,256]{1,0:T(8,128)(2,1)} %constant.38.clone.second_fwd) | copy-start | bytes 1179652
  15.0 14.7 %copy-start.15 = (bf16[256,384]{1,0:T(8,128)(2,1)S(1)}, bf16[256,384]{1,0:T(8,128)(2,1)}, u32[]{:S(2)}) copy-start(bf16[256,384]{1,0:T(8,128)(2,1)} %constant.37.clone.first_fwd) | copy-start | bytes 589828
  15.0 14.7 %copy-start.17 = (f32[128,256]{1,0:T(8,128)S(1)}, f32[128,256]{1,0:T(8,128)}, u32[]{:S(2)}) copy-start(f32[128,256]{1,0:T(8,128)} %constant.39.clone.twiddle) | copy-start | bytes 393220
  21.7 1.3 %copy-start.18 = (f32[64,8192]{1,0:T(8,128)}, f32[64,8192]{1,0:T(8,128)S(1)}, u32[]{:S(2)}) copy-start(f32[64,8192]{1,0:T(8,128)S(1)} %get-tuple-element.45.cos1) | copy-start | bytes 6291460
  23.1 1.3 %copy-start.20 = (f32[64,8192]{1,0:T(8,128)}, f32[64,8192]{1,0:T(8,128)S(1)}, u32[]{:S(2)}) copy-start(f32[64,8192]{1,0:T(8,128)S(1)} %get-tuple-element.48.cos2) | copy-start | bytes 6291460
  24.4 1.0 %copy-start.22 = (bf16[64,8192]{1,0:T(8,128)(2,1)}, bf16[64,8192]{1,0:T(8,128)(2,1)S(1)}, u32[]{:S(2)}) copy-start(bf16[64,8192]{1,0:T(8,128)(2,1)S(1)} %get-tuple-element.43.h1_high) | copy-start | bytes 3145732
  25.4 1.0 %copy-start.24 = (bf16[64,8192]{1,0:T(8,128)(2,1)}, bf16[64,8192]{1,0:T(8,128)(2,1)S(1)}, u32[]{:S(2)}) copy-start(bf16[64,8192]{1,0:T(8,128)(2,1)S(1)} %get-tuple-element.44.h1_low) | copy-start | bytes 3145732
  26.4 1.0 %copy-start.26 = (bf16[64,8192]{1,0:T(8,128)(2,1)}, bf16[64,8192]{1,0:T(8,128)(2,1)S(1)}, u32[]{:S(2)}) copy-start(bf16[64,8192]{1,0:T(8,128)(2,1)S(1)} %get-tuple-element.46.h2_high) | copy-start | bytes 3145732
  27.4 1.0 %copy-start.28 = (bf16[64,8192]{1,0:T(8,128)(2,1)}, bf16[64,8192]{1,0:T(8,128)(2,1)S(1)}, u32[]{:S(2)}) copy-start(bf16[64,8192]{1,0:T(8,128)(2,1)S(1)} %get-tuple-element.47.h2_low) | copy-start | bytes 3145732
  28.4 2.2 %copy-start.14 = (bf16[768,256]{1,0:T(8,128)(2,1)S(1)}, bf16[768,256]{1,0:T(8,128)(2,1)}, u32[]{:S(2)}) copy-start(bf16[768,256]{1,0:T(8,128)(2,1)} %constant.40.clone.second_inv) | copy-start | bytes 1179652
  28.4 2.2 %copy-start.16 = (bf16[128,768]{1,0:T(8,128)(2,1)S(1)}, bf16[128,768]{1,0:T(8,128)(2,1)}, u32[]{:S(2)}) copy-start(bf16[128,768]{1,0:T(8,128)(2,1)} %constant.41.clone.first_inv) | copy-start | bytes 589828
  28.4 1.3 %collective-permute-start = (f32[256,128]{1,0:T(8,128)S(1)}, f32[256,128]{1,0:T(8,128)S(1)}, u32[]{:S(2)}, u32[]{:S(2)}) collective-permute-start(f32[256,128]{1,0:T(8,128)S(1)} %get-tuple-element.34), channel_id=1, source_target_pairs={{0,8},{8,0},{16,24},{24,16},{32,40},{40,32},{48,56},{56,48},{64,72... | collective-permute-start | bytes 393224 | tf_op jit(solution)/shard_map/ppermute | solution.py:463
  30.6 5.5 %copy-start.19 = (f32[64,8192]{1,0:T(8,128)S(1)}, f32[64,8192]{1,0:T(8,128)}, u32[]{:S(2)}) copy-start(f32[64,8192]{1,0:T(8,128)} %copy-done.18) | copy-start | bytes 6291460
  30.7 5.5 %copy-start.21 = (f32[64,8192]{1,0:T(8,128)S(1)}, f32[64,8192]{1,0:T(8,128)}, u32[]{:S(2)}) copy-start(f32[64,8192]{1,0:T(8,128)} %copy-done.20) | copy-start | bytes 6291460
  30.7 5.5 %copy-start.23 = (bf16[64,8192]{1,0:T(8,128)(2,1)S(1)}, bf16[64,8192]{1,0:T(8,128)(2,1)}, u32[]{:S(2)}) copy-start(bf16[64,8192]{1,0:T(8,128)(2,1)} %copy-done.22) | copy-start | bytes 3145732
  30.7 5.5 %copy-start.25 = (bf16[64,8192]{1,0:T(8,128)(2,1)S(1)}, bf16[64,8192]{1,0:T(8,128)(2,1)}, u32[]{:S(2)}) copy-start(bf16[64,8192]{1,0:T(8,128)(2,1)} %copy-done.24) | copy-start | bytes 3145732
  30.7 5.5 %copy-start.27 = (bf16[64,8192]{1,0:T(8,128)(2,1)S(1)}, bf16[64,8192]{1,0:T(8,128)(2,1)}, u32[]{:S(2)}) copy-start(bf16[64,8192]{1,0:T(8,128)(2,1)} %copy-done.26) | copy-start | bytes 3145732
  30.7 5.5 %copy-start.29 = (bf16[64,8192]{1,0:T(8,128)(2,1)S(1)}, bf16[64,8192]{1,0:T(8,128)(2,1)}, u32[]{:S(2)}) copy-start(bf16[64,8192]{1,0:T(8,128)(2,1)} %copy-done.28) | copy-start | bytes 3145732
  34.6 1.5 %collective-permute-start.1 = (f32[512,128]{1,0:T(8,128)S(1)}, f32[512,128]{1,0:T(8,128)S(1)}, u32[]{:S(2)}, u32[]{:S(2)}) collective-permute-start(f32[512,128]{1,0:T(8,128)S(1)} %get-tuple-element.50), channel_id=1, source_target_pairs={{0,8},{8,0},{16,24},{24,16},{32,40},{40,32},{48,56},{56,48},{64,72... | collective-permute-start | bytes 786440 | tf_op jit(solution)/shard_map/ppermute | solution.py:463
  41.6 43.1 %copy-start.1 = (bf16[512,128]{1,0:T(8,128)(2,1)S(1)}, bf16[512,128]{1,0:T(8,128)(2,1)}, u32[]{:S(2)}) copy-start(bf16[512,128]{1,0:T(8,128)(2,1)} %query.3) | copy-start | bytes 393220
  41.7 43.1 %copy-start.3 = (bf16[512,128]{1,0:T(8,128)(2,1)S(1)}, bf16[512,128]{1,0:T(8,128)(2,1)}, u32[]{:S(2)}) copy-start(bf16[512,128]{1,0:T(8,128)(2,1)} %key.3) | copy-start | bytes 393220
  41.7 43.1 %copy-start.5 = (bf16[512,128]{1,0:T(8,128)(2,1)S(1)}, bf16[512,128]{1,0:T(8,128)(2,1)}, u32[]{:S(2)}) copy-start(bf16[512,128]{1,0:T(8,128)(2,1)} %value.3) | copy-start | bytes 393220
  41.7 43.1 %copy-start.7 = (bf16[512,128]{1,0:T(8,128)(2,1)S(1)}, bf16[512,128]{1,0:T(8,128)(2,1)}, u32[]{:S(2)}) copy-start(bf16[512,128]{1,0:T(8,128)(2,1)} %grad.3) | copy-start | bytes 393220
  41.7 43.1 %copy-start.8 = (f32[128]{0:T(128)S(1)}, f32[128]{0:T(128)}, u32[]{:S(2)}) copy-start(f32[128]{0:T(128)} %param.23) | copy-start | bytes 1540
  41.7 2.9 %collective-permute-start.2 = (f32[40,128]{1,0:T(8,128)S(1)}, f32[40,128]{1,0:T(8,128)S(1)}, u32[]{:S(2)}, u32[]{:S(2)}) collective-permute-start(f32[40,128]{1,0:T(8,128)S(1)} %slice.8), channel_id=1, source_target_pairs={{0,1},{1,0},{2,3},{3,2},{4,5},{5,4},{6,7},{7,6},{8,9},{9,8},{10,11... | collective-permute-start | bytes 61448 | tf_op jit(solution)/shard_map/ppermute | solution.py:463
  44.6 7.5 %collective-permute-start.5 = (f32[40,128]{1,0:T(8,128)S(1)}, f32[40,128]{1,0:T(8,128)S(1)}, u32[]{:S(2)}, u32[]{:S(2)}) collective-permute-start(f32[40,128]{1,0:T(8,128)S(1)} %slice_add_fusion), channel_id=1, source_target_pairs={{0,5},{1,4},{2,7},{3,6},{4,1},{5,0},{6,3},{7,2},{8,13},{9,12},{10,... | collective-permute-start | bytes 61448 | tf_op jit(solution)/shard_map/ppermute | solution.py:463
  50.9 4.7 %collective-permute-start.4 = (f32[40,128]{1,0:T(8,128)S(1)}, f32[40,128]{1,0:T(8,128)S(1)}, u32[]{:S(2)}, u32[]{:S(2)}) collective-permute-start(f32[40,128]{1,0:T(8,128)S(1)} %slice_add_fusion), channel_id=1, source_target_pairs={{0,6},{1,7},{2,4},{3,5},{4,2},{5,3},{6,0},{7,1},{8,14},{9,15},{10,... | collective-permute-start | bytes 61448 | tf_op jit(solution)/shard_map/ppermute | solution.py:463
  51.2 4.5 %collective-permute-start.3 = (f32[40,128]{1,0:T(8,128)S(1)}, f32[40,128]{1,0:T(8,128)S(1)}, u32[]{:S(2)}, u32[]{:S(2)}) collective-permute-start(f32[40,128]{1,0:T(8,128)S(1)} %slice_add_fusion), channel_id=1, source_target_pairs={{0,2},{1,3},{2,0},{3,1},{4,6},{5,7},{6,4},{7,5},{8,10},{9,11},{10,... | collective-permute-start | bytes 61448 | tf_op jit(solution)/shard_map/ppermute | solution.py:463
  55.7 14.9 %collective-permute-start.7 = (f32[112,128]{1,0:T(8,128)S(1)}, f32[112,128]{1,0:T(8,128)S(1)}, u32[]{:S(2)}, u32[]{:S(2)}) collective-permute-start(f32[112,128]{1,0:T(8,128)S(1)} %pad_maximum_fusion), channel_id=1, source_target_pairs={{0,128},{8,136},{16,144},{24,152},{32,160},{40,168},{48,176},{56,1... | collective-permute-start | bytes 172040 | tf_op jit(solution)/shard_map/ppermute | solution.py:463
  58.7 12.0 %collective-permute-start.8 = (f32[112,128]{1,0:T(8,128)S(1)}, f32[112,128]{1,0:T(8,128)S(1)}, u32[]{:S(2)}, u32[]{:S(2)}) collective-permute-start(f32[112,128]{1,0:T(8,128)S(1)} %pad_maximum_fusion), channel_id=1, source_target_pairs={{0,192},{8,200},{16,208},{24,216},{32,224},{40,232},{48,240},{56,2... | collective-permute-start | bytes 172040 | tf_op jit(solution)/shard_map/ppermute | solution.py:463
  59.6 11.1 %collective-permute-start.6 = (f32[112,128]{1,0:T(8,128)S(1)}, f32[112,128]{1,0:T(8,128)S(1)}, u32[]{:S(2)}, u32[]{:S(2)}) collective-permute-start(f32[112,128]{1,0:T(8,128)S(1)} %pad_maximum_fusion), channel_id=1, source_target_pairs={{0,64},{8,72},{16,80},{24,88},{32,96},{40,104},{48,112},{56,120},{... | collective-permute-start | bytes 172040 | tf_op jit(solution)/shard_map/ppermute | solution.py:463
  59.6 25.2 %all-to-all-start.1 = ((f32[32,32,128]{2,1,0:T(8,128)}), f32[32,32,128]{2,1,0:T(8,128)S(1)}, u32[]{:S(2)}, u32[]{:S(2)}) async-start(f32[32,32,128]{2,1,0:T(8,128)} %bitcast.4), calls=%async_computation.1 | async-start | bytes 1048576 | tf_op jit(solution)/shard_map/all_to_all | solution.py:482
  70.7 9.2 %collective-permute-start.11 = (f32[112,128]{1,0:T(8,128)S(1)}, f32[112,128]{1,0:T(8,128)S(1)}, u32[]{:S(2)}, u32[]{:S(2)}) collective-permute-start(f32[112,128]{1,0:T(8,128)S(1)} %add_add_fusion.1), channel_id=1, source_target_pairs={{0,48},{8,56},{16,32},{24,40},{32,16},{40,24},{48,0},{56,8},{64,11... | collective-permute-start | bytes 172040 | tf_op jit(solution)/shard_map/ppermute | solution.py:463
  73.4 8.7 %collective-permute-start.10 = (f32[112,128]{1,0:T(8,128)S(1)}, f32[112,128]{1,0:T(8,128)S(1)}, u32[]{:S(2)}, u32[]{:S(2)}) collective-permute-start(f32[112,128]{1,0:T(8,128)S(1)} %add_add_fusion.1), channel_id=1, source_target_pairs={{0,32},{8,40},{16,48},{24,56},{32,0},{40,8},{48,16},{56,24},{64,96... | collective-permute-start | bytes 172040 | tf_op jit(solution)/shard_map/ppermute | solution.py:463
  73.9 8.2 %collective-permute-start.9 = (f32[112,128]{1,0:T(8,128)S(1)}, f32[112,128]{1,0:T(8,128)S(1)}, u32[]{:S(2)}, u32[]{:S(2)}) collective-permute-start(f32[112,128]{1,0:T(8,128)S(1)} %add_add_fusion.1), channel_id=1, source_target_pairs={{0,16},{8,24},{16,0},{24,8},{32,48},{40,56},{48,32},{56,40},{64,80... | collective-permute-start | bytes 172040 | tf_op jit(solution)/shard_map/ppermute | solution.py:463
  82.1 1.9 %collective-permute-start.12 = (f32[112,128]{1,0:T(8,128)S(1)}, f32[112,128]{1,0:T(8,128)S(1)}, u32[]{:S(2)}, u32[]{:S(2)}) collective-permute-start(f32[112,128]{1,0:T(8,128)S(1)} %add_add_fusion.mine), channel_id=1, source_target_pairs={{0,8},{8,0},{16,24},{24,16},{32,40},{40,32},{48,56},{56,48},{64,72... | collective-permute-start | bytes 172040 | tf_op jit(solution)/shard_map/ppermute | solution.py:463

commit v3 on v2

--- a/solution.py
+++ b/solution.py
@@ -8,7 +8,7 @@
 from jax import lax
 from jax.experimental import pallas as pl
 from jax.experimental.pallas import tpu as pltpu
-from jax.sharding import PartitionSpec as P
+from jax.sharding import Mesh, PartitionSpec as P
 
 F32 = jnp.float32
 BF16 = jnp.bfloat16
@@ -22,6 +22,7 @@
 PIECE = 256
 HALF = LENGTH // 2
 MIB = 1 << 20
+SEQ_AXES = ("x", "y", "core")
 
 
 def split_table(table):
@@ -145,6 +146,10 @@
 
 def out(shape, dtype=F32):
     return jax.ShapeDtypeStruct(shape, dtype)
+
+
+def in_hbm(x):
+    return pltpu.with_memory_space_constraint(x, pltpu.HBM)
 
 
 def call(kernel, grid, in_specs, out_specs, out_shape, scratch=(), limit=16, flops=1, nbytes=1, interpret=False):
@@ -256,25 +261,24 @@
             theirs[pl.ds(64 * c, 64), :] = shaped[pl.ds(c + OWN, 64, stride=8), :]
 
 
-def spectrum_kernel(place, mine, other, decay, first_fwd, second_fwd, twiddle, spectrum, filt, window):
-    me = place()
+def filter_fields(me, mine, other, decay):
     time = position_grid()
+    lower = me % 2 == 0
     rates = jnp.sum(own_channels(me) * decay[...], axis=1, keepdims=True)
-    lower = me % 2 == 0
-    fields = []
     for c in range(OWN):
         rate = rates[c : c + 1, :]
-        window_c = jnp.exp(-rate * time) * jnp.sqrt(rate + 1.0 / LENGTH)
+        window = jnp.exp(-rate * time) * jnp.sqrt(rate + 1.0 / LENGTH)
         here, there = mine[pl.ds(64 * c, 64), :], other[pl.ds(64 * c, 64), :]
-        field = jnp.concatenate([jnp.where(lower, here, there), jnp.where(lower, there, here)]) * window_c
-        window[pl.ds(SIDE * c, SIDE), :] = window_c
-        filt[pl.ds(SIDE * c, SIDE), :] = field
-        fields.append(field)
+        yield window, jnp.concatenate([jnp.where(lower, here, there), jnp.where(lower, there, here)]), rate
+
+
+def spectrum_kernel(place, mine, other, decay, first_fwd, second_fwd, twiddle, spectrum):
+    fields = [window * shaped for window, shaped, _ in filter_fields(place(), mine, other, decay)]
     spectrum[...] = forward_rows(fields, first_fwd, second_fwd, twiddle)
 
 
-def convolve_kernel(place, field, spectrum, filt, window, decay, first_fwd, second_fwd, twiddle, second_inv, first_inv,
-                    sent, mine, theirs, sums):
+def convolve_kernel(place, field, spectrum, shaped_mine, shaped_other, decay, first_fwd, second_fwd, twiddle, second_inv,
+                    first_inv, sent, mine, theirs, sums):
     fields = []
     for c in range(OWN):
         for offset in (0, OWN):
@@ -302,36 +306,35 @@
     time = position_grid()
     me = place()
     lower = me % 2 == 0
-    rates = jnp.sum(own_channels(me) * decay[...], axis=1, keepdims=True)
-    zeros = jnp.zeros((64, SIDE), F32)
-    for c in range(OWN):
+    pair = lambda x: (jnp.where(lower, x, 0.0), jnp.where(lower, 0.0, x))
+    for c, (window, shaped, rate) in enumerate(filter_fields(me, shaped_mine, shaped_other, decay)):
         for offset, result in ((0, results[2 * c]), (OWN, results[2 * c + 1])):
             for h in range(ROWS // SIDE):
                 sent[pl.ds(8 * h + offset + c, SEQ, stride=SEQ), :] = result[SEQ * h : SEQ * (h + 1), :]
-        dfilt = results[2 * OWN + c]
-        dshaped = dfilt * window[pl.ds(SIDE * c, SIDE), :]
-        mine[pl.ds(c, 64, stride=8), :] = jnp.where(lower, dshaped[:64], dshaped[64:])
-        mine[pl.ds(c + OWN, 64, stride=8), :] = zeros
-        theirs[pl.ds(c, 64, stride=8), :] = zeros
-        theirs[pl.ds(c + OWN, 64, stride=8), :] = jnp.where(lower, dshaped[64:], dshaped[:64])
-        slope = 0.5 / (rates[c : c + 1, :] + 1.0 / LENGTH) - time
-        sums[pl.ds(c, 1), :] = jnp.sum(dfilt * filt[pl.ds(SIDE * c, SIDE), :] * slope, axis=0, keepdims=True)
-        sums[pl.ds(c + OWN, 1), :] = jnp.sum(fields[2 * c] * fields[2 * c + 1], axis=0, keepdims=True)
+        dshaped = results[2 * OWN + c] * window
+        slope = 0.5 / (rate + 1.0 / LENGTH) - time
+        for part, sum_row, value in (
+            (mine, None, jnp.where(lower, dshaped[:64], dshaped[64:])),
+            (theirs, None, jnp.where(lower, dshaped[64:], dshaped[:64])),
+            (sums, 0, jnp.sum(dshaped * shaped * slope, axis=0, keepdims=True)),
+            (sums, 8, jnp.sum(fields[2 * c] * fields[2 * c + 1], axis=0, keepdims=True)),
+        ):
+            for offset, v in zip((0, OWN), pair(value)):
+                rows = pl.ds(c + offset, 64, stride=8) if sum_row is None else pl.ds(sum_row + c + offset, 1)
+                part[rows, :] = v
+
+
+def pair_channels(place):
+    row = lax.broadcasted_iota(jnp.int32, (8, SIDE), 0)
+    lane = lax.broadcasted_iota(jnp.int32, (8, SIDE), 1)
+    return jnp.where(lane == place - place % 2 + row // OWN + SEQ * (row % OWN), 1.0, 0.0).astype(F32)
 
 
 def backward_kernel(place, features, h1_high, h1_low, cos1, h2_high, h2_low, cos2, mine, other, sums, filter_mid, filter_out,
-                    grads, grad_mid, grad_in, grad_out, d2_high, d2_low, d1_high, d1_low):
+                    grads, total, d2_high, d2_low, d1_high, d1_low):
     step = pl.program_id(0)
-    own = own_channels(place())
-    weight3 = weight_left(dot_nt(filter_out[...], own, lax.Precision.HIGHEST), 1)
+    weight3 = weight_left(dot_nt(filter_out[...], pair_channels(place()), lax.Precision.HIGHEST), 1)
     weight2 = weight_left(filter_mid[...], 1)
-
-    @pl.when(step == 0)
-    def _():
-        grad_mid[...] = jnp.zeros_like(grad_mid)
-        grad_in[...] = jnp.zeros_like(grad_in)
-        grad_out[...] = jnp.zeros_like(grad_out)
-
     pieces = [pl.ds(PIECE * k, PIECE) for k in range(STEP // PIECE)]
     shaped_high, shaped_low = halves(
         jnp.concatenate([mine[pl.ds(8 * m, 8), :] + other[pl.ds(8 * m, 8), :] for m in range(STEP // SIDE)], axis=1)
@@ -345,55 +348,67 @@
         d1_high[:, piece], d1_low[:, piece] = halves(
             dot(weight2, jnp.concatenate([high, d2_low[:, piece], high])) * cos1[:, piece]
         )
-    grad_mid[...] += dot_nt(jnp.concatenate([h1_high[...], h1_low[...]]), jnp.concatenate([d2_high[...], d2_low[...]]))
-    grad_in[...] += dot_nt(features[...], jnp.concatenate([d1_high[...], d1_low[...]]))
-    grad_out[...] += dot_nt(jnp.concatenate([shaped_high, shaped_low]), jnp.concatenate([h2_high[...], h2_low[...]]))
+    left = jnp.concatenate([h1_high[...], h1_low[...], h2_high[...], h2_low[...], d1_high[...], d1_low[...]])
+    right = jnp.concatenate([d2_high[...], d2_low[...], shaped_high, shaped_low, features[...]])
+    product = dot_nt(left, right)
+
+    @pl.when(step == 0)
+    def _():
+        total[...] = product
+
+    @pl.when(step > 0)
+    def _():
+        total[...] += product
 
     @pl.when(step == HALF // STEP - 1)
     def _():
-        def joined(x, half):
-            return x[:half, :ORDER] + (x[:half, ORDER:] + x[half:, :ORDER])
-
-        mid = joined(grad_mid, 64)
-        first = joined(grad_in, 16)
-        third = joined(grad_out, 8)
+        mid = total[:64, :64] + (total[:64, 64:128] + total[64:128, :64])
         grads[pl.ds(0, 32), :] = jnp.concatenate([mid[:32], mid[32:]], axis=1)
+        side = [jnp.concatenate([total[64 * k : 64 * (k + 1), 128:], jnp.zeros((64, 80), F32)], axis=1).T for k in range(2, 6)]
+        first = side[2][16:32] + (side[2][32:48] + side[3][16:32])
+        third = side[0][:8] + (side[0][8:16] + side[1][:8])
         grads[pl.ds(32, 8), :] = jnp.concatenate([first[:8], first[8:]], axis=1)
-        grads[pl.ds(40, 64), :] = dot_tn(third, own, lax.Precision.HIGHEST)
-        totals = jnp.sum(sums[...], axis=1, keepdims=True)
-        grads[pl.ds(104, 8), :] = jnp.concatenate([
-            jnp.sum(own[:OWN] * totals[:OWN], axis=0, keepdims=True),
-            jnp.sum(own[:OWN] * totals[OWN:], axis=0, keepdims=True),
-            jnp.zeros((6, SIDE), F32),
-        ])
-
-
-def finish_kernel(mine, other, grad_in, grad_mid, grad_out, grad_decay, grad_skip):
-    total = mine[...] + other[...]
-    grad_mid[pl.ds(0, 32), :] = total[:32, :ORDER]
-    grad_mid[pl.ds(32, 32), :] = total[:32, ORDER:]
-    grad_in[pl.ds(0, 8), :] = total[32:40, :ORDER]
-    grad_in[pl.ds(8, 8), :] = total[32:40, ORDER:]
-    grad_out[...] = total[40:104]
-    grad_decay[...] = total[104:105]
-    grad_skip[...] = total[105:106]
+        lane = lax.broadcasted_iota(jnp.int32, (8, SIDE), 1)
+        rates = jnp.sum(sums[pl.ds(0, 8), :], axis=1, keepdims=True)
+        gains = jnp.sum(sums[pl.ds(8, 8), :], axis=1, keepdims=True)
+        grads[pl.ds(40, 8), :] = jnp.concatenate([third, jnp.zeros((8, 64), F32)], axis=1) + (
+            jnp.where(lane == 64, rates, 0.0) + jnp.where(lane == 65, gains, 0.0)
+        )
+
+
+def finish_kernel(gathered, grad_in, grad_mid, grad_out, grad_decay, grad_skip):
+    shared = gathered[pl.ds(0, 40), :]
+    for chip in range(1, 16):
+        shared = shared + gathered[pl.ds(48 * chip, 40), :]
+    grad_mid[pl.ds(0, 32), :] = shared[:32, :ORDER]
+    grad_mid[pl.ds(32, 32), :] = shared[:32, ORDER:]
+    grad_in[pl.ds(0, 8), :] = shared[32:, :ORDER]
+    grad_in[pl.ds(8, 8), :] = shared[32:, ORDER:]
+    row = lax.broadcasted_iota(jnp.int32, (SIDE, SIDE), 0)
+    lane = lax.broadcasted_iota(jnp.int32, (SIDE, SIDE), 1)
+    moved = jnp.where(lane == 2 * (row // 8) + row % 8 // OWN + SEQ * (row % OWN), 1.0, 0.0).astype(F32)
+    rows = jnp.concatenate([gathered[pl.ds(48 * chip + 40, 8), :] for chip in range(16)])
+    channels = dot_tn(rows, moved, lax.Precision.HIGHEST)
+    grad_out[...] = channels[:64]
+    grad_decay[...] = channels[64:65]
+    grad_skip[...] = channels[65:66]
 
 
 def seq_place():
-    return lax.axis_index("seq")
+    return lax.axis_index(SEQ_AXES)
 
 
 def run_send(query, key, value, grad, **kw):
     return call(
         send_kernel, 1, [pl.BlockSpec(memory_space=pltpu.HBM)] * 4, spec((1024, SIDE)), out((1024, SIDE)),
         scratch=[pltpu.VMEM((4, ROWS, SIDE), BF16), pltpu.SemaphoreType.DMA((4,))], **kw,
-    )(query, key, value, grad)
+    )(*[in_hbm(x) for x in (query, key, value, grad)])
 
 
 def run_filter(features, filter_in, filter_mid, filter_out, place=seq_place, **kw):
     wide = lambda i: (0, i)
     hidden = spec((ORDER, STEP), wide)
-    half, full = out((ORDER, HALF), BF16), out((ORDER, HALF))
+    half, full = pltpu.HBM((ORDER, HALF), BF16), pltpu.HBM((ORDER, HALF), F32)
     return call(
         functools.partial(filter_kernel, place),
         HALF // STEP,
@@ -411,23 +426,23 @@
         functools.partial(spectrum_kernel, place),
         1,
         [spec((256, SIDE))] * 2 + [spec((1, SIDE)), spec((256, 384)), spec((768, 256)), spec((SIDE, 256))],
-        [spec((512, 256)), spec((512, SIDE)), spec((512, SIDE))],
-        [out((512, 256)), out((512, SIDE)), out((512, SIDE))],
+        spec((512, 256)),
+        out((512, 256)),
         flops=10**9, nbytes=MIB, **kw,
     )(mine, other, decay, first_fwd, second_fwd, twiddle)
 
 
-def run_convolve(field, spectrum, filt, window, decay, place=seq_place, **kw):
+def run_convolve(field, spectrum, mine, other, decay, place=seq_place, **kw):
     first_fwd, second_fwd, twiddle, second_inv, first_inv = transform_tables()
     return call(
         functools.partial(convolve_kernel, place),
         1,
-        [spec((1024, SIDE)), spec((512, 256)), spec((512, SIDE)), spec((512, SIDE)), spec((1, SIDE)),
+        [spec((1024, SIDE)), spec((512, 256)), spec((256, SIDE)), spec((256, SIDE)), spec((1, SIDE)),
          spec((256, 384)), spec((768, 256)), spec((SIDE, 256)), spec((768, 256)), spec((SIDE, 768))],
-        [spec((1024, SIDE)), spec((512, SIDE)), spec((512, SIDE)), spec((8, SIDE))],
-        [out((1024, SIDE)), out((512, SIDE)), out((512, SIDE)), out((8, SIDE))],
+        [spec((1024, SIDE)), spec((512, SIDE)), spec((512, SIDE)), spec((16, SIDE))],
+        [out((1024, SIDE)), out((512, SIDE)), out((512, SIDE)), out((16, SIDE))],
         flops=4 * 10**9, nbytes=4 * MIB, **kw,
-    )(field, spectrum, filt, window, decay, first_fwd, second_fwd, twiddle, second_inv, first_inv)
+    )(field, spectrum, mine, other, decay, first_fwd, second_fwd, twiddle, second_inv, first_inv)
 
 
 def run_backward(features, hidden, mine, other, sums, filter_mid, filter_out, place=seq_place, **kw):
@@ -437,13 +452,12 @@
     return call(
         functools.partial(backward_kernel, place),
         HALF // STEP,
-        [spec((32, STEP), wide)] + [block] * 6 + [deep, deep, spec((8, SIDE)), spec((ORDER, ORDER)), spec((ORDER, SIDE))],
-        spec((112, SIDE)),
-        out((112, SIDE)),
-        scratch=[pltpu.VMEM((SIDE, SIDE), F32), pltpu.VMEM((32, SIDE), F32), pltpu.VMEM((16, SIDE), F32)]
-        + [pltpu.VMEM((ORDER, STEP), BF16)] * 4,
+        [spec((32, STEP), wide)] + [block] * 6 + [deep, deep, spec((16, SIDE)), spec((ORDER, ORDER)), spec((ORDER, SIDE))],
+        spec((48, SIDE)),
+        out((48, SIDE)),
+        scratch=[pltpu.VMEM((384, 176), F32)] + [pltpu.VMEM((ORDER, STEP), BF16)] * 4,
         flops=4 * 10**9, nbytes=10 * MIB, **kw,
-    )(features, *hidden, mine, other, sums, filter_mid, filter_out)
+    )(features, *[in_hbm(x) for x in hidden], mine, other, sums, filter_mid, filter_out)
 
 
 def run_receive(query, key, value, grad, skip, field, **kw):
@@ -452,11 +466,9 @@
                 [out((ROWS, SIDE), BF16)] * 4, **kw)(query, key, value, grad, skip, field)
 
 
-def run_finish(mine, other, **kw):
+def run_finish(gathered, **kw):
     shapes = [(16, ORDER), (ORDER, ORDER), (ORDER, SIDE), (1, SIDE), (1, SIDE)]
-    return call(finish_kernel, 1, [spec((112, SIDE))] * 2, [spec(s) for s in shapes], [out(s) for s in shapes], **kw)(
-        mine, other
-    )
+    return call(finish_kernel, 1, [spec((768, SIDE))], [spec(s) for s in shapes], [out(s) for s in shapes], **kw)(gathered)
 
 
 def exchanged(x, axis, distance):
@@ -473,28 +485,33 @@
 def body(query, key, value, grad, filter_in, filter_mid, filter_out, decay_rate, skip_gain):
     decay = decay_rate.reshape(1, SIDE)
     skip = skip_gain.reshape(1, SIDE)
-    features = lax.dynamic_slice_in_dim(jnp.asarray(feature_table()), HALF * (lax.axis_index("seq") % 2), HALF, axis=1)
+    core = lax.axis_index("core")
+    features = lax.dynamic_slice_in_dim(jnp.asarray(feature_table()), HALF * core, HALF, axis=1)
     sent = run_send(query, key, value, grad).reshape(SEQ, SEQ, SIDE)
-    field = lax.all_to_all(sent, "seq", 0, 0, tiled=True).reshape(1024, SIDE)
+    field = lax.all_to_all(sent, SEQ_AXES, 0, 0, tiled=True).reshape(1024, SIDE)
     *hidden, mine, theirs = run_filter(features, filter_in, filter_mid, filter_out)
-    spectrum, filt, window = run_spectrum(mine, exchanged(theirs, "seq", 1), decay)
-    sent, mine, theirs, sums = run_convolve(field, spectrum, filt, window, decay)
-    field = lax.all_to_all(sent.reshape(SEQ, SEQ, SIDE), "seq", 0, 0, tiled=True).reshape(1024, SIDE)
-    grads = run_backward(features, hidden, mine, exchanged(theirs, "seq", 1), sums, filter_mid, filter_out)
+    other = exchanged(theirs, "core", 1)
+    spectrum = run_spectrum(mine, other, decay)
+    sent, mine, theirs, sums = run_convolve(field, spectrum, mine, other, decay)
+    field = lax.all_to_all(sent.reshape(SEQ, SEQ, SIDE), SEQ_AXES, 0, 0, tiled=True).reshape(1024, SIDE)
+    grads = run_backward(features, hidden, mine, exchanged(theirs, "core", 1), sums, filter_mid, filter_out)
+    grads = group_sum(grads, "core", (1,))
+    shared = group_sum(grads[:40], "chan", (1, 2, 3))
+    shared, field = lax.optimization_barrier((shared, field))
+    shared = group_sum(shared, "chan", (6,))
+    grads = jnp.broadcast_to(jnp.concatenate([shared, grads[40:]])[None], (16, 48, SIDE))
+    gathered = lax.all_to_all(grads, ("x", "y"), 0, 0, tiled=True).reshape(768, SIDE)
     output, grad_query, grad_key, grad_value = run_receive(query, key, value, grad, skip, field)
-    shared = group_sum(group_sum(grads[:40], "chan", (1,)), "chan", (2, 6, 5))
-    grads = jnp.concatenate([shared, grads[40:]])
-    grads = group_sum(grads, "seq", (8, 16, 24))
-    grads = group_sum(grads, "seq", (2, 4, 6))
-    first, second, third, rates, gains = run_finish(grads, exchanged(grads, "seq", 1))
+    first, second, third, rates, gains = run_finish(gathered)
     return (output, grad_query, grad_key, grad_value, first, second, third, rates.reshape(SIDE), gains.reshape(SIDE))
 
 
 def solution(mesh):
-    wide = P("seq", "chan")
+    parts = Mesh(mesh.devices.reshape(4, 4, 2, 8), SEQ_AXES + ("chan",))
+    wide = P(SEQ_AXES, "chan")
     return jax.shard_map(
         body,
-        mesh=mesh,
+        mesh=parts,
         in_specs=(wide, wide, wide, wide, P(), P(), P(None, "chan"), P("chan"), P("chan")),
         out_specs=(wide, wide, wide, wide, P(), P(), P(None, "chan"), P("chan"), P("chan")),
         check_vma=False,

time: 86.3 us -> 74.9 us (0.87)
  the two profiles are of different devices: /device:TPU:1 before, /device:TPU:32 now
where the time goes in v3:
time: 74.9 us; the launch traced here: 74.4 us
  starting transfers between devices  32 us (43%)
  Pallas kernels  23.6 us (32%)
  waiting for transfers between devices  15.3 us (20%)
  local copies, waits for them, and re-layouts  2.54 us (3%)
  between operations  0.9 us (1%)
    ppermute x7, starting transfers between devices, exchanged(): lax.ppermute(x, axis, [(i, i ^ distance) for i in range(lax.axis_size(axi...  12 us
    all_to_all x1, waiting for transfers between devices, body(): lax.all_to_all(grads, ('x', 'y'), 0, 0, tiled=True).reshape(768, SIDE)  7.92 us
    pallas_call x1, Pallas kernels, run_filter(): call(functools.partial(filter_kernel, place), HALF // STEP, [spec((32, ST...  7.46 us
    all_to_all x1, starting transfers between devices, body(): field = lax.all_to_all(sent, SEQ_AXES, 0, 0, tiled=True).reshape(1024, SIDE)  7.33 us
    all_to_all x1, starting transfers between devices, body(): lax.all_to_all(grads, ('x', 'y'), 0, 0, tiled=True).reshape(768, SIDE)  7.1 us
    pallas_call x1, Pallas kernels, run_backward(): call(functools.partial(backward_kernel, place), HALF // STEP, [spec((32,...  7 us
    ppermute x7, waiting for transfers between devices, exchanged(): lax.ppermute(x, axis, [(i, i ^ distance) for i in range(lax.axis_size(axi...  6.09 us
    all_to_all x1, starting transfers between devices, body(): lax.all_to_all(sent.reshape(SEQ, SEQ, SIDE), SEQ_AXES, 0, 0, tiled=True)  5.56 us
  transfers between devices with their start and end apart: 10, of which 7 were waited for; matrix products, arithmetic and copies ran while one was open for 0% of the time, Pallas kernels for 22%

profile of v3, /device:TPU:32, one launch (start us, length us, event | category | flops | bytes accessed | tf_op | source)
XLA Modules:
  0.0 74.4 jit_solution(14165244264554917393)
XLA Ops:
  0.6 0.0 copy-start.16
  0.7 0.0 copy-start.6
  0.7 0.0 copy-start.5
  0.7 0.0 copy-start.7
  0.7 2.4 %shard_map.215 = f32[1024,128]{1,0:T(8,128)} custom-call(bf16[512,128]{1,0:T(8,128)(2,1)} %query.3, bf16[512,128]{1,0:T(8,128)(2,1)} %key.3, bf16[512,128]{1,0:T(8,128)(2,1)} %value.3, bf16[512,128]{1,0:T(8,128)(2,1)} %grad.3), custom_call_target="tpu_custom_call" | custom-call | flops 1 | bytes 1 | tf_op jit(solution)/shard_map/pallas_call | solution.py:402
  3.1 7.3 %all-to-all-start = ((f32[32,32,128]{2,1,0:T(8,128)}), f32[32,32,128]{2,1,0:T(8,128)S(1)}, u32[]{:S(2)}, u32[]{:S(2)}) async-start(f32[32,32,128]{2,1,0:T(8,128)} %bitcast.1), calls=%async_computation | async-start | bytes 1048576 | tf_op jit(solution)/shard_map/all_to_all | solution.py:491
  10.4 0.0 copy-done.16
  10.5 0.0 copy-done.6
  10.5 0.0 copy-done.5
  10.5 0.0 copy-done.7
  10.5 0.0 copy-start.8
  10.5 0.0 copy-start.9
  10.6 0.0 copy-start.11
  10.6 0.0 copy-start.13
  10.6 7.5 %shard_map.214 = (bf16[64,8192]{1,0:T(8,128)(2,1)}, bf16[64,8192]{1,0:T(8,128)(2,1)}, f32[64,8192]{1,0:T(8,128)}, bf16[64,8192]{1,0:T(8,128)(2,1)}, bf16[64,8192...) custom-call(bf16[32,8192]{1,0:T(8,128)(2,1)S(1)} %constant_dynamic-slice_fusion.features, ...), custom_call_target="tpu_custom_call" | custom-call | flops 4000000000 | bytes 10485760 | tf_op jit(solution)/shard_map/pallas_call | solution.py:412
  18.0 0.0 copy-start.10
  18.0 0.0 copy-start.12
  18.0 0.4 collective-permute-start
  18.4 1.1 %collective-permute-done.other.shaped_other = f32[256,128]{1,0:T(8,128)S(1)} collective-permute-done((f32[256,128]{1,0:T(8,128)S(1)}, f32[256,128]{1,0:T(8,128)S(1)}, u32[]{:S(2)}, u32[]{:S(2)}) %collective-permute-start) | collective-permute-done | bytes 131104 | tf_op jit(solution)/shard_map/ppermute | solution.py:475
  19.5 0.0 copy-done.8
  19.5 0.0 copy-done.9
  19.5 0.0 copy-done.11
  19.5 0.0 copy-done.13
  19.5 0.8 %shard_map.216.spectrum = f32[512,256]{1,0:T(8,128)S(1)} custom-call(f32[256,128]{1,0:T(8,128)S(1)} %get-tuple-element.38.mine.shaped_mine, f32[256,128]{1,0:T(8,128)S(1)} %collective-permute-done.other.shaped_other, f32[1,128]{1,0:T(1,128)S(1)} %bitcast.13, bf16[256,384]{1,0:T(8,128)(2,1)S(1)} %copy-done.11, bf16[768,256]{1,0:T(8,128)(2,1)S(1)} %copy-done.9, ...), custom_call_target="tpu_custom_call" | custom-call | flops 1000000000 | bytes 1048576 | tf_op jit(solution)/shard_map/pallas_call | solution.py:425
  20.3 1.3 %all-to-all-done = f32[32,32,128]{2,1,0:T(8,128)S(1)} async-done(((f32[32,32,128]{2,1,0:T(8,128)}), f32[32,32,128]{2,1,0:T(8,128)S(1)}, u32[]{:S(2)}, u32[]{:S(2)}) %all-to-all-start) | async-done | bytes 524320 | tf_op jit(solution)/shard_map/all_to_all | solution.py:491
  21.6 0.0 copy-done.10
  21.6 0.0 copy-done.12
  21.6 3.9 %shard_map.217 = (f32[1024,128]{1,0:T(8,128)}, f32[512,128]{1,0:T(8,128)S(1)}, f32[512,128]{1,0:T(8,128)S(1)}, f32[16,128]{1,0:T(8,128)S(1)}) custom-call(f32[1024,128]{1,0:T(8,128)S(1)} %bitcast.11, f32[512,256]{1,0:T(8,128)S(1)} %shard_map.216.spectrum, f32[256,128]{1,0:T(8,128)S(1)} %get-tuple-element.38.mine.shaped_mine, ...), custom_call_target="tpu_custom_call" | custom-call | flops 4000000000 | bytes 4194304 | tf_op jit(solution)/shard_map/pallas_call | solution.py:437
  25.5 0.0 copy-start.14
  25.5 0.7 copy-done.14
  26.2 0.7 collective-permute-start.1
  27.0 5.6 %all-to-all-start.1 = ((f32[32,32,128]{2,1,0:T(8,128)}), f32[32,32,128]{2,1,0:T(8,128)S(1)}, u32[]{:S(2)}, u32[]{:S(2)}) async-start(f32[32,32,128]{2,1,0:T(8,128)} %bitcast.4), calls=%async_computation.1 | async-start | bytes 1048576 | tf_op jit(solution)/shard_map/all_to_all | solution.py:496
  32.5 0.0 collective-permute-done.1.other
  32.5 0.0 copy-start.15
  32.5 0.9 %copy-done.15 = f32[512,128]{1,0:T(8,128)S(1)} copy-done((f32[512,128]{1,0:T(8,128)S(1)}, f32[512,128]{1,0:T(8,128)}, u32[]{:S(2)}) %copy-start.15) | copy-done | bytes 262168
  33.5 0.0 copy-start
  33.5 0.0 copy-start.1
  33.5 0.0 copy-start.2
  33.5 0.0 copy-start.3
  33.5 0.0 copy-start.4
  33.5 7.0 %shard_map.218 = f32[48,128]{1,0:T(8,128)S(1)} custom-call(bf16[32,8192]{1,0:T(8,128)(2,1)S(1)} %constant_dynamic-slice_fusion.features, bf16[64,8192]{1,0:T(8,128)(2,1)} %get-tuple-element.32.h1_high, bf16[64,8192]{1,0:T(8,128)(2,1)} %get-tuple-element.33.h1_low, f32[64,8192]{1,0:T(8,128)} %get-tuple-element.34.cos1, ...), custom_call_target="tpu_custom_call" | custom-call | flops 4000000000 | bytes 10485760 | tf_op jit(solution)/shard_map/pallas_call | solution.py:452
  40.5 0.4 collective-permute-start.2
  40.9 0.9 %collective-permute-done.2 = f32[48,128]{1,0:T(8,128)S(1)} collective-permute-done((f32[48,128]{1,0:T(8,128)S(1)}, f32[48,128]{1,0:T(8,128)S(1)}, u32[]{:S(2)}, u32[]{:S(2)}) %collective-permute-start.2) | collective-permute-done | bytes 24608 | tf_op jit(solution)/shard_map/ppermute | solution.py:475
  41.8 3.4 %collective-permute-start.4 = (f32[40,128]{1,0:T(8,128)S(1)}, f32[40,128]{1,0:T(8,128)S(1)}, u32[]{:S(2)}, u32[]{:S(2)}) collective-permute-start(f32[40,128]{1,0:T(8,128)S(1)} %slice.8), channel_id=1, source_target_pairs={{0,2},{1,3},{2,0},{3,1},{4,6},{5,7},{6,4},{7,5},{8,10},{9,11},{10,... | collective-permute-start | bytes 61448 | tf_op jit(solution)/shard_map/ppermute | solution.py:475
  45.2 0.0 collective-permute-start.5
  45.2 1.6 %collective-permute-start.3 = (f32[40,128]{1,0:T(8,128)S(1)}, f32[40,128]{1,0:T(8,128)S(1)}, u32[]{:S(2)}, u32[]{:S(2)}) collective-permute-start(f32[40,128]{1,0:T(8,128)S(1)} %slice.8), channel_id=1, source_target_pairs={{0,1},{1,0},{2,3},{3,2},{4,5},{5,4},{6,7},{7,6},{8,9},{9,8},{10,11... | collective-permute-start | bytes 61448 | tf_op jit(solution)/shard_map/ppermute | solution.py:475
  46.7 0.2 collective-permute-done.4
  46.9 2.0 %collective-permute-done.5 = f32[40,128]{1,0:T(8,128)S(1)} collective-permute-done((f32[40,128]{1,0:T(8,128)S(1)}, f32[40,128]{1,0:T(8,128)S(1)}, u32[]{:S(2)}, u32[]{:S(2)}) %collective-permute-start.5) | collective-permute-done | bytes 20512 | tf_op jit(solution)/shard_map/ppermute | solution.py:475
  48.9 0.0 collective-permute-done.3
  49.0 0.0 all-to-all-done.1
  49.0 5.7 %collective-permute-start.6 = (f32[40,128]{1,0:T(8,128)S(1)}, f32[40,128]{1,0:T(8,128)S(1)}, u32[]{:S(2)}, u32[]{:S(2)}) collective-permute-start(f32[40,128]{1,0:T(8,128)S(1)} %add_add_fusion), channel_id=1, source_target_pairs={{0,6},{1,7},{2,4},{3,5},{4,2},{5,3},{6,0},{7,1},{8,14},{9,15},{10,... | collective-permute-start | bytes 61448 | tf_op jit(solution)/shard_map/ppermute | solution.py:475
  54.6 1.9 %collective-permute-done.6 = f32[40,128]{1,0:T(8,128)S(1)} collective-permute-done((f32[40,128]{1,0:T(8,128)S(1)}, f32[40,128]{1,0:T(8,128)S(1)}, u32[]{:S(2)}, u32[]{:S(2)}) %collective-permute-start.6) | collective-permute-done | bytes 20512 | tf_op jit(solution)/shard_map/ppermute | solution.py:475
  56.5 0.8 %broadcast_in_dim.2 = f32[16,48,128]{2,1,0:T(8,128)} broadcast(f32[48,128]{1,0:T(8,128)S(1)} %pad_maximum_fusion), dimensions={1,2} | broadcast | bytes 417792 | tf_op jit(solution)/shard_map/broadcast_in_dim | solution.py:502
  57.3 7.1 %all-to-all-start.2 = ((f32[16,48,128]{2,1,0:T(8,128)}), f32[16,48,128]{2,1,0:T(8,128)S(1)}, u32[]{:S(2)}, u32[]{:S(2)}) async-start(f32[16,48,128]{2,1,0:T(8,128)} %broadcast_in_dim.2), calls=%async_computation.2 | async-start | bytes 786432 | tf_op jit(solution)/shard_map/all_to_all | solution.py:503
  64.4 0.0 copy-done
  64.4 0.0 copy-done.1
  64.4 0.0 copy-done.2
  64.4 0.0 copy-done.3
  64.4 0.0 copy-done.4
  64.4 1.2 %shard_map.219 = (bf16[512,128]{1,0:T(8,128)(2,1)}, bf16[512,128]{1,0:T(8,128)(2,1)}, bf16[512,128]{1,0:T(8,128)(2,1)}, bf16[512,128]{1,0:T(8,128)(2,1)}) custom-call(bf16[512,128]{1,0:T(8,128)(2,1)S(1)} %copy-done, bf16[512,128]{1,0:T(8,128)(2,1)S(1)} %copy-done.1, bf16[512,128]{1,0:T(8,128)(2,1)S(1)} %copy-done.2, bf16[512,128]{1,0:T(8,128)(2,1)S(1)} %copy-done.3, ...), custom_call_target="tpu_custom_call" | custom-call | flops 1 | bytes 1 | tf_op jit(solution)/shard_map/pallas_call | solution.py:465
  65.6 7.9 %all-to-all-done.2 = f32[16,48,128]{2,1,0:T(8,128)S(1)} async-done(((f32[16,48,128]{2,1,0:T(8,128)}), f32[16,48,128]{2,1,0:T(8,128)S(1)}, u32[]{:S(2)}, u32[]{:S(2)}) %all-to-all-start.2) | async-done | bytes 393248 | tf_op jit(solution)/shard_map/all_to_all | solution.py:503
  73.5 0.9 %shard_map.220 = (f32[16,64]{1,0:T(8,128)}, f32[64,64]{1,0:T(8,128)}, f32[64,128]{1,0:T(8,128)}, f32[1,128]{1,0:T(1,128)}, f32[1,128]{1,0:T(1,128)}) custom-call(f32[768,128]{1,0:T(8,128)S(1)} %bitcast.10), custom_call_target="tpu_custom_call" | custom-call | flops 1 | bytes 1 | tf_op jit(solution)/shard_map/pallas_call | solution.py:471
  (7 shorter events, 0.1 us)
Async XLA Ops:
  0.6 9.8 %copy-start.16 = (bf16[32,16384]{1,0:T(8,128)(2,1)S(1)}, bf16[32,16384]{1,0:T(8,128)(2,1)}, u32[]{:S(2)}) copy-start(bf16[32,16384]{1,0:T(8,128)(2,1)} %constant.24.clone) | copy-start | bytes 3145732
  0.7 9.9 %copy-start.6 = (f32[64,128]{1,0:T(8,128)S(1)}, f32[64,128]{1,0:T(8,128)}, u32[]{:S(2)}) copy-start(f32[64,128]{1,0:T(8,128)} %filter_out.3) | copy-start | bytes 98308
  0.7 9.9 %copy-start.5 = (f32[64,64]{1,0:T(8,128)S(1)}, f32[64,64]{1,0:T(8,128)}, u32[]{:S(2)}) copy-start(f32[64,64]{1,0:T(8,128)} %filter_mid.3) | copy-start | bytes 49156
  0.7 9.9 %copy-start.7 = (f32[16,64]{1,0:T(8,128)S(1)}, f32[16,64]{1,0:T(8,128)}, u32[]{:S(2)}) copy-start(f32[16,64]{1,0:T(8,128)} %filter_in.1) | copy-start | bytes 12292
  3.1 18.5 %all-to-all-start = ((f32[32,32,128]{2,1,0:T(8,128)}), f32[32,32,128]{2,1,0:T(8,128)S(1)}, u32[]{:S(2)}, u32[]{:S(2)}) async-start(f32[32,32,128]{2,1,0:T(8,128)} %bitcast.1), calls=%async_computation | async-start | bytes 1048576 | tf_op jit(solution)/shard_map/all_to_all | solution.py:491
  10.5 8.9 %copy-start.8 = (f32[128]{0:T(128)S(1)}, f32[128]{0:T(128)}, u32[]{:S(2)}) copy-start(f32[128]{0:T(128)} %param.22) | copy-start | bytes 1540
  10.5 8.9 %copy-start.9 = (bf16[768,256]{1,0:T(8,128)(2,1)S(1)}, bf16[768,256]{1,0:T(8,128)(2,1)}, u32[]{:S(2)}) copy-start(bf16[768,256]{1,0:T(8,128)(2,1)} %constant.26.clone.second_fwd) | copy-start | bytes 1179652
  10.6 8.9 %copy-start.11 = (bf16[256,384]{1,0:T(8,128)(2,1)S(1)}, bf16[256,384]{1,0:T(8,128)(2,1)}, u32[]{:S(2)}) copy-start(bf16[256,384]{1,0:T(8,128)(2,1)} %constant.25.clone.first_fwd) | copy-start | bytes 589828
  10.6 8.9 %copy-start.13 = (f32[128,256]{1,0:T(8,128)S(1)}, f32[128,256]{1,0:T(8,128)}, u32[]{:S(2)}) copy-start(f32[128,256]{1,0:T(8,128)} %constant.27.clone.twiddle) | copy-start | bytes 393220
  18.0 3.6 %copy-start.10 = (bf16[768,256]{1,0:T(8,128)(2,1)S(1)}, bf16[768,256]{1,0:T(8,128)(2,1)}, u32[]{:S(2)}) copy-start(bf16[768,256]{1,0:T(8,128)(2,1)} %constant.28.clone.second_inv) | copy-start | bytes 1179652
  18.0 3.6 %copy-start.12 = (bf16[128,768]{1,0:T(8,128)(2,1)S(1)}, bf16[128,768]{1,0:T(8,128)(2,1)}, u32[]{:S(2)}) copy-start(bf16[128,768]{1,0:T(8,128)(2,1)} %constant.29.clone.first_inv) | copy-start | bytes 589828
  18.0 1.4 %collective-permute-start = (f32[256,128]{1,0:T(8,128)S(1)}, f32[256,128]{1,0:T(8,128)S(1)}, u32[]{:S(2)}, u32[]{:S(2)}) collective-permute-start(f32[256,128]{1,0:T(8,128)S(1)} %get-tuple-element.39), channel_id=1, source_target_pairs={{0,8},{8,0},{1,9},{9,1},{2,10},{10,2},{3,11},{11,3},{4,12},{12,4},... | collective-permute-start | bytes 393224 | tf_op jit(solution)/shard_map/ppermute | solution.py:475
  25.5 0.7 copy-start.14
  26.2 6.3 %collective-permute-start.1 = (f32[512,128]{1,0:T(8,128)S(1)}, f32[512,128]{1,0:T(8,128)S(1)}, u32[]{:S(2)}, u32[]{:S(2)}) collective-permute-start(f32[512,128]{1,0:T(8,128)S(1)} %get-tuple-element.41), channel_id=1, source_target_pairs={{0,8},{8,0},{1,9},{9,1},{2,10},{10,2},{3,11},{11,3},{4,12},{12,4},... | collective-permute-start | bytes 786440 | tf_op jit(solution)/shard_map/ppermute | solution.py:475
  27.0 22.0 %all-to-all-start.1 = ((f32[32,32,128]{2,1,0:T(8,128)}), f32[32,32,128]{2,1,0:T(8,128)S(1)}, u32[]{:S(2)}, u32[]{:S(2)}) async-start(f32[32,32,128]{2,1,0:T(8,128)} %bitcast.4), calls=%async_computation.1 | async-start | bytes 1048576 | tf_op jit(solution)/shard_map/all_to_all | solution.py:496
  32.5 1.0 %copy-start.15 = (f32[512,128]{1,0:T(8,128)S(1)}, f32[512,128]{1,0:T(8,128)}, u32[]{:S(2)}) copy-start(f32[512,128]{1,0:T(8,128)} %copy-done.14) | copy-start | bytes 786436
  33.5 30.9 %copy-start = (bf16[512,128]{1,0:T(8,128)(2,1)S(1)}, bf16[512,128]{1,0:T(8,128)(2,1)}, u32[]{:S(2)}) copy-start(bf16[512,128]{1,0:T(8,128)(2,1)} %query.3) | copy-start | bytes 393220
  33.5 30.9 %copy-start.1 = (bf16[512,128]{1,0:T(8,128)(2,1)S(1)}, bf16[512,128]{1,0:T(8,128)(2,1)}, u32[]{:S(2)}) copy-start(bf16[512,128]{1,0:T(8,128)(2,1)} %key.3) | copy-start | bytes 393220
  33.5 30.9 %copy-start.2 = (bf16[512,128]{1,0:T(8,128)(2,1)S(1)}, bf16[512,128]{1,0:T(8,128)(2,1)}, u32[]{:S(2)}) copy-start(bf16[512,128]{1,0:T(8,128)(2,1)} %value.3) | copy-start | bytes 393220
  33.5 30.9 %copy-start.3 = (bf16[512,128]{1,0:T(8,128)(2,1)S(1)}, bf16[512,128]{1,0:T(8,128)(2,1)}, u32[]{:S(2)}) copy-start(bf16[512,128]{1,0:T(8,128)(2,1)} %grad.3) | copy-start | bytes 393220
  33.5 30.9 %copy-start.4 = (f32[128]{0:T(128)S(1)}, f32[128]{0:T(128)}, u32[]{:S(2)}) copy-start(f32[128]{0:T(128)} %param.23) | copy-start | bytes 1540
  40.5 1.3 %collective-permute-start.2 = (f32[48,128]{1,0:T(8,128)S(1)}, f32[48,128]{1,0:T(8,128)S(1)}, u32[]{:S(2)}, u32[]{:S(2)}) collective-permute-start(f32[48,128]{1,0:T(8,128)S(1)} %shard_map.218), channel_id=1, source_target_pairs={{0,8},{8,0},{1,9},{9,1},{2,10},{10,2},{3,11},{11,3},{4,12},{12,4},... | collective-permute-start | bytes 73736 | tf_op jit(solution)/shard_map/ppermute | solution.py:475
  41.8 5.1 %collective-permute-start.4 = (f32[40,128]{1,0:T(8,128)S(1)}, f32[40,128]{1,0:T(8,128)S(1)}, u32[]{:S(2)}, u32[]{:S(2)}) collective-permute-start(f32[40,128]{1,0:T(8,128)S(1)} %slice.8), channel_id=1, source_target_pairs={{0,2},{1,3},{2,0},{3,1},{4,6},{5,7},{6,4},{7,5},{8,10},{9,11},{10,... | collective-permute-start | bytes 61448 | tf_op jit(solution)/shard_map/ppermute | solution.py:475
  45.2 3.8 %collective-permute-start.5 = (f32[40,128]{1,0:T(8,128)S(1)}, f32[40,128]{1,0:T(8,128)S(1)}, u32[]{:S(2)}, u32[]{:S(2)}) collective-permute-start(f32[40,128]{1,0:T(8,128)S(1)} %slice.8), channel_id=1, source_target_pairs={{0,3},{1,2},{2,1},{3,0},{4,7},{5,6},{6,5},{7,4},{8,11},{9,10},{10,... | collective-permute-start | bytes 61448 | tf_op jit(solution)/shard_map/ppermute | solution.py:475
  45.2 3.8 %collective-permute-start.3 = (f32[40,128]{1,0:T(8,128)S(1)}, f32[40,128]{1,0:T(8,128)S(1)}, u32[]{:S(2)}, u32[]{:S(2)}) collective-permute-start(f32[40,128]{1,0:T(8,128)S(1)} %slice.8), channel_id=1, source_target_pairs={{0,1},{1,0},{2,3},{3,2},{4,5},{5,4},{6,7},{7,6},{8,9},{9,8},{10,11... | collective-permute-start | bytes 61448 | tf_op jit(solution)/shard_map/ppermute | solution.py:475
  49.0 7.5 %collective-permute-start.6 = (f32[40,128]{1,0:T(8,128)S(1)}, f32[40,128]{1,0:T(8,128)S(1)}, u32[]{:S(2)}, u32[]{:S(2)}) collective-permute-start(f32[40,128]{1,0:T(8,128)S(1)} %add_add_fusion), channel_id=1, source_target_pairs={{0,6},{1,7},{2,4},{3,5},{4,2},{5,3},{6,0},{7,1},{8,14},{9,15},{10,... | collective-permute-start | bytes 61448 | tf_op jit(solution)/shard_map/ppermute | solution.py:475
  57.3 16.2 %all-to-all-start.2 = ((f32[16,48,128]{2,1,0:T(8,128)}), f32[16,48,128]{2,1,0:T(8,128)S(1)}, u32[]{:S(2)}, u32[]{:S(2)}) async-start(f32[16,48,128]{2,1,0:T(8,128)} %broadcast_in_dim.2), calls=%async_computation.2 | async-start | bytes 786432 | tf_op jit(solution)/shard_map/all_to_all | solution.py:503

commit v4 on v3

--- a/solution.py
+++ b/solution.py
@@ -20,6 +20,7 @@
 ORDER = 64
 STEP = 2048
 PIECE = 256
+BACK = 4096
 HALF = LENGTH // 2
 MIB = 1 << 20
 SEQ_AXES = ("x", "y", "core")
@@ -123,6 +124,10 @@
     return jnp.concatenate([high, high, low], axis=axis)
 
 
+def picked(filter_out, channels):
+    return dot_nt(jnp.concatenate(halves(filter_out[...])), channels.astype(BF16))
+
+
 def own_channels(place):
     row = lax.broadcasted_iota(jnp.int32, (8, SIDE), 0)
     lane = lax.broadcasted_iota(jnp.int32, (8, SIDE), 1)
@@ -234,7 +239,8 @@
     in_high, in_low = halves(filter_in[...].T * turn)
     weight1 = jnp.concatenate([in_high, in_low, in_high], axis=1)
     weight2 = weight_left(filter_mid[...].T * turn, 1)
-    weight3 = weight_left(dot_nt(own, filter_out[...], lax.Precision.HIGHEST), 1)
+    weight3 = picked(filter_out, own).T.astype(BF16)
+    weight3 = jnp.concatenate([weight3[:, :64], weight3[:, :64], weight3[:, 64:]], axis=1)
     pieces = [pl.ds(PIECE * k, PIECE) for k in range(STEP // PIECE)]
     for piece in pieces:
         feature = features[:, piece]
@@ -333,11 +339,12 @@
 def backward_kernel(place, features, h1_high, h1_low, cos1, h2_high, h2_low, cos2, mine, other, sums, filter_mid, filter_out,
                     grads, total, d2_high, d2_low, d1_high, d1_low):
     step = pl.program_id(0)
-    weight3 = weight_left(dot_nt(filter_out[...], pair_channels(place()), lax.Precision.HIGHEST), 1)
+    weight3 = picked(filter_out, pair_channels(place())).astype(BF16)
+    weight3 = jnp.concatenate([weight3[:64], weight3[:64], weight3[64:]], axis=1)
     weight2 = weight_left(filter_mid[...], 1)
-    pieces = [pl.ds(PIECE * k, PIECE) for k in range(STEP // PIECE)]
+    pieces = [pl.ds(PIECE * k, PIECE) for k in range(BACK // PIECE)]
     shaped_high, shaped_low = halves(
-        jnp.concatenate([mine[pl.ds(8 * m, 8), :] + other[pl.ds(8 * m, 8), :] for m in range(STEP // SIDE)], axis=1)
+        jnp.concatenate([mine[pl.ds(8 * m, 8), :] + other[pl.ds(8 * m, 8), :] for m in range(BACK // SIDE)], axis=1)
     )
     for k, piece in enumerate(pieces):
         part = slice(PIECE * k, PIECE * (k + 1))
@@ -360,7 +367,7 @@
     def _():
         total[...] += product
 
-    @pl.when(step == HALF // STEP - 1)
+    @pl.when(step == HALF // BACK - 1)
     def _():
         mid = total[:64, :64] + (total[:64, 64:128] + total[64:128, :64])
         grads[pl.ds(0, 32), :] = jnp.concatenate([mid[:32], mid[32:]], axis=1)
@@ -440,24 +447,24 @@
         [spec((1024, SIDE)), spec((512, 256)), spec((256, SIDE)), spec((256, SIDE)), spec((1, SIDE)),
          spec((256, 384)), spec((768, 256)), spec((SIDE, 256)), spec((768, 256)), spec((SIDE, 768))],
         [spec((1024, SIDE)), spec((512, SIDE)), spec((512, SIDE)), spec((16, SIDE))],
-        [out((1024, SIDE)), out((512, SIDE)), out((512, SIDE)), out((16, SIDE))],
+        [out((1024, SIDE)), pltpu.HBM((512, SIDE), F32), out((512, SIDE)), pltpu.HBM((16, SIDE), F32)],
         flops=4 * 10**9, nbytes=4 * MIB, **kw,
     )(field, spectrum, mine, other, decay, first_fwd, second_fwd, twiddle, second_inv, first_inv)
 
 
 def run_backward(features, hidden, mine, other, sums, filter_mid, filter_out, place=seq_place, **kw):
     wide = lambda i: (0, i)
-    block = spec((ORDER, STEP), wide)
-    deep = spec((STEP // 16, SIDE), lambda i: (i, 0))
+    block = spec((ORDER, BACK), wide)
+    deep = spec((BACK // 16, SIDE), lambda i: (i, 0))
     return call(
         functools.partial(backward_kernel, place),
-        HALF // STEP,
-        [spec((32, STEP), wide)] + [block] * 6 + [deep, deep, spec((16, SIDE)), spec((ORDER, ORDER)), spec((ORDER, SIDE))],
+        HALF // BACK,
+        [spec((32, BACK), wide)] + [block] * 6 + [deep, deep, spec((16, SIDE)), spec((ORDER, ORDER)), spec((ORDER, SIDE))],
         spec((48, SIDE)),
         out((48, SIDE)),
-        scratch=[pltpu.VMEM((384, 176), F32)] + [pltpu.VMEM((ORDER, STEP), BF16)] * 4,
+        scratch=[pltpu.VMEM((384, 176), F32)] + [pltpu.VMEM((ORDER, BACK), BF16)] * 4,
         flops=4 * 10**9, nbytes=10 * MIB, **kw,
-    )(features, *[in_hbm(x) for x in hidden], mine, other, sums, filter_mid, filter_out)
+    )(features, *[in_hbm(x) for x in hidden], in_hbm(mine), other, in_hbm(sums), in_hbm(filter_mid), in_hbm(filter_out))
 
 
 def run_receive(query, key, value, grad, skip, field, **kw):

time: 74.9 us -> 72.6 us (0.969)
  local copies, waits for them, and re-layouts: 2.54 us -> 0.92 us
    unnamed x34 -> x30, local copies, waits for them, and re-layouts: 1.72 us -> 0.09 us
    pallas_call x1, Pallas kernels: 7 us -> 6.08 us  [run_backward(): call(functools.partial(backward_kernel, place), HALF // BACK, [spec((32,...]
where the time goes in v4:
time: 72.6 us; the launch traced here: 72.2 us
  starting transfers between devices  32.2 us (44%)
  Pallas kernels  23 us (32%)
  waiting for transfers between devices  15.1 us (21%)
  local copies, waits for them, and re-layouts  0.92 us (1%)
  between operations  0.92 us (1%)
    ppermute x7, starting transfers between devices, exchanged(): lax.ppermute(x, axis, [(i, i ^ distance) for i in range(lax.axis_size(axi...  12.1 us
    all_to_all x1, waiting for transfers between devices, body(): lax.all_to_all(grads, ('x', 'y'), 0, 0, tiled=True).reshape(768, SIDE)  7.92 us
    pallas_call x1, Pallas kernels, run_filter(): call(functools.partial(filter_kernel, place), HALF // STEP, [spec((32, ST...  7.65 us
    all_to_all x1, starting transfers between devices, body(): field = lax.all_to_all(sent, SEQ_AXES, 0, 0, tiled=True).reshape(1024, SIDE)  7.33 us
    all_to_all x1, starting transfers between devices, body(): lax.all_to_all(grads, ('x', 'y'), 0, 0, tiled=True).reshape(768, SIDE)  7.09 us
    pallas_call x1, Pallas kernels, run_backward(): call(functools.partial(backward_kernel, place), HALF // BACK, [spec((32,...  6.08 us
    ppermute x7, waiting for transfers between devices, exchanged(): lax.ppermute(x, axis, [(i, i ^ distance) for i in range(lax.axis_size(axi...  6.08 us
    all_to_all x1, starting transfers between devices, body(): lax.all_to_all(sent.reshape(SEQ, SEQ, SIDE), SEQ_AXES, 0, 0, tiled=True)  5.73 us
  transfers between devices with their start and end apart: 10, of which 7 were waited for; matrix products, arithmetic and copies ran while one was open for 0% of the time, Pallas kernels for 22%

profile of v4, /device:TPU:32, one launch (start us, length us, event | category | flops | bytes accessed | tf_op | source)
XLA Modules:
  0.0 72.2 jit_solution(5105720713694672501)
XLA Ops:
  0.6 0.0 copy-start.14
  0.7 0.0 copy-start.6
  0.7 0.0 copy-start.5
  0.7 0.0 copy-start.7
  0.7 2.4 %shard_map.215 = f32[1024,128]{1,0:T(8,128)} custom-call(bf16[512,128]{1,0:T(8,128)(2,1)} %query.3, bf16[512,128]{1,0:T(8,128)(2,1)} %key.3, bf16[512,128]{1,0:T(8,128)(2,1)} %value.3, bf16[512,128]{1,0:T(8,128)(2,1)} %grad.3), custom_call_target="tpu_custom_call" | custom-call | flops 1 | bytes 1 | tf_op jit(solution)/shard_map/pallas_call | solution.py:409
  3.1 7.3 %all-to-all-start = ((f32[32,32,128]{2,1,0:T(8,128)}), f32[32,32,128]{2,1,0:T(8,128)S(1)}, u32[]{:S(2)}, u32[]{:S(2)}) async-start(f32[32,32,128]{2,1,0:T(8,128)} %bitcast.1), calls=%async_computation | async-start | bytes 1048576 | tf_op jit(solution)/shard_map/all_to_all | solution.py:498
  10.5 0.0 copy-done.14
  10.5 0.0 copy-done.6
  10.5 0.0 copy-done.5
  10.6 0.0 copy-done.7
  10.6 0.0 copy-start.8
  10.6 0.0 copy-start.9
  10.6 0.0 copy-start.11
  10.6 0.0 copy-start.13
  10.6 7.6 %shard_map.214 = (bf16[64,8192]{1,0:T(8,128)(2,1)}, bf16[64,8192]{1,0:T(8,128)(2,1)}, f32[64,8192]{1,0:T(8,128)}, bf16[64,8192]{1,0:T(8,128)(2,1)}, bf16[64,8192...) custom-call(bf16[32,8192]{1,0:T(8,128)(2,1)S(1)} %constant_dynamic-slice_fusion.features, ...), custom_call_target="tpu_custom_call" | custom-call | flops 4000000000 | bytes 10485760 | tf_op jit(solution)/shard_map/pallas_call | solution.py:419
  18.3 0.0 copy-start.10
  18.3 0.0 copy-start.12
  18.3 0.4 collective-permute-start
  18.6 1.1 %collective-permute-done.other.shaped_other = f32[256,128]{1,0:T(8,128)S(1)} collective-permute-done((f32[256,128]{1,0:T(8,128)S(1)}, f32[256,128]{1,0:T(8,128)S(1)}, u32[]{:S(2)}, u32[]{:S(2)}) %collective-permute-start) | collective-permute-done | bytes 131104 | tf_op jit(solution)/shard_map/ppermute | solution.py:482
  19.7 0.0 copy-done.8
  19.7 0.0 copy-done.9
  19.7 0.0 copy-done.11
  19.7 0.0 copy-done.13
  19.7 0.8 %shard_map.216.spectrum = f32[512,256]{1,0:T(8,128)S(1)} custom-call(f32[256,128]{1,0:T(8,128)S(1)} %get-tuple-element.38.mine.shaped_mine, f32[256,128]{1,0:T(8,128)S(1)} %collective-permute-done.other.shaped_other, f32[1,128]{1,0:T(1,128)S(1)} %bitcast.13, bf16[256,384]{1,0:T(8,128)(2,1)S(1)} %copy-done.11, bf16[768,256]{1,0:T(8,128)(2,1)S(1)} %copy-done.9, ...), custom_call_target="tpu_custom_call" | custom-call | flops 1000000000 | bytes 1048576 | tf_op jit(solution)/shard_map/pallas_call | solution.py:432
  20.5 1.1 %all-to-all-done = f32[32,32,128]{2,1,0:T(8,128)S(1)} async-done(((f32[32,32,128]{2,1,0:T(8,128)}), f32[32,32,128]{2,1,0:T(8,128)S(1)}, u32[]{:S(2)}, u32[]{:S(2)}) %all-to-all-start) | async-done | bytes 524320 | tf_op jit(solution)/shard_map/all_to_all | solution.py:498
  21.7 0.0 copy-done.10
  21.7 0.0 copy-done.12
  21.7 4.0 %shard_map.217 = (f32[1024,128]{1,0:T(8,128)}, f32[512,128]{1,0:T(8,128)}, f32[512,128]{1,0:T(8,128)S(1)}, f32[16,128]{1,0:T(8,128)}) custom-call(f32[1024,128]{1,0:T(8,128)S(1)} %bitcast.11, f32[512,256]{1,0:T(8,128)S(1)} %shard_map.216.spectrum, f32[256,128]{1,0:T(8,128)S(1)} %get-tuple-element.38.mine.shaped_mine, ...), custom_call_target="tpu_custom_call" | custom-call | flops 4000000000 | bytes 4194304 | tf_op jit(solution)/shard_map/pallas_call | solution.py:444
  25.7 0.7 collective-permute-start.1
  26.4 5.7 %all-to-all-start.1 = ((f32[32,32,128]{2,1,0:T(8,128)}), f32[32,32,128]{2,1,0:T(8,128)S(1)}, u32[]{:S(2)}, u32[]{:S(2)}) async-start(f32[32,32,128]{2,1,0:T(8,128)} %bitcast.4), calls=%async_computation.1 | async-start | bytes 1048576 | tf_op jit(solution)/shard_map/all_to_all | solution.py:503
  32.1 0.0 collective-permute-done.1.other
  32.1 0.0 copy-start
  32.2 0.0 copy-start.1
  32.2 0.0 copy-start.2
  32.2 0.0 copy-start.3
  32.2 0.0 copy-start.4
  32.2 6.1 %shard_map.218 = f32[48,128]{1,0:T(8,128)S(1)} custom-call(bf16[32,8192]{1,0:T(8,128)(2,1)S(1)} %constant_dynamic-slice_fusion.features, bf16[64,8192]{1,0:T(8,128)(2,1)} %get-tuple-element.32.h1_high, bf16[64,8192]{1,0:T(8,128)(2,1)} %get-tuple-element.33.h1_low, f32[64,8192]{1,0:T(8,128)} %get-tuple-element.34.cos1, ...), custom_call_target="tpu_custom_call" | custom-call | flops 4000000000 | bytes 10485760 | tf_op jit(solution)/shard_map/pallas_call | solution.py:459
  38.3 0.4 collective-permute-start.2
  38.7 0.9 %collective-permute-done.2 = f32[48,128]{1,0:T(8,128)S(1)} collective-permute-done((f32[48,128]{1,0:T(8,128)S(1)}, f32[48,128]{1,0:T(8,128)S(1)}, u32[]{:S(2)}, u32[]{:S(2)}) %collective-permute-start.2) | collective-permute-done | bytes 24608 | tf_op jit(solution)/shard_map/ppermute | solution.py:482
  39.6 3.4 %collective-permute-start.4 = (f32[40,128]{1,0:T(8,128)S(1)}, f32[40,128]{1,0:T(8,128)S(1)}, u32[]{:S(2)}, u32[]{:S(2)}) collective-permute-start(f32[40,128]{1,0:T(8,128)S(1)} %slice.8), channel_id=1, source_target_pairs={{0,2},{1,3},{2,0},{3,1},{4,6},{5,7},{6,4},{7,5},{8,10},{9,11},{10,... | collective-permute-start | bytes 61448 | tf_op jit(solution)/shard_map/ppermute | solution.py:482
  43.0 0.0 collective-permute-start.5
  43.0 1.6 %collective-permute-start.3 = (f32[40,128]{1,0:T(8,128)S(1)}, f32[40,128]{1,0:T(8,128)S(1)}, u32[]{:S(2)}, u32[]{:S(2)}) collective-permute-start(f32[40,128]{1,0:T(8,128)S(1)} %slice.8), channel_id=1, source_target_pairs={{0,1},{1,0},{2,3},{3,2},{4,5},{5,4},{6,7},{7,6},{8,9},{9,8},{10,11... | collective-permute-start | bytes 61448 | tf_op jit(solution)/shard_map/ppermute | solution.py:482
  44.5 0.2 collective-permute-done.4
  44.7 2.0 %collective-permute-done.5 = f32[40,128]{1,0:T(8,128)S(1)} collective-permute-done((f32[40,128]{1,0:T(8,128)S(1)}, f32[40,128]{1,0:T(8,128)S(1)}, u32[]{:S(2)}, u32[]{:S(2)}) %collective-permute-start.5) | collective-permute-done | bytes 20512 | tf_op jit(solution)/shard_map/ppermute | solution.py:482
  46.7 0.0 collective-permute-done.3
  46.8 0.0 all-to-all-done.1
  46.8 5.7 %collective-permute-start.6 = (f32[40,128]{1,0:T(8,128)S(1)}, f32[40,128]{1,0:T(8,128)S(1)}, u32[]{:S(2)}, u32[]{:S(2)}) collective-permute-start(f32[40,128]{1,0:T(8,128)S(1)} %add_add_fusion), channel_id=1, source_target_pairs={{0,6},{1,7},{2,4},{3,5},{4,2},{5,3},{6,0},{7,1},{8,14},{9,15},{10,... | collective-permute-start | bytes 61448 | tf_op jit(solution)/shard_map/ppermute | solution.py:482
  52.4 1.9 %collective-permute-done.6 = f32[40,128]{1,0:T(8,128)S(1)} collective-permute-done((f32[40,128]{1,0:T(8,128)S(1)}, f32[40,128]{1,0:T(8,128)S(1)}, u32[]{:S(2)}, u32[]{:S(2)}) %collective-permute-start.6) | collective-permute-done | bytes 20512 | tf_op jit(solution)/shard_map/ppermute | solution.py:482
  54.3 0.8 %broadcast_in_dim.2 = f32[16,48,128]{2,1,0:T(8,128)} broadcast(f32[48,128]{1,0:T(8,128)S(1)} %pad_maximum_fusion), dimensions={1,2} | broadcast | bytes 417792 | tf_op jit(solution)/shard_map/broadcast_in_dim | solution.py:509
  55.1 7.1 %all-to-all-start.2 = ((f32[16,48,128]{2,1,0:T(8,128)}), f32[16,48,128]{2,1,0:T(8,128)S(1)}, u32[]{:S(2)}, u32[]{:S(2)}) async-start(f32[16,48,128]{2,1,0:T(8,128)} %broadcast_in_dim.2), calls=%async_computation.2 | async-start | bytes 786432 | tf_op jit(solution)/shard_map/all_to_all | solution.py:510
  62.2 0.0 copy-done
  62.2 0.0 copy-done.1
  62.2 0.0 copy-done.2
  62.2 0.0 copy-done.3
  62.3 0.0 copy-done.4
  62.3 1.2 %shard_map.219 = (bf16[512,128]{1,0:T(8,128)(2,1)}, bf16[512,128]{1,0:T(8,128)(2,1)}, bf16[512,128]{1,0:T(8,128)(2,1)}, bf16[512,128]{1,0:T(8,128)(2,1)}) custom-call(bf16[512,128]{1,0:T(8,128)(2,1)S(1)} %copy-done, bf16[512,128]{1,0:T(8,128)(2,1)S(1)} %copy-done.1, bf16[512,128]{1,0:T(8,128)(2,1)S(1)} %copy-done.2, bf16[512,128]{1,0:T(8,128)(2,1)S(1)} %copy-done.3, ...), custom_call_target="tpu_custom_call" | custom-call | flops 1 | bytes 1 | tf_op jit(solution)/shard_map/pallas_call | solution.py:472
  63.4 7.9 %all-to-all-done.2 = f32[16,48,128]{2,1,0:T(8,128)S(1)} async-done(((f32[16,48,128]{2,1,0:T(8,128)}), f32[16,48,128]{2,1,0:T(8,128)S(1)}, u32[]{:S(2)}, u32[]{:S(2)}) %all-to-all-start.2) | async-done | bytes 393248 | tf_op jit(solution)/shard_map/all_to_all | solution.py:510
  71.3 0.9 %shard_map.220 = (f32[16,64]{1,0:T(8,128)}, f32[64,64]{1,0:T(8,128)}, f32[64,128]{1,0:T(8,128)}, f32[1,128]{1,0:T(1,128)}, f32[1,128]{1,0:T(1,128)}) custom-call(f32[768,128]{1,0:T(8,128)S(1)} %bitcast.10), custom_call_target="tpu_custom_call" | custom-call | flops 1 | bytes 1 | tf_op jit(solution)/shard_map/pallas_call | solution.py:478
  (7 shorter events, 0.1 us)
Async XLA Ops:
  0.6 9.8 %copy-start.14 = (bf16[32,16384]{1,0:T(8,128)(2,1)S(1)}, bf16[32,16384]{1,0:T(8,128)(2,1)}, u32[]{:S(2)}) copy-start(bf16[32,16384]{1,0:T(8,128)(2,1)} %constant.24.clone) | copy-start | bytes 3145732
  0.7 9.9 %copy-start.6 = (f32[64,128]{1,0:T(8,128)S(1)}, f32[64,128]{1,0:T(8,128)}, u32[]{:S(2)}) copy-start(f32[64,128]{1,0:T(8,128)} %filter_out.3) | copy-start | bytes 98308
  0.7 9.9 %copy-start.5 = (f32[64,64]{1,0:T(8,128)S(1)}, f32[64,64]{1,0:T(8,128)}, u32[]{:S(2)}) copy-start(f32[64,64]{1,0:T(8,128)} %filter_mid.3) | copy-start | bytes 49156
  0.7 9.9 %copy-start.7 = (f32[16,64]{1,0:T(8,128)S(1)}, f32[16,64]{1,0:T(8,128)}, u32[]{:S(2)}) copy-start(f32[16,64]{1,0:T(8,128)} %filter_in.1) | copy-start | bytes 12292
  3.1 18.5 %all-to-all-start = ((f32[32,32,128]{2,1,0:T(8,128)}), f32[32,32,128]{2,1,0:T(8,128)S(1)}, u32[]{:S(2)}, u32[]{:S(2)}) async-start(f32[32,32,128]{2,1,0:T(8,128)} %bitcast.1), calls=%async_computation | async-start | bytes 1048576 | tf_op jit(solution)/shard_map/all_to_all | solution.py:498
  10.6 9.1 %copy-start.8 = (f32[128]{0:T(128)S(1)}, f32[128]{0:T(128)}, u32[]{:S(2)}) copy-start(f32[128]{0:T(128)} %param.22) | copy-start | bytes 1540
  10.6 9.1 %copy-start.9 = (bf16[768,256]{1,0:T(8,128)(2,1)S(1)}, bf16[768,256]{1,0:T(8,128)(2,1)}, u32[]{:S(2)}) copy-start(bf16[768,256]{1,0:T(8,128)(2,1)} %constant.26.clone.second_fwd) | copy-start | bytes 1179652
  10.6 9.1 %copy-start.11 = (bf16[256,384]{1,0:T(8,128)(2,1)S(1)}, bf16[256,384]{1,0:T(8,128)(2,1)}, u32[]{:S(2)}) copy-start(bf16[256,384]{1,0:T(8,128)(2,1)} %constant.25.clone.first_fwd) | copy-start | bytes 589828
  10.6 9.1 %copy-start.13 = (f32[128,256]{1,0:T(8,128)S(1)}, f32[128,256]{1,0:T(8,128)}, u32[]{:S(2)}) copy-start(f32[128,256]{1,0:T(8,128)} %constant.27.clone.twiddle) | copy-start | bytes 393220
  18.3 3.4 %copy-start.10 = (bf16[768,256]{1,0:T(8,128)(2,1)S(1)}, bf16[768,256]{1,0:T(8,128)(2,1)}, u32[]{:S(2)}) copy-start(bf16[768,256]{1,0:T(8,128)(2,1)} %constant.28.clone.second_inv) | copy-start | bytes 1179652
  18.3 3.4 %copy-start.12 = (bf16[128,768]{1,0:T(8,128)(2,1)S(1)}, bf16[128,768]{1,0:T(8,128)(2,1)}, u32[]{:S(2)}) copy-start(bf16[128,768]{1,0:T(8,128)(2,1)} %constant.29.clone.first_inv) | copy-start | bytes 589828
  18.3 1.4 %collective-permute-start = (f32[256,128]{1,0:T(8,128)S(1)}, f32[256,128]{1,0:T(8,128)S(1)}, u32[]{:S(2)}, u32[]{:S(2)}) collective-permute-start(f32[256,128]{1,0:T(8,128)S(1)} %get-tuple-element.39), channel_id=1, source_target_pairs={{0,8},{8,0},{1,9},{9,1},{2,10},{10,2},{3,11},{11,3},{4,12},{12,4},... | collective-permute-start | bytes 393224 | tf_op jit(solution)/shard_map/ppermute | solution.py:482
  25.7 6.5 %collective-permute-start.1 = (f32[512,128]{1,0:T(8,128)S(1)}, f32[512,128]{1,0:T(8,128)S(1)}, u32[]{:S(2)}, u32[]{:S(2)}) collective-permute-start(f32[512,128]{1,0:T(8,128)S(1)} %get-tuple-element.41), channel_id=1, source_target_pairs={{0,8},{8,0},{1,9},{9,1},{2,10},{10,2},{3,11},{11,3},{4,12},{12,4},... | collective-permute-start | bytes 786440 | tf_op jit(solution)/shard_map/ppermute | solution.py:482
  26.4 20.4 %all-to-all-start.1 = ((f32[32,32,128]{2,1,0:T(8,128)}), f32[32,32,128]{2,1,0:T(8,128)S(1)}, u32[]{:S(2)}, u32[]{:S(2)}) async-start(f32[32,32,128]{2,1,0:T(8,128)} %bitcast.4), calls=%async_computation.1 | async-start | bytes 1048576 | tf_op jit(solution)/shard_map/all_to_all | solution.py:503
  32.1 30.1 %copy-start = (bf16[512,128]{1,0:T(8,128)(2,1)S(1)}, bf16[512,128]{1,0:T(8,128)(2,1)}, u32[]{:S(2)}) copy-start(bf16[512,128]{1,0:T(8,128)(2,1)} %query.3) | copy-start | bytes 393220
  32.2 30.1 %copy-start.1 = (bf16[512,128]{1,0:T(8,128)(2,1)S(1)}, bf16[512,128]{1,0:T(8,128)(2,1)}, u32[]{:S(2)}) copy-start(bf16[512,128]{1,0:T(8,128)(2,1)} %key.3) | copy-start | bytes 393220
  32.2 30.1 %copy-start.2 = (bf16[512,128]{1,0:T(8,128)(2,1)S(1)}, bf16[512,128]{1,0:T(8,128)(2,1)}, u32[]{:S(2)}) copy-start(bf16[512,128]{1,0:T(8,128)(2,1)} %value.3) | copy-start | bytes 393220
  32.2 30.1 %copy-start.3 = (bf16[512,128]{1,0:T(8,128)(2,1)S(1)}, bf16[512,128]{1,0:T(8,128)(2,1)}, u32[]{:S(2)}) copy-start(bf16[512,128]{1,0:T(8,128)(2,1)} %grad.3) | copy-start | bytes 393220
  32.2 30.1 %copy-start.4 = (f32[128]{0:T(128)S(1)}, f32[128]{0:T(128)}, u32[]{:S(2)}) copy-start(f32[128]{0:T(128)} %param.23) | copy-start | bytes 1540
  38.3 1.3 %collective-permute-start.2 = (f32[48,128]{1,0:T(8,128)S(1)}, f32[48,128]{1,0:T(8,128)S(1)}, u32[]{:S(2)}, u32[]{:S(2)}) collective-permute-start(f32[48,128]{1,0:T(8,128)S(1)} %shard_map.218), channel_id=1, source_target_pairs={{0,8},{8,0},{1,9},{9,1},{2,10},{10,2},{3,11},{11,3},{4,12},{12,4},... | collective-permute-start | bytes 73736 | tf_op jit(solution)/shard_map/ppermute | solution.py:482
  39.6 5.1 %collective-permute-start.4 = (f32[40,128]{1,0:T(8,128)S(1)}, f32[40,128]{1,0:T(8,128)S(1)}, u32[]{:S(2)}, u32[]{:S(2)}) collective-permute-start(f32[40,128]{1,0:T(8,128)S(1)} %slice.8), channel_id=1, source_target_pairs={{0,2},{1,3},{2,0},{3,1},{4,6},{5,7},{6,4},{7,5},{8,10},{9,11},{10,... | collective-permute-start | bytes 61448 | tf_op jit(solution)/shard_map/ppermute | solution.py:482
  43.0 3.8 %collective-permute-start.5 = (f32[40,128]{1,0:T(8,128)S(1)}, f32[40,128]{1,0:T(8,128)S(1)}, u32[]{:S(2)}, u32[]{:S(2)}) collective-permute-start(f32[40,128]{1,0:T(8,128)S(1)} %slice.8), channel_id=1, source_target_pairs={{0,3},{1,2},{2,1},{3,0},{4,7},{5,6},{6,5},{7,4},{8,11},{9,10},{10,... | collective-permute-start | bytes 61448 | tf_op jit(solution)/shard_map/ppermute | solution.py:482
  43.0 3.8 %collective-permute-start.3 = (f32[40,128]{1,0:T(8,128)S(1)}, f32[40,128]{1,0:T(8,128)S(1)}, u32[]{:S(2)}, u32[]{:S(2)}) collective-permute-start(f32[40,128]{1,0:T(8,128)S(1)} %slice.8), channel_id=1, source_target_pairs={{0,1},{1,0},{2,3},{3,2},{4,5},{5,4},{6,7},{7,6},{8,9},{9,8},{10,11... | collective-permute-start | bytes 61448 | tf_op jit(solution)/shard_map/ppermute | solution.py:482
  46.8 7.5 %collective-permute-start.6 = (f32[40,128]{1,0:T(8,128)S(1)}, f32[40,128]{1,0:T(8,128)S(1)}, u32[]{:S(2)}, u32[]{:S(2)}) collective-permute-start(f32[40,128]{1,0:T(8,128)S(1)} %add_add_fusion), channel_id=1, source_target_pairs={{0,6},{1,7},{2,4},{3,5},{4,2},{5,3},{6,0},{7,1},{8,14},{9,15},{10,... | collective-permute-start | bytes 61448 | tf_op jit(solution)/shard_map/ppermute | solution.py:482
  55.1 16.2 %all-to-all-start.2 = ((f32[16,48,128]{2,1,0:T(8,128)}), f32[16,48,128]{2,1,0:T(8,128)S(1)}, u32[]{:S(2)}, u32[]{:S(2)}) async-start(f32[16,48,128]{2,1,0:T(8,128)} %broadcast_in_dim.2), calls=%async_computation.2 | async-start | bytes 786432 | tf_op jit(solution)/shard_map/all_to_all | solution.py:510

commit v5 on v4

--- a/solution.py
+++ b/solution.py
@@ -80,7 +80,7 @@
         return np.linalg.lstsq(basis * weight[:, None], values, rcond=None)[0]
 
     sine = fit(np.sin(2 * np.pi * nodes), nodes, 6)
-    cosine = fit(np.cos(2 * np.pi * nodes), np.ones_like(nodes), 7)
+    cosine = fit(np.cos(2 * np.pi * nodes), np.ones_like(nodes), 6)
     return [float(c) for c in sine], [float(c) for c in cosine]
 
 
@@ -232,7 +232,7 @@
 
 
 def filter_kernel(place, features, filter_in, filter_mid, filter_out,
-                  h1_high, h1_low, cos1, h2_high, h2_low, cos2, mine, theirs, shaped):
+                  hidden, cosines, mine, theirs, shaped):
     step = pl.program_id(0)
     own = own_channels(place())
     turn = 1.0 / (2.0 * math.pi)
@@ -246,16 +246,16 @@
         feature = features[:, piece]
         rows = jnp.concatenate([feature[:16], feature[:16], feature[16:]])
         sine, cosine = sine_cosine(dot(weight1, rows))
-        cos1[:, piece] = cosine
-        h1_high[:, piece], h1_low[:, piece] = halves(sine)
+        cosines[pl.ds(0, 64), piece] = cosine
+        hidden[pl.ds(0, 128), piece] = jnp.concatenate(halves(sine))
     for piece in pieces:
-        high = h1_high[:, piece]
-        sine, cosine = sine_cosine(dot(weight2, jnp.concatenate([high, h1_low[:, piece], high])))
-        cos2[:, piece] = cosine
-        h2_high[:, piece], h2_low[:, piece] = halves(sine)
+        rows = hidden[pl.ds(0, 128), piece]
+        sine, cosine = sine_cosine(dot(weight2, jnp.concatenate([rows, rows[:64]])))
+        cosines[pl.ds(64, 64), piece] = cosine
+        hidden[pl.ds(128, 128), piece] = jnp.concatenate(halves(sine))
     for k, piece in enumerate(pieces):
-        high = h2_high[:, piece]
-        values = dot(weight3, jnp.concatenate([high, h2_low[:, piece], high]))
+        rows = hidden[pl.ds(128, 128), piece]
+        values = dot(weight3, jnp.concatenate([rows, rows[:64]]))
         for m in range(PIECE // SIDE):
             row = 8 * (step * (STEP // SIDE) + k * (PIECE // SIDE) + m)
             shaped[pl.ds(pl.multiple_of(row, 8), 8), :] = values[:, SIDE * m : SIDE * (m + 1)]
@@ -283,41 +283,29 @@
     spectrum[...] = forward_rows(fields, first_fwd, second_fwd, twiddle)
 
 
-def convolve_kernel(place, field, spectrum, shaped_mine, shaped_other, decay, first_fwd, second_fwd, twiddle, second_inv,
-                    first_inv, sent, mine, theirs, sums):
+def correlate_kernel(place, field, shaped_mine, shaped_other, decay, first_fwd, second_fwd, twiddle, second_inv, first_inv,
+                     spectra, mine, theirs, sums):
     fields = []
     for c in range(OWN):
         for offset in (0, OWN):
             fields.append(
                 jnp.concatenate([field[pl.ds(8 * h + offset + c, SEQ, stride=SEQ), :] for h in range(ROWS // SIDE)])
             )
-    spectra = forward_rows(fields, first_fwd, second_fwd, twiddle)
+    spectra[...] = forward_rows(fields, first_fwd, second_fwd, twiddle)
     products = []
     for c in range(OWN):
-        gated, incoming = (spectra[SIDE * k : SIDE * (k + 1)] for k in (2 * c, 2 * c + 1))
-        kernel = spectrum[pl.ds(SIDE * c, SIDE), :]
+        gated, incoming = (spectra[pl.ds(SIDE * k, SIDE), :] for k in (2 * c, 2 * c + 1))
         gated_re, gated_im = gated[:, :SIDE], gated[:, SIDE:]
         incoming_re, incoming_im = incoming[:, :SIDE], incoming[:, SIDE:]
-        kernel_re, kernel_im = kernel[:, :SIDE], kernel[:, SIDE:]
-        products.append((
-            jnp.concatenate([kernel_re * gated_re - kernel_im * gated_im,
-                             kernel_re * gated_im + kernel_im * gated_re], axis=1),
-            jnp.concatenate([kernel_re * incoming_re + kernel_im * incoming_im,
-                             kernel_re * incoming_im - kernel_im * incoming_re], axis=1),
-            jnp.concatenate([gated_re * incoming_re + gated_im * incoming_im,
-                             gated_re * incoming_im - gated_im * incoming_re], axis=1),
-        ))
-    results = inverse_rows([p for c in range(OWN) for p in products[c][:2]] + [products[c][2] for c in range(OWN)],
-                           first_inv, second_inv, twiddle)
+        products.append(jnp.concatenate([gated_re * incoming_re + gated_im * incoming_im,
+                                         gated_re * incoming_im - gated_im * incoming_re], axis=1))
+    results = inverse_rows(products, first_inv, second_inv, twiddle)
     time = position_grid()
     me = place()
     lower = me % 2 == 0
     pair = lambda x: (jnp.where(lower, x, 0.0), jnp.where(lower, 0.0, x))
     for c, (window, shaped, rate) in enumerate(filter_fields(me, shaped_mine, shaped_other, decay)):
-        for offset, result in ((0, results[2 * c]), (OWN, results[2 * c + 1])):
-            for h in range(ROWS // SIDE):
-                sent[pl.ds(8 * h + offset + c, SEQ, stride=SEQ), :] = result[SEQ * h : SEQ * (h + 1), :]
-        dshaped = results[2 * OWN + c] * window
+        dshaped = results[c] * window
         slope = 0.5 / (rate + 1.0 / LENGTH) - time
         for part, sum_row, value in (
             (mine, None, jnp.where(lower, dshaped[:64], dshaped[64:])),
@@ -330,14 +318,34 @@
                 part[rows, :] = v
 
 
+def convolve_kernel(spectra, spectrum, twiddle, second_inv, first_inv, sent):
+    products = []
+    for c in range(OWN):
+        gated, incoming = (spectra[pl.ds(SIDE * k, SIDE), :] for k in (2 * c, 2 * c + 1))
+        kernel = spectrum[pl.ds(SIDE * c, SIDE), :]
+        gated_re, gated_im = gated[:, :SIDE], gated[:, SIDE:]
+        incoming_re, incoming_im = incoming[:, :SIDE], incoming[:, SIDE:]
+        kernel_re, kernel_im = kernel[:, :SIDE], kernel[:, SIDE:]
+        products += [
+            jnp.concatenate([kernel_re * gated_re - kernel_im * gated_im,
+                             kernel_re * gated_im + kernel_im * gated_re], axis=1),
+            jnp.concatenate([kernel_re * incoming_re + kernel_im * incoming_im,
+                             kernel_re * incoming_im - kernel_im * incoming_re], axis=1),
+        ]
+    results = inverse_rows(products, first_inv, second_inv, twiddle)
+    for c in range(OWN):
+        for offset, result in ((0, results[2 * c]), (OWN, results[2 * c + 1])):
+            for h in range(ROWS // SIDE):
+                sent[pl.ds(8 * h + offset + c, SEQ, stride=SEQ), :] = result[SEQ * h : SEQ * (h + 1), :]
+
+
 def pair_channels(place):
     row = lax.broadcasted_iota(jnp.int32, (8, SIDE), 0)
     lane = lax.broadcasted_iota(jnp.int32, (8, SIDE), 1)
     return jnp.where(lane == place - place % 2 + row // OWN + SEQ * (row % OWN), 1.0, 0.0).astype(F32)
 
 
-def backward_kernel(place, features, h1_high, h1_low, cos1, h2_high, h2_low, cos2, mine, other, sums, filter_mid, filter_out,
-                    grads, total, d2_high, d2_low, d1_high, d1_low):
+def backward_kernel(place, features, hidden, cosines, mine, other, sums, filter_mid, filter_out, grads, total, d2, d1):
     step = pl.program_id(0)
     weight3 = picked(filter_out, pair_channels(place())).astype(BF16)
     weight3 = jnp.concatenate([weight3[:64], weight3[:64], weight3[64:]], axis=1)
@@ -349,14 +357,14 @@
     for k, piece in enumerate(pieces):
         part = slice(PIECE * k, PIECE * (k + 1))
         rows = jnp.concatenate([shaped_high[:, part], shaped_low[:, part], shaped_high[:, part]])
-        d2_high[:, piece], d2_low[:, piece] = halves(dot(weight3, rows) * cos2[:, piece])
+        d2[:, piece] = jnp.concatenate(halves(dot(weight3, rows) * cosines[pl.ds(64, 64), piece]))
     for piece in pieces:
-        high = d2_high[:, piece]
-        d1_high[:, piece], d1_low[:, piece] = halves(
-            dot(weight2, jnp.concatenate([high, d2_low[:, piece], high])) * cos1[:, piece]
+        rows = d2[:, piece]
+        d1[:, piece] = jnp.concatenate(
+            halves(dot(weight2, jnp.concatenate([rows, rows[:64]])) * cosines[pl.ds(0, 64), piece])
         )
-    left = jnp.concatenate([h1_high[...], h1_low[...], h2_high[...], h2_low[...], d1_high[...], d1_low[...]])
-    right = jnp.concatenate([d2_high[...], d2_low[...], shaped_high, shaped_low, features[...]])
+    left = jnp.concatenate([hidden[...], d1[...]])
+    right = jnp.concatenate([d2[...], shaped_high, shaped_low, features[...]])
     product = dot_nt(left, right)
 
     @pl.when(step == 0)
@@ -375,30 +383,25 @@
         first = side[2][16:32] + (side[2][32:48] + side[3][16:32])
         third = side[0][:8] + (side[0][8:16] + side[1][:8])
         grads[pl.ds(32, 8), :] = jnp.concatenate([first[:8], first[8:]], axis=1)
-        lane = lax.broadcasted_iota(jnp.int32, (8, SIDE), 1)
+        channels = pair_channels(place())
         rates = jnp.sum(sums[pl.ds(0, 8), :], axis=1, keepdims=True)
         gains = jnp.sum(sums[pl.ds(8, 8), :], axis=1, keepdims=True)
-        grads[pl.ds(40, 8), :] = jnp.concatenate([third, jnp.zeros((8, 64), F32)], axis=1) + (
-            jnp.where(lane == 64, rates, 0.0) + jnp.where(lane == 65, gains, 0.0)
-        )
-
-
-def finish_kernel(gathered, grad_in, grad_mid, grad_out, grad_decay, grad_skip):
-    shared = gathered[pl.ds(0, 40), :]
-    for chip in range(1, 16):
-        shared = shared + gathered[pl.ds(48 * chip, 40), :]
-    grad_mid[pl.ds(0, 32), :] = shared[:32, :ORDER]
-    grad_mid[pl.ds(32, 32), :] = shared[:32, ORDER:]
-    grad_in[pl.ds(0, 8), :] = shared[32:, :ORDER]
-    grad_in[pl.ds(8, 8), :] = shared[32:, ORDER:]
-    row = lax.broadcasted_iota(jnp.int32, (SIDE, SIDE), 0)
-    lane = lax.broadcasted_iota(jnp.int32, (SIDE, SIDE), 1)
-    moved = jnp.where(lane == 2 * (row // 8) + row % 8 // OWN + SEQ * (row % OWN), 1.0, 0.0).astype(F32)
-    rows = jnp.concatenate([gathered[pl.ds(48 * chip + 40, 8), :] for chip in range(16)])
-    channels = dot_tn(rows, moved, lax.Precision.HIGHEST)
-    grad_out[...] = channels[:64]
-    grad_decay[...] = channels[64:65]
-    grad_skip[...] = channels[65:66]
+        grads[pl.ds(40, 64), :] = dot_tn(third, channels, lax.Precision.HIGHEST)
+        grads[pl.ds(104, 8), :] = jnp.concatenate([
+            jnp.sum(channels * rates, axis=0, keepdims=True),
+            jnp.sum(channels * gains, axis=0, keepdims=True),
+            jnp.zeros((6, SIDE), F32),
+        ])
+
+
+def finish_kernel(total, grad_in, grad_mid, grad_out, grad_decay, grad_skip):
+    grad_mid[pl.ds(0, 32), :] = total[:32, :ORDER]
+    grad_mid[pl.ds(32, 32), :] = total[:32, ORDER:]
+    grad_in[pl.ds(0, 8), :] = total[32:40, :ORDER]
+    grad_in[pl.ds(8, 8), :] = total[32:40, ORDER:]
+    grad_out[...] = total[40:104]
+    grad_decay[...] = total[104:105]
+    grad_skip[...] = total[105:106]
 
 
 def seq_place():
@@ -414,17 +417,15 @@
 
 def run_filter(features, filter_in, filter_mid, filter_out, place=seq_place, **kw):
     wide = lambda i: (0, i)
-    hidden = spec((ORDER, STEP), wide)
-    half, full = pltpu.HBM((ORDER, HALF), BF16), pltpu.HBM((ORDER, HALF), F32)
     return call(
         functools.partial(filter_kernel, place),
         HALF // STEP,
         [spec((32, STEP), wide), spec((16, ORDER)), spec((ORDER, ORDER)), spec((ORDER, SIDE))],
-        [hidden] * 6 + [spec((256, SIDE))] * 2,
-        [half, half, full, half, half, full, out((256, SIDE)), out((256, SIDE))],
+        [spec((256, STEP), wide), spec((SIDE, STEP), wide)] + [spec((256, SIDE))] * 2,
+        [pltpu.HBM((256, HALF), BF16), pltpu.HBM((SIDE, HALF), F32), out((256, SIDE)), out((256, SIDE))],
         scratch=[pltpu.VMEM((512, SIDE), F32)],
         flops=4 * 10**9, nbytes=10 * MIB, **kw,
-    )(features, filter_in, filter_mid, filter_out)
+    )(features, in_hbm(filter_in), in_hbm(filter_mid), in_hbm(filter_out))
 
 
 def run_spectrum(mine, other, decay, place=seq_place, **kw):
@@ -439,32 +440,43 @@
     )(mine, other, decay, first_fwd, second_fwd, twiddle)
 
 
-def run_convolve(field, spectrum, mine, other, decay, place=seq_place, **kw):
+def run_correlate(field, mine, other, decay, place=seq_place, **kw):
     first_fwd, second_fwd, twiddle, second_inv, first_inv = transform_tables()
     return call(
-        functools.partial(convolve_kernel, place),
+        functools.partial(correlate_kernel, place),
         1,
-        [spec((1024, SIDE)), spec((512, 256)), spec((256, SIDE)), spec((256, SIDE)), spec((1, SIDE)),
+        [spec((1024, SIDE)), spec((256, SIDE)), spec((256, SIDE)), spec((1, SIDE)),
          spec((256, 384)), spec((768, 256)), spec((SIDE, 256)), spec((768, 256)), spec((SIDE, 768))],
-        [spec((1024, SIDE)), spec((512, SIDE)), spec((512, SIDE)), spec((16, SIDE))],
-        [out((1024, SIDE)), pltpu.HBM((512, SIDE), F32), out((512, SIDE)), pltpu.HBM((16, SIDE), F32)],
-        flops=4 * 10**9, nbytes=4 * MIB, **kw,
-    )(field, spectrum, mine, other, decay, first_fwd, second_fwd, twiddle, second_inv, first_inv)
+        [spec((1024, 256)), spec((512, SIDE)), spec((512, SIDE)), spec((16, SIDE))],
+        [out((1024, 256)), out((512, SIDE)), out((512, SIDE)), out((16, SIDE))],
+        flops=2 * 10**9, nbytes=4 * MIB, **kw,
+    )(field, mine, other, decay, first_fwd, second_fwd, twiddle, second_inv, first_inv)
+
+
+def run_convolve(spectra, spectrum, **kw):
+    _, _, twiddle, second_inv, first_inv = transform_tables()
+    return call(
+        convolve_kernel,
+        1,
+        [spec((1024, 256)), spec((512, 256)), spec((SIDE, 256)), spec((768, 256)), spec((SIDE, 768))],
+        spec((1024, SIDE)),
+        out((1024, SIDE)),
+        flops=2 * 10**9, nbytes=3 * MIB, **kw,
+    )(spectra, spectrum, twiddle, second_inv, first_inv)
 
 
 def run_backward(features, hidden, mine, other, sums, filter_mid, filter_out, place=seq_place, **kw):
     wide = lambda i: (0, i)
-    block = spec((ORDER, BACK), wide)
     deep = spec((BACK // 16, SIDE), lambda i: (i, 0))
     return call(
         functools.partial(backward_kernel, place),
         HALF // BACK,
-        [spec((32, BACK), wide)] + [block] * 6 + [deep, deep, spec((16, SIDE)), spec((ORDER, ORDER)), spec((ORDER, SIDE))],
-        spec((48, SIDE)),
-        out((48, SIDE)),
-        scratch=[pltpu.VMEM((384, 176), F32)] + [pltpu.VMEM((ORDER, BACK), BF16)] * 4,
+        [spec((32, BACK), wide), spec((256, BACK), wide), spec((SIDE, BACK), wide), deep, deep, spec((16, SIDE)), spec((ORDER, ORDER)), spec((ORDER, SIDE))],
+        spec((112, SIDE)),
+        out((112, SIDE)),
+        scratch=[pltpu.VMEM((384, 176), F32)] + [pltpu.VMEM((SIDE, BACK), BF16)] * 2,
         flops=4 * 10**9, nbytes=10 * MIB, **kw,
-    )(features, *[in_hbm(x) for x in hidden], in_hbm(mine), other, in_hbm(sums), in_hbm(filter_mid), in_hbm(filter_out))
+    )(features, *hidden, mine, other, sums, in_hbm(filter_mid), in_hbm(filter_out))
 
 
 def run_receive(query, key, value, grad, skip, field, **kw):
@@ -473,9 +485,11 @@
                 [out((ROWS, SIDE), BF16)] * 4, **kw)(query, key, value, grad, skip, field)
 
 
-def run_finish(gathered, **kw):
+def run_finish(total, **kw):
     shapes = [(16, ORDER), (ORDER, ORDER), (ORDER, SIDE), (1, SIDE), (1, SIDE)]
-    return call(finish_kernel, 1, [spec((768, SIDE))], [spec(s) for s in shapes], [out(s) for s in shapes], **kw)(gathered)
+    return call(finish_kernel, 1, [spec((112, SIDE))], [spec(s) for s in shapes], [out(s) for s in shapes], **kw)(
+        total
+    )
 
 
 def exchanged(x, axis, distance):
@@ -499,17 +513,23 @@
     *hidden, mine, theirs = run_filter(features, filter_in, filter_mid, filter_out)
     other = exchanged(theirs, "core", 1)
     spectrum = run_spectrum(mine, other, decay)
-    sent, mine, theirs, sums = run_convolve(field, spectrum, mine, other, decay)
+    spectra, mine, theirs, sums = run_correlate(field, mine, other, decay)
+    mine, spectrum = lax.optimization_barrier((mine, spectrum))
+    grads = run_backward(features, hidden, mine, exchanged(theirs, "core", 1), sums, filter_mid, filter_out)
+    grads, spectra = lax.optimization_barrier((grads, spectra))
+    sent = run_convolve(spectra, spectrum)
     field = lax.all_to_all(sent.reshape(SEQ, SEQ, SIDE), SEQ_AXES, 0, 0, tiled=True).reshape(1024, SIDE)
-    grads = run_backward(features, hidden, mine, exchanged(theirs, "core", 1), sums, filter_mid, filter_out)
     grads = group_sum(grads, "core", (1,))
     shared = group_sum(grads[:40], "chan", (1, 2, 3))
-    shared, field = lax.optimization_barrier((shared, field))
+    shared, sent = lax.optimization_barrier((shared, sent))
     shared = group_sum(shared, "chan", (6,))
-    grads = jnp.broadcast_to(jnp.concatenate([shared, grads[40:]])[None], (16, 48, SIDE))
-    gathered = lax.all_to_all(grads, ("x", "y"), 0, 0, tiled=True).reshape(768, SIDE)
+    grads = jnp.concatenate([shared, grads[40:]])
+    grads = group_sum(grads, "x", (1, 2, 3))
+    grads, field = lax.optimization_barrier((grads, field))
+    grads = group_sum(grads, "y", (1, 2, 3))
     output, grad_query, grad_key, grad_value = run_receive(query, key, value, grad, skip, field)
-    first, second, third, rates, gains = run_finish(gathered)
+    grads, output = lax.optimization_barrier((grads, output))
+    first, second, third, rates, gains = run_finish(grads)
     return (output, grad_query, grad_key, grad_value, first, second, third, rates.reshape(SIDE), gains.reshape(SIDE))
 
 

time: 72.6 us -> 70.9 us (0.977); the launches traced: 72.2 us -> 69.5 us
  waiting for transfers between devices: 15.1 us -> 12 us
  starting transfers between devices: 32.2 us -> 33.4 us
  Pallas kernels: 23 us -> 22 us
    all_to_all x1 -> x0, waiting for transfers between devices: 7.92 us -> none  [body(): lax.all_to_all(grads, ('x', 'y'), 0, 0, tiled=True).reshape(768, SIDE)]
    ppermute x7 -> x13, starting transfers between devices: 12.1 us -> 19.6 us  [exchanged(): lax.ppermute(x, axis, [(i, i ^ distance) for i in range(lax.axis_size(axi...]
    all_to_all x1 -> x0, starting transfers between devices: 7.09 us -> none  [body(): lax.all_to_all(grads, ('x', 'y'), 0, 0, tiled=True).reshape(768, SIDE)]
    ppermute x7 -> x13, waiting for transfers between devices: 6.08 us -> 11.4 us  [exchanged(): lax.ppermute(x, axis, [(i, i ^ distance) for i in range(lax.axis_size(axi...]
    pallas_call x1, Pallas kernels: 6.08 us -> 4.81 us  [run_backward(): call(functools.partial(backward_kernel, place), HALF // BACK, [spec((32,...]
    dynamic_slice x1, local copies, waits for them, and re-layouts: 0.04 us -> 1.08 us  [body(): lax.dynamic_slice_in_dim(jnp.asarray(feature_table()), HALF * core, HALF,...]
    broadcast_in_dim x1 -> x0, local copies, waits for them, and re-layouts: 0.79 us -> none  [body(): jnp.broadcast_to(jnp.concatenate([shared, grads[40:]])[None], (16, 48, SI...]
    all_to_all x1, starting transfers between devices: 5.73 us -> 6.46 us  [body(): lax.all_to_all(sent.reshape(SEQ, SEQ, SIDE), SEQ_AXES, 0, 0, tiled=True)]
  transfers between devices with their start and end apart: 10 -> 15, of which waited for: 7 -> 9; matrix products, arithmetic and copies ran while one was open for 0% -> 2% of each run, Pallas kernels for 22% -> 18%
where the time goes in v5:
time: 70.9 us; the launch traced here: 69.5 us
  starting transfers between devices  33.4 us (47%)
  Pallas kernels  22 us (31%)
  waiting for transfers between devices  12 us (17%)
  local copies, waits for them, and re-layouts  1.17 us (2%)
  between operations  0.92 us (1%)
    ppermute x13, starting transfers between devices, exchanged(): lax.ppermute(x, axis, [(i, i ^ distance) for i in range(lax.axis_size(axi...  19.6 us
    ppermute x13, waiting for transfers between devices, exchanged(): lax.ppermute(x, axis, [(i, i ^ distance) for i in range(lax.axis_size(axi...  11.4 us
    pallas_call x1, Pallas kernels, run_filter(): call(functools.partial(filter_kernel, place), HALF // STEP, [spec((32, ST...  8.11 us
    all_to_all x1, starting transfers between devices, body(): field = lax.all_to_all(sent, SEQ_AXES, 0, 0, tiled=True).reshape(1024, SIDE)  7.33 us
    all_to_all x1, starting transfers between devices, body(): lax.all_to_all(sent.reshape(SEQ, SEQ, SIDE), SEQ_AXES, 0, 0, tiled=True)  6.46 us
    pallas_call x1, Pallas kernels, run_backward(): call(functools.partial(backward_kernel, place), HALF // BACK, [spec((32,...  4.81 us
    pallas_call x1, Pallas kernels, run_send(): call(send_kernel, 1, [pl.BlockSpec(memory_space=pltpu.HBM)] * 4, spec((10...  2.33 us
    pallas_call x1, Pallas kernels, run_convolve(): call(convolve_kernel, 1, [spec((1024, 256)), spec((512, 256)), spec((SIDE...  2.11 us
  transfers between devices with their start and end apart: 15, of which 9 were waited for; matrix products, arithmetic and copies ran while one was open for 2% of the time, Pallas kernels for 18%

profile of v5, /device:TPU:32, one launch (start us, length us, event | category | flops | bytes accessed | tf_op | source)
XLA Modules:
  0.0 69.5 jit_solution(2150191833393996712)
XLA Ops:
  0.6 2.3 %shard_map.215 = f32[1024,128]{1,0:T(8,128)} custom-call(bf16[512,128]{1,0:T(8,128)(2,1)} %query.3, bf16[512,128]{1,0:T(8,128)(2,1)} %key.3, bf16[512,128]{1,0:T(8,128)(2,1)} %value.3, bf16[512,128]{1,0:T(8,128)(2,1)} %grad.3), custom_call_target="tpu_custom_call" | custom-call | flops 1 | bytes 1 | tf_op jit(solution)/shard_map/pallas_call | solution.py:412
  3.0 7.3 %all-to-all-start = ((f32[32,32,128]{2,1,0:T(8,128)}), f32[32,32,128]{2,1,0:T(8,128)S(1)}, u32[]{:S(2)}, u32[]{:S(2)}) async-start(f32[32,32,128]{2,1,0:T(8,128)} %bitcast), calls=%async_computation | async-start | bytes 1048576 | tf_op jit(solution)/shard_map/all_to_all | solution.py:512
  10.3 1.1 %constant_dynamic-slice_fusion.features = bf16[32,8192]{1,0:T(8,128)(2,1)S(1)} fusion(bf16[32,16384]{1,0:T(8,128)(2,1)} %constant.24.clone, s32[]{:T(128)S(6)} %select_n.3), kind=kLoop, calls=%fused_computation.4 | loop fusion | bytes 1048580 | tf_op jit(solution)/shard_map/dynamic_slice | solution.py:510
  11.4 0.0 copy-start.5
  11.4 0.0 copy-start.6
  11.4 0.0 copy-start.7
  11.4 0.0 copy-start.8
  11.5 0.0 copy-start.9
  11.5 0.0 copy-start.10
  11.5 8.1 %shard_map.214 = (bf16[256,8192]{1,0:T(8,128)(2,1)}, f32[128,8192]{1,0:T(8,128)}, f32[256,128]{1,0:T(8,128)S(1)}, f32[256,128]{1,0:T(8,128)S(1)}) custom-call(bf16[32,8192]{1,0:T(8,128)(2,1)S(1)} %constant_dynamic-slice_fusion.features, f32[16,64]{1,0:T(8,128)} %filter_in.1, f32[64,64]{1,0:T(8,128)} %filter_mid.3, f32[64,128]{1,0:T(8,128)} %filter_out.3), custom_call_target="tpu_custom_call" | custom-call | flops 4000000000 | bytes 10485760 | tf_op jit(solution)/shard_map/pallas_call | solution.py:420
  19.6 0.3 collective-permute-start
  19.9 1.1 %collective-permute-done.shaped_other.other = f32[256,128]{1,0:T(8,128)S(1)} collective-permute-done((f32[256,128]{1,0:T(8,128)S(1)}, f32[256,128]{1,0:T(8,128)S(1)}, u32[]{:S(2)}, u32[]{:S(2)}) %collective-permute-start) | collective-permute-done | bytes 131104 | tf_op jit(solution)/shard_map/ppermute | solution.py:496
  20.9 0.6 all-to-all-done
  21.5 0.0 copy-done.5
  21.5 0.0 copy-done.6
  21.5 0.0 copy-done.7
  21.5 0.0 copy-done.8
  21.5 0.0 copy-done.9
  21.5 0.0 copy-done.10
  21.5 0.0 copy-start.11
  21.6 0.0 copy-start.12
  21.6 2.0 %shard_map.216 = (f32[1024,256]{1,0:T(8,128)S(1)}, f32[512,128]{1,0:T(8,128)S(1)}, f32[512,128]{1,0:T(8,128)S(1)}, f32[16,128]{1,0:T(8,128)S(1)}) custom-call(f32[1024,128]{1,0:T(8,128)S(1)} %bitcast.9, f32[256,128]{1,0:T(8,128)S(1)} %get-tuple-element.37.shaped_mine.mine, f32[256,128]{1,0:T(8,128)S(1)} %collective-permute-done.shaped_other.other, ...), custom_call_target="tpu_custom_call" | custom-call | flops 2000000000 | bytes 4194304 | tf_op jit(solution)/shard_map/pallas_call | solution.py:445
  23.6 0.8 %collective-permute-start.1 = (f32[512,128]{1,0:T(8,128)S(1)}, f32[512,128]{1,0:T(8,128)S(1)}, u32[]{:S(2)}, u32[]{:S(2)}) collective-permute-start(f32[512,128]{1,0:T(8,128)S(1)} %get-tuple-element.41), channel_id=1, source_target_pairs={{0,8},{8,0},{1,9},{9,1},{2,10},{10,2},{3,11},{11,3},{4,12},{12,4},... | collective-permute-start | bytes 786440 | tf_op jit(solution)/shard_map/ppermute | solution.py:496
  24.4 0.8 %shard_map.217.spectrum = f32[512,256]{1,0:T(8,128)S(1)} custom-call(f32[256,128]{1,0:T(8,128)S(1)} %get-tuple-element.37.shaped_mine.mine, f32[256,128]{1,0:T(8,128)S(1)} %collective-permute-done.shaped_other.other, f32[1,128]{1,0:T(1,128)S(1)} %bitcast.12, bf16[256,384]{1,0:T(8,128)(2,1)S(1)} %copy-done.9, bf16[768,256]{1,0:T(8,128)(2,1)S(1)} %copy-done.7, ...), custom_call_target="tpu_custom_call" | custom-call | flops 1000000000 | bytes 1048576 | tf_op jit(solution)/shard_map/pallas_call | solution.py:433
  25.2 0.3 collective-permute-done.1.other
  25.5 0.0 copy-done.11
  25.5 0.0 copy-done.12
  25.5 4.8 %shard_map.218 = f32[112,128]{1,0:T(8,128)S(1)} custom-call(bf16[32,8192]{1,0:T(8,128)(2,1)S(1)} %constant_dynamic-slice_fusion.features, bf16[256,8192]{1,0:T(8,128)(2,1)S(1)} %copy-done.11, f32[128,8192]{1,0:T(8,128)S(1)} %copy-done.12, f32[512,128]{1,0:T(8,128)S(1)} %get-tuple-element.40.mine, f32[512,128]{1,0:T(8,128)S(1)} %collective-permute-done.1.other, ...), custom_call_target="tpu_custom_call" | custom-call | flops 4000000000 | bytes 10485760 | tf_op jit(solution)/shard_map/pallas_call | solution.py:471
  30.4 0.5 collective-permute-start.2
  30.8 0.9 %collective-permute-done.2 = f32[112,128]{1,0:T(8,128)S(1)} collective-permute-done((f32[112,128]{1,0:T(8,128)S(1)}, f32[112,128]{1,0:T(8,128)S(1)}, u32[]{:S(2)}, u32[]{:S(2)}) %collective-permute-start.2) | collective-permute-done | bytes 57376 | tf_op jit(solution)/shard_map/ppermute | solution.py:496
  31.7 0.0 copy-start
  31.7 0.0 copy-start.1
  31.8 0.0 copy-start.2
  31.8 0.0 copy-start.3
  31.8 0.0 copy-start.4
  31.8 3.4 %collective-permute-start.4 = (f32[40,128]{1,0:T(8,128)S(1)}, f32[40,128]{1,0:T(8,128)S(1)}, u32[]{:S(2)}, u32[]{:S(2)}) collective-permute-start(f32[40,128]{1,0:T(8,128)S(1)} %slice.8), channel_id=1, source_target_pairs={{0,2},{1,3},{2,0},{3,1},{4,6},{5,7},{6,4},{7,5},{8,10},{9,11},{10,... | collective-permute-start | bytes 61448 | tf_op jit(solution)/shard_map/ppermute | solution.py:496
  35.2 0.0 collective-permute-start.5
  35.2 1.6 %collective-permute-start.3 = (f32[40,128]{1,0:T(8,128)S(1)}, f32[40,128]{1,0:T(8,128)S(1)}, u32[]{:S(2)}, u32[]{:S(2)}) collective-permute-start(f32[40,128]{1,0:T(8,128)S(1)} %slice.8), channel_id=1, source_target_pairs={{0,1},{1,0},{2,3},{3,2},{4,5},{5,4},{6,7},{7,6},{8,9},{9,8},{10,11... | collective-permute-start | bytes 61448 | tf_op jit(solution)/shard_map/ppermute | solution.py:496
  36.7 2.1 %shard_map.219 = f32[1024,128]{1,0:T(8,128)} custom-call(f32[1024,256]{1,0:T(8,128)S(1)} %get-tuple-element.45.spectra, f32[512,256]{1,0:T(8,128)S(1)} %shard_map.217.spectrum, f32[128,256]{1,0:T(8,128)S(1)} %copy-done.10, bf16[768,256]{1,0:T(8,128)(2,1)S(1)} %copy-done.6, bf16[128,768]{1,0:T(8,128)(2,1)S(1)} %copy-done.8), custom_call_target="tpu_custom_call" | custom-call | flops 2000000000 | bytes 3145728 | tf_op jit(solution)/shard_map/pallas_call | solution.py:458
  38.8 6.5 %all-to-all-start.1 = ((f32[32,32,128]{2,1,0:T(8,128)}), f32[32,32,128]{2,1,0:T(8,128)S(1)}, u32[]{:S(2)}, u32[]{:S(2)}) async-start(f32[32,32,128]{2,1,0:T(8,128)} %bitcast.3), calls=%async_computation.1 | async-start | bytes 1048576 | tf_op jit(solution)/shard_map/all_to_all | solution.py:521
  45.3 0.0 collective-permute-done.4
  45.3 0.0 collective-permute-done.5
  45.3 0.0 collective-permute-done.3
  45.4 4.1 %collective-permute-start.6 = (f32[40,128]{1,0:T(8,128)S(1)}, f32[40,128]{1,0:T(8,128)S(1)}, u32[]{:S(2)}, u32[]{:S(2)}) collective-permute-start(f32[40,128]{1,0:T(8,128)S(1)} %add_add_fusion.2), channel_id=1, source_target_pairs={{0,6},{1,7},{2,4},{3,5},{4,2},{5,3},{6,0},{7,1},{8,14},{9,15},{10,... | collective-permute-start | bytes 61448 | tf_op jit(solution)/shard_map/ppermute | solution.py:496
  49.5 1.8 %collective-permute-done.6 = f32[40,128]{1,0:T(8,128)S(1)} collective-permute-done((f32[40,128]{1,0:T(8,128)S(1)}, f32[40,128]{1,0:T(8,128)S(1)}, u32[]{:S(2)}, u32[]{:S(2)}) %collective-permute-start.6) | collective-permute-done | bytes 20512 | tf_op jit(solution)/shard_map/ppermute | solution.py:496
  51.4 3.6 %collective-permute-start.8 = (f32[112,128]{1,0:T(8,128)S(1)}, f32[112,128]{1,0:T(8,128)S(1)}, u32[]{:S(2)}, u32[]{:S(2)}) collective-permute-start(f32[112,128]{1,0:T(8,128)S(1)} %pad_maximum_fusion), channel_id=1, source_target_pairs={{0,128},{64,192},{128,0},{192,64},{1,129},{65,193},{129,1},{193,65... | collective-permute-start | bytes 172040 | tf_op jit(solution)/shard_map/ppermute | solution.py:496
  54.9 1.2 %collective-permute-start.9 = (f32[112,128]{1,0:T(8,128)S(1)}, f32[112,128]{1,0:T(8,128)S(1)}, u32[]{:S(2)}, u32[]{:S(2)}) collective-permute-start(f32[112,128]{1,0:T(8,128)S(1)} %pad_maximum_fusion), channel_id=1, source_target_pairs={{0,192},{64,128},{128,64},{192,0},{1,193},{65,129},{129,65},{193,1... | collective-permute-start | bytes 172040 | tf_op jit(solution)/shard_map/ppermute | solution.py:496
  56.1 0.0 collective-permute-start.7
  56.1 1.2 %collective-permute-done.8 = f32[112,128]{1,0:T(8,128)S(1)} collective-permute-done((f32[112,128]{1,0:T(8,128)S(1)}, f32[112,128]{1,0:T(8,128)S(1)}, u32[]{:S(2)}, u32[]{:S(2)}) %collective-permute-start.8) | collective-permute-done | bytes 57376 | tf_op jit(solution)/shard_map/ppermute | solution.py:496
  57.3 3.0 %collective-permute-done.9 = f32[112,128]{1,0:T(8,128)S(1)} collective-permute-done((f32[112,128]{1,0:T(8,128)S(1)}, f32[112,128]{1,0:T(8,128)S(1)}, u32[]{:S(2)}, u32[]{:S(2)}) %collective-permute-start.9) | collective-permute-done | bytes 57376 | tf_op jit(solution)/shard_map/ppermute | solution.py:496
  60.3 0.0 collective-permute-done.7
  60.3 0.0 all-to-all-done.1
  60.3 3.1 %collective-permute-start.11 = (f32[112,128]{1,0:T(8,128)S(1)}, f32[112,128]{1,0:T(8,128)S(1)}, u32[]{:S(2)}, u32[]{:S(2)}) collective-permute-start(f32[112,128]{1,0:T(8,128)S(1)} %add_add_fusion.1), channel_id=1, source_target_pairs={{0,32},{16,48},{32,0},{48,16},{1,33},{17,49},{33,1},{49,17},{2,34}... | collective-permute-start | bytes 172040 | tf_op jit(solution)/shard_map/ppermute | solution.py:496
  63.4 1.2 %collective-permute-start.12 = (f32[112,128]{1,0:T(8,128)S(1)}, f32[112,128]{1,0:T(8,128)S(1)}, u32[]{:S(2)}, u32[]{:S(2)}) collective-permute-start(f32[112,128]{1,0:T(8,128)S(1)} %add_add_fusion.1), channel_id=1, source_target_pairs={{0,48},{16,32},{32,16},{48,0},{1,49},{17,33},{33,17},{49,1},{2,50}... | collective-permute-start | bytes 172040 | tf_op jit(solution)/shard_map/ppermute | solution.py:496
  64.6 0.0 collective-permute-start.10
  64.6 0.0 copy-done
  64.6 0.0 copy-done.2
  64.6 0.0 copy-done.3
  64.6 0.0 copy-done.4
  64.6 1.2 %shard_map.220 = (bf16[512,128]{1,0:T(8,128)(2,1)}, bf16[512,128]{1,0:T(8,128)(2,1)}, bf16[512,128]{1,0:T(8,128)(2,1)}, bf16[512,128]{1,0:T(8,128)(2,1)}) custom-call(bf16[512,128]{1,0:T(8,128)(2,1)S(1)} %copy-done, bf16[512,128]{1,0:T(8,128)(2,1)S(1)} %copy-done.1, bf16[512,128]{1,0:T(8,128)(2,1)S(1)} %copy-done.2, bf16[512,128]{1,0:T(8,128)(2,1)S(1)} %copy-done.3, ...), custom_call_target="tpu_custom_call" | custom-call | flops 1 | bytes 1 | tf_op jit(solution)/shard_map/pallas_call | solution.py:484
  65.8 0.6 collective-permute-done.11
  66.4 2.4 %collective-permute-done.12 = f32[112,128]{1,0:T(8,128)S(1)} collective-permute-done((f32[112,128]{1,0:T(8,128)S(1)}, f32[112,128]{1,0:T(8,128)S(1)}, u32[]{:S(2)}, u32[]{:S(2)}) %collective-permute-start.12) | collective-permute-done | bytes 57376 | tf_op jit(solution)/shard_map/ppermute | solution.py:496
  68.8 0.0 collective-permute-done.10
  68.8 0.7 %shard_map.221 = (f32[16,64]{1,0:T(8,128)}, f32[64,64]{1,0:T(8,128)}, f32[64,128]{1,0:T(8,128)}, f32[1,128]{1,0:T(1,128)}, f32[1,128]{1,0:T(1,128)}) custom-call(f32[112,128]{1,0:T(8,128)S(1)} %add_add_fusion.total), custom_call_target="tpu_custom_call" | custom-call | flops 1 | bytes 1 | tf_op jit(solution)/shard_map/pallas_call | solution.py:490
  (9 shorter events, 0.1 us)
Async XLA Ops:
  3.0 18.5 %all-to-all-start = ((f32[32,32,128]{2,1,0:T(8,128)}), f32[32,32,128]{2,1,0:T(8,128)S(1)}, u32[]{:S(2)}, u32[]{:S(2)}) async-start(f32[32,32,128]{2,1,0:T(8,128)} %bitcast), calls=%async_computation | async-start | bytes 1048576 | tf_op jit(solution)/shard_map/all_to_all | solution.py:512
  11.4 10.1 %copy-start.5 = (f32[128]{0:T(128)S(1)}, f32[128]{0:T(128)}, u32[]{:S(2)}) copy-start(f32[128]{0:T(128)} %param.22) | copy-start | bytes 1540
  11.4 10.1 %copy-start.6 = (bf16[768,256]{1,0:T(8,128)(2,1)S(1)}, bf16[768,256]{1,0:T(8,128)(2,1)}, u32[]{:S(2)}) copy-start(bf16[768,256]{1,0:T(8,128)(2,1)} %constant.28.clone.second_inv) | copy-start | bytes 1179652
  11.4 10.1 %copy-start.7 = (bf16[768,256]{1,0:T(8,128)(2,1)S(1)}, bf16[768,256]{1,0:T(8,128)(2,1)}, u32[]{:S(2)}) copy-start(bf16[768,256]{1,0:T(8,128)(2,1)} %constant.26.clone.second_fwd) | copy-start | bytes 1179652
  11.4 10.1 %copy-start.8 = (bf16[128,768]{1,0:T(8,128)(2,1)S(1)}, bf16[128,768]{1,0:T(8,128)(2,1)}, u32[]{:S(2)}) copy-start(bf16[128,768]{1,0:T(8,128)(2,1)} %constant.29.clone.first_inv) | copy-start | bytes 589828
  11.5 10.1 %copy-start.9 = (bf16[256,384]{1,0:T(8,128)(2,1)S(1)}, bf16[256,384]{1,0:T(8,128)(2,1)}, u32[]{:S(2)}) copy-start(bf16[256,384]{1,0:T(8,128)(2,1)} %constant.25.clone.first_fwd) | copy-start | bytes 589828
  11.5 10.1 %copy-start.10 = (f32[128,256]{1,0:T(8,128)S(1)}, f32[128,256]{1,0:T(8,128)}, u32[]{:S(2)}) copy-start(f32[128,256]{1,0:T(8,128)} %constant.27.clone.twiddle) | copy-start | bytes 393220
  19.6 1.3 %collective-permute-start = (f32[256,128]{1,0:T(8,128)S(1)}, f32[256,128]{1,0:T(8,128)S(1)}, u32[]{:S(2)}, u32[]{:S(2)}) collective-permute-start(f32[256,128]{1,0:T(8,128)S(1)} %get-tuple-element.38), channel_id=1, source_target_pairs={{0,8},{8,0},{1,9},{9,1},{2,10},{10,2},{3,11},{11,3},{4,12},{12,4},... | collective-permute-start | bytes 393224 | tf_op jit(solution)/shard_map/ppermute | solution.py:496
  21.5 4.0 %copy-start.11 = (bf16[256,8192]{1,0:T(8,128)(2,1)S(1)}, bf16[256,8192]{1,0:T(8,128)(2,1)}, u32[]{:S(2)}) copy-start(bf16[256,8192]{1,0:T(8,128)(2,1)} %get-tuple-element.35.hidden) | copy-start | bytes 12582916
  21.6 4.0 %copy-start.12 = (f32[128,8192]{1,0:T(8,128)S(1)}, f32[128,8192]{1,0:T(8,128)}, u32[]{:S(2)}) copy-start(f32[128,8192]{1,0:T(8,128)} %get-tuple-element.36.cosines) | copy-start | bytes 12582916
  23.6 2.0 %collective-permute-start.1 = (f32[512,128]{1,0:T(8,128)S(1)}, f32[512,128]{1,0:T(8,128)S(1)}, u32[]{:S(2)}, u32[]{:S(2)}) collective-permute-start(f32[512,128]{1,0:T(8,128)S(1)} %get-tuple-element.41), channel_id=1, source_target_pairs={{0,8},{8,0},{1,9},{9,1},{2,10},{10,2},{3,11},{11,3},{4,12},{12,4},... | collective-permute-start | bytes 786440 | tf_op jit(solution)/shard_map/ppermute | solution.py:496
  30.4 1.4 %collective-permute-start.2 = (f32[112,128]{1,0:T(8,128)S(1)}, f32[112,128]{1,0:T(8,128)S(1)}, u32[]{:S(2)}, u32[]{:S(2)}) collective-permute-start(f32[112,128]{1,0:T(8,128)S(1)} %shard_map.218), channel_id=1, source_target_pairs={{0,8},{8,0},{1,9},{9,1},{2,10},{10,2},{3,11},{11,3},{4,12},{12,4},... | collective-permute-start | bytes 172040 | tf_op jit(solution)/shard_map/ppermute | solution.py:496
  31.7 32.8 %copy-start = (bf16[512,128]{1,0:T(8,128)(2,1)S(1)}, bf16[512,128]{1,0:T(8,128)(2,1)}, u32[]{:S(2)}) copy-start(bf16[512,128]{1,0:T(8,128)(2,1)} %query.3) | copy-start | bytes 393220
  31.7 32.8 %copy-start.1 = (bf16[512,128]{1,0:T(8,128)(2,1)S(1)}, bf16[512,128]{1,0:T(8,128)(2,1)}, u32[]{:S(2)}) copy-start(bf16[512,128]{1,0:T(8,128)(2,1)} %key.3) | copy-start | bytes 393220
  31.8 32.8 %copy-start.2 = (bf16[512,128]{1,0:T(8,128)(2,1)S(1)}, bf16[512,128]{1,0:T(8,128)(2,1)}, u32[]{:S(2)}) copy-start(bf16[512,128]{1,0:T(8,128)(2,1)} %value.3) | copy-start | bytes 393220
  31.8 32.8 %copy-start.3 = (bf16[512,128]{1,0:T(8,128)(2,1)S(1)}, bf16[512,128]{1,0:T(8,128)(2,1)}, u32[]{:S(2)}) copy-start(bf16[512,128]{1,0:T(8,128)(2,1)} %grad.3) | copy-start | bytes 393220
  31.8 32.8 %copy-start.4 = (f32[128]{0:T(128)S(1)}, f32[128]{0:T(128)}, u32[]{:S(2)}) copy-start(f32[128]{0:T(128)} %param.23) | copy-start | bytes 1540
  31.8 13.5 %collective-permute-start.4 = (f32[40,128]{1,0:T(8,128)S(1)}, f32[40,128]{1,0:T(8,128)S(1)}, u32[]{:S(2)}, u32[]{:S(2)}) collective-permute-start(f32[40,128]{1,0:T(8,128)S(1)} %slice.8), channel_id=1, source_target_pairs={{0,2},{1,3},{2,0},{3,1},{4,6},{5,7},{6,4},{7,5},{8,10},{9,11},{10,... | collective-permute-start | bytes 61448 | tf_op jit(solution)/shard_map/ppermute | solution.py:496
  35.2 10.2 %collective-permute-start.5 = (f32[40,128]{1,0:T(8,128)S(1)}, f32[40,128]{1,0:T(8,128)S(1)}, u32[]{:S(2)}, u32[]{:S(2)}) collective-permute-start(f32[40,128]{1,0:T(8,128)S(1)} %slice.8), channel_id=1, source_target_pairs={{0,3},{1,2},{2,1},{3,0},{4,7},{5,6},{6,5},{7,4},{8,11},{9,10},{10,... | collective-permute-start | bytes 61448 | tf_op jit(solution)/shard_map/ppermute | solution.py:496
  35.2 10.2 %collective-permute-start.3 = (f32[40,128]{1,0:T(8,128)S(1)}, f32[40,128]{1,0:T(8,128)S(1)}, u32[]{:S(2)}, u32[]{:S(2)}) collective-permute-start(f32[40,128]{1,0:T(8,128)S(1)} %slice.8), channel_id=1, source_target_pairs={{0,1},{1,0},{2,3},{3,2},{4,5},{5,4},{6,7},{7,6},{8,9},{9,8},{10,11... | collective-permute-start | bytes 61448 | tf_op jit(solution)/shard_map/ppermute | solution.py:496
  38.8 21.5 %all-to-all-start.1 = ((f32[32,32,128]{2,1,0:T(8,128)}), f32[32,32,128]{2,1,0:T(8,128)S(1)}, u32[]{:S(2)}, u32[]{:S(2)}) async-start(f32[32,32,128]{2,1,0:T(8,128)} %bitcast.3), calls=%async_computation.1 | async-start | bytes 1048576 | tf_op jit(solution)/shard_map/all_to_all | solution.py:521
  45.4 6.0 %collective-permute-start.6 = (f32[40,128]{1,0:T(8,128)S(1)}, f32[40,128]{1,0:T(8,128)S(1)}, u32[]{:S(2)}, u32[]{:S(2)}) collective-permute-start(f32[40,128]{1,0:T(8,128)S(1)} %add_add_fusion.2), channel_id=1, source_target_pairs={{0,6},{1,7},{2,4},{3,5},{4,2},{5,3},{6,0},{7,1},{8,14},{9,15},{10,... | collective-permute-start | bytes 61448 | tf_op jit(solution)/shard_map/ppermute | solution.py:496
  51.4 5.9 %collective-permute-start.8 = (f32[112,128]{1,0:T(8,128)S(1)}, f32[112,128]{1,0:T(8,128)S(1)}, u32[]{:S(2)}, u32[]{:S(2)}) collective-permute-start(f32[112,128]{1,0:T(8,128)S(1)} %pad_maximum_fusion), channel_id=1, source_target_pairs={{0,128},{64,192},{128,0},{192,64},{1,129},{65,193},{129,1},{193,65... | collective-permute-start | bytes 172040 | tf_op jit(solution)/shard_map/ppermute | solution.py:496
  54.9 5.4 %collective-permute-start.9 = (f32[112,128]{1,0:T(8,128)S(1)}, f32[112,128]{1,0:T(8,128)S(1)}, u32[]{:S(2)}, u32[]{:S(2)}) collective-permute-start(f32[112,128]{1,0:T(8,128)S(1)} %pad_maximum_fusion), channel_id=1, source_target_pairs={{0,192},{64,128},{128,64},{192,0},{1,193},{65,129},{129,65},{193,1... | collective-permute-start | bytes 172040 | tf_op jit(solution)/shard_map/ppermute | solution.py:496
  56.1 4.2 %collective-permute-start.7 = (f32[112,128]{1,0:T(8,128)S(1)}, f32[112,128]{1,0:T(8,128)S(1)}, u32[]{:S(2)}, u32[]{:S(2)}) collective-permute-start(f32[112,128]{1,0:T(8,128)S(1)} %pad_maximum_fusion), channel_id=1, source_target_pairs={{0,64},{64,0},{128,192},{192,128},{1,65},{65,1},{129,193},{193,129... | collective-permute-start | bytes 172040 | tf_op jit(solution)/shard_map/ppermute | solution.py:496
  60.3 6.0 %collective-permute-start.11 = (f32[112,128]{1,0:T(8,128)S(1)}, f32[112,128]{1,0:T(8,128)S(1)}, u32[]{:S(2)}, u32[]{:S(2)}) collective-permute-start(f32[112,128]{1,0:T(8,128)S(1)} %add_add_fusion.1), channel_id=1, source_target_pairs={{0,32},{16,48},{32,0},{48,16},{1,33},{17,49},{33,1},{49,17},{2,34}... | collective-permute-start | bytes 172040 | tf_op jit(solution)/shard_map/ppermute | solution.py:496
  63.4 5.4 %collective-permute-start.12 = (f32[112,128]{1,0:T(8,128)S(1)}, f32[112,128]{1,0:T(8,128)S(1)}, u32[]{:S(2)}, u32[]{:S(2)}) collective-permute-start(f32[112,128]{1,0:T(8,128)S(1)} %add_add_fusion.1), channel_id=1, source_target_pairs={{0,48},{16,32},{32,16},{48,0},{1,49},{17,33},{33,17},{49,1},{2,50}... | collective-permute-start | bytes 172040 | tf_op jit(solution)/shard_map/ppermute | solution.py:496
  64.6 4.2 %collective-permute-start.10 = (f32[112,128]{1,0:T(8,128)S(1)}, f32[112,128]{1,0:T(8,128)S(1)}, u32[]{:S(2)}, u32[]{:S(2)}) collective-permute-start(f32[112,128]{1,0:T(8,128)S(1)} %add_add_fusion.1), channel_id=1, source_target_pairs={{0,16},{16,0},{32,48},{48,32},{1,17},{17,1},{33,49},{49,33},{2,18}... | collective-permute-start | bytes 172040 | tf_op jit(solution)/shard_map/ppermute | solution.py:496

commit v6 on v5

--- a/solution.py
+++ b/solution.py
@@ -20,7 +20,6 @@
 ORDER = 64
 STEP = 2048
 PIECE = 256
-BACK = 4096
 HALF = LENGTH // 2
 MIB = 1 << 20
 SEQ_AXES = ("x", "y", "core")
@@ -171,11 +170,18 @@
     )
 
 
-def send_kernel(query, key, value, grad, sent, held, sems):
+def send_kernel(place, query, key, value, grad, table, sent, features, held, half_held, sems):
+    half = pl.ds(pl.multiple_of(HALF * (place() % 2), HALF), HALF)
+    features_in = pltpu.make_async_copy(table.at[:, half], half_held, sems.at[4])
+    features_out = pltpu.make_async_copy(half_held, features, sems.at[5])
     copies = [pltpu.make_async_copy(x, held.at[k], sems.at[k]) for k, x in enumerate((key, value, grad, query))]
     for copy in copies:
         copy.start()
+    features_in.start()
     for offset, first, second in ((0, 0, 1), (OWN, 2, 3)):
+        if offset:
+            features_in.wait()
+            features_out.start()
         copies[first].wait()
         copies[second].wait()
         for h in range(ROWS // SIDE):
@@ -183,6 +189,7 @@
             block = (held[first, rows, :].astype(F32) * held[second, rows, :].astype(F32)).T
             for c in range(OWN):
                 sent[pl.ds(8 * h + offset + c, SEQ, stride=SEQ), :] = block[SEQ * c : SEQ * (c + 1), :]
+    features_out.wait()
 
 
 def receive_kernel(query, key, value, grad, skip, field, output, grad_query, grad_key, grad_value):
@@ -345,53 +352,44 @@
     return jnp.where(lane == place - place % 2 + row // OWN + SEQ * (row % OWN), 1.0, 0.0).astype(F32)
 
 
-def backward_kernel(place, features, hidden, cosines, mine, other, sums, filter_mid, filter_out, grads, total, d2, d1):
-    step = pl.program_id(0)
+def backward_kernel(place, features, hidden, cosines, mine, other, sums, filter_mid, filter_out, grads, d2, d1, shaped):
     weight3 = picked(filter_out, pair_channels(place())).astype(BF16)
     weight3 = jnp.concatenate([weight3[:64], weight3[:64], weight3[64:]], axis=1)
     weight2 = weight_left(filter_mid[...], 1)
-    pieces = [pl.ds(PIECE * k, PIECE) for k in range(BACK // PIECE)]
-    shaped_high, shaped_low = halves(
-        jnp.concatenate([mine[pl.ds(8 * m, 8), :] + other[pl.ds(8 * m, 8), :] for m in range(BACK // SIDE)], axis=1)
-    )
-    for k, piece in enumerate(pieces):
-        part = slice(PIECE * k, PIECE * (k + 1))
-        rows = jnp.concatenate([shaped_high[:, part], shaped_low[:, part], shaped_high[:, part]])
+    pieces = range(0, HALF, PIECE)
+    for start in pieces:
+        piece = pl.ds(start, PIECE)
+        tiles = range(start // SIDE, (start + PIECE) // SIDE)
+        both = jnp.concatenate(
+            halves(jnp.concatenate([mine[pl.ds(8 * m, 8), :] + other[pl.ds(8 * m, 8), :] for m in tiles], axis=1))
+        )
+        shaped[:, piece] = both
+        rows = jnp.concatenate([both, both[:8]])
         d2[:, piece] = jnp.concatenate(halves(dot(weight3, rows) * cosines[pl.ds(64, 64), piece]))
-    for piece in pieces:
+    for start in pieces:
+        piece = pl.ds(start, PIECE)
         rows = d2[:, piece]
         d1[:, piece] = jnp.concatenate(
             halves(dot(weight2, jnp.concatenate([rows, rows[:64]])) * cosines[pl.ds(0, 64), piece])
         )
     left = jnp.concatenate([hidden[...], d1[...]])
-    right = jnp.concatenate([d2[...], shaped_high, shaped_low, features[...]])
-    product = dot_nt(left, right)
-
-    @pl.when(step == 0)
-    def _():
-        total[...] = product
-
-    @pl.when(step > 0)
-    def _():
-        total[...] += product
-
-    @pl.when(step == HALF // BACK - 1)
-    def _():
-        mid = total[:64, :64] + (total[:64, 64:128] + total[64:128, :64])
-        grads[pl.ds(0, 32), :] = jnp.concatenate([mid[:32], mid[32:]], axis=1)
-        side = [jnp.concatenate([total[64 * k : 64 * (k + 1), 128:], jnp.zeros((64, 80), F32)], axis=1).T for k in range(2, 6)]
-        first = side[2][16:32] + (side[2][32:48] + side[3][16:32])
-        third = side[0][:8] + (side[0][8:16] + side[1][:8])
-        grads[pl.ds(32, 8), :] = jnp.concatenate([first[:8], first[8:]], axis=1)
-        channels = pair_channels(place())
-        rates = jnp.sum(sums[pl.ds(0, 8), :], axis=1, keepdims=True)
-        gains = jnp.sum(sums[pl.ds(8, 8), :], axis=1, keepdims=True)
-        grads[pl.ds(40, 64), :] = dot_tn(third, channels, lax.Precision.HIGHEST)
-        grads[pl.ds(104, 8), :] = jnp.concatenate([
-            jnp.sum(channels * rates, axis=0, keepdims=True),
-            jnp.sum(channels * gains, axis=0, keepdims=True),
-            jnp.zeros((6, SIDE), F32),
-        ])
+    right = jnp.concatenate([d2[...], shaped[...], features[...]])
+    total = dot_nt(left, right)
+    mid = total[:64, :64] + (total[:64, 64:128] + total[64:128, :64])
+    grads[pl.ds(0, 32), :] = jnp.concatenate([mid[:32], mid[32:]], axis=1)
+    side = [jnp.concatenate([total[64 * k : 64 * (k + 1), 128:], jnp.zeros((64, 80), F32)], axis=1).T for k in range(2, 6)]
+    first = side[2][16:32] + (side[2][32:48] + side[3][16:32])
+    third = side[0][:8] + (side[0][8:16] + side[1][:8])
+    grads[pl.ds(32, 8), :] = jnp.concatenate([first[:8], first[8:]], axis=1)
+    channels = pair_channels(place())
+    rates = jnp.sum(sums[pl.ds(0, 8), :], axis=1, keepdims=True)
+    gains = jnp.sum(sums[pl.ds(8, 8), :], axis=1, keepdims=True)
+    grads[pl.ds(40, 64), :] = dot_tn(third, channels, lax.Precision.HIGHEST)
+    grads[pl.ds(104, 8), :] = jnp.concatenate([
+        jnp.sum(channels * rates, axis=0, keepdims=True),
+        jnp.sum(channels * gains, axis=0, keepdims=True),
+        jnp.zeros((6, SIDE), F32),
+    ])
 
 
 def finish_kernel(total, grad_in, grad_mid, grad_out, grad_decay, grad_skip):
@@ -408,11 +406,13 @@
     return lax.axis_index(SEQ_AXES)
 
 
-def run_send(query, key, value, grad, **kw):
+def run_send(query, key, value, grad, place=seq_place, **kw):
+    whole = pl.BlockSpec(memory_space=pl.ANY)
     return call(
-        send_kernel, 1, [pl.BlockSpec(memory_space=pltpu.HBM)] * 4, spec((1024, SIDE)), out((1024, SIDE)),
-        scratch=[pltpu.VMEM((4, ROWS, SIDE), BF16), pltpu.SemaphoreType.DMA((4,))], **kw,
-    )(*[in_hbm(x) for x in (query, key, value, grad)])
+        functools.partial(send_kernel, place), 1, [whole] * 5, [spec((1024, SIDE)), whole],
+        [out((1024, SIDE)), pltpu.HBM((32, HALF), BF16)],
+        scratch=[pltpu.VMEM((4, ROWS, SIDE), BF16), pltpu.VMEM((32, HALF), BF16), pltpu.SemaphoreType.DMA((6,))], **kw,
+    )(*[in_hbm(x) for x in (query, key, value, grad, jnp.asarray(feature_table()))])
 
 
 def run_filter(features, filter_in, filter_mid, filter_out, place=seq_place, **kw):
@@ -425,7 +425,7 @@
         [pltpu.HBM((256, HALF), BF16), pltpu.HBM((SIDE, HALF), F32), out((256, SIDE)), out((256, SIDE))],
         scratch=[pltpu.VMEM((512, SIDE), F32)],
         flops=4 * 10**9, nbytes=10 * MIB, **kw,
-    )(features, in_hbm(filter_in), in_hbm(filter_mid), in_hbm(filter_out))
+    )(in_hbm(features), in_hbm(filter_in), in_hbm(filter_mid), in_hbm(filter_out))
 
 
 def run_spectrum(mine, other, decay, place=seq_place, **kw):
@@ -466,15 +466,14 @@
 
 
 def run_backward(features, hidden, mine, other, sums, filter_mid, filter_out, place=seq_place, **kw):
-    wide = lambda i: (0, i)
-    deep = spec((BACK // 16, SIDE), lambda i: (i, 0))
+    held = pl.BlockSpec(memory_space=pltpu.VMEM)
     return call(
         functools.partial(backward_kernel, place),
-        HALF // BACK,
-        [spec((32, BACK), wide), spec((256, BACK), wide), spec((SIDE, BACK), wide), deep, deep, spec((16, SIDE)), spec((ORDER, ORDER)), spec((ORDER, SIDE))],
+        1,
+        [held] * 6 + [spec((ORDER, ORDER)), spec((ORDER, SIDE))],
         spec((112, SIDE)),
         out((112, SIDE)),
-        scratch=[pltpu.VMEM((384, 176), F32)] + [pltpu.VMEM((SIDE, BACK), BF16)] * 2,
+        scratch=[pltpu.VMEM((SIDE, HALF), BF16)] * 2 + [pltpu.VMEM((16, HALF), BF16)],
         flops=4 * 10**9, nbytes=10 * MIB, **kw,
     )(features, *hidden, mine, other, sums, in_hbm(filter_mid), in_hbm(filter_out))
 
@@ -506,10 +505,8 @@
 def body(query, key, value, grad, filter_in, filter_mid, filter_out, decay_rate, skip_gain):
     decay = decay_rate.reshape(1, SIDE)
     skip = skip_gain.reshape(1, SIDE)
-    core = lax.axis_index("core")
-    features = lax.dynamic_slice_in_dim(jnp.asarray(feature_table()), HALF * core, HALF, axis=1)
-    sent = run_send(query, key, value, grad).reshape(SEQ, SEQ, SIDE)
-    field = lax.all_to_all(sent, SEQ_AXES, 0, 0, tiled=True).reshape(1024, SIDE)
+    sent, features = run_send(query, key, value, grad)
+    field = lax.all_to_all(sent.reshape(SEQ, SEQ, SIDE), SEQ_AXES, 0, 0, tiled=True).reshape(1024, SIDE)
     *hidden, mine, theirs = run_filter(features, filter_in, filter_mid, filter_out)
     other = exchanged(theirs, "core", 1)
     spectrum = run_spectrum(mine, other, decay)

time: 70.9 us -> 69.8 us (0.984)
  starting transfers between devices: 33.4 us -> 32.3 us
  local copies, waits for them, and re-layouts: 1.17 us -> 0.09 us
  waiting for transfers between devices: 12 us -> 13 us
    all_to_all x1 -> x0, starting transfers between devices: 7.33 us -> none  [body(): field = lax.all_to_all(sent, SEQ_AXES, 0, 0, tiled=True).reshape(1024, SIDE)]
    all_to_all x1 -> x2, starting transfers between devices: 6.46 us -> 12.7 us  [body(): lax.all_to_all(sent.reshape(SEQ, SEQ, SIDE), SEQ_AXES, 0, 0, tiled=True)]
    all_to_all x1 -> x2, waiting for transfers between devices: 0.01 us -> 1.61 us  [body(): lax.all_to_all(sent.reshape(SEQ, SEQ, SIDE), SEQ_AXES, 0, 0, tiled=True)]
    dynamic_slice x1 -> x0, local copies, waits for them, and re-layouts: 1.08 us -> none  [body(): lax.dynamic_slice_in_dim(jnp.asarray(feature_table()), HALF * core, HALF,...]
  transfers between devices with their start and end apart: 15 -> 15, of which waited for: 9 -> 9; matrix products, arithmetic and copies ran while one was open for 2% -> 0% of each run, Pallas kernels for 18% -> 18%
where the time goes in v6:
time: 69.8 us; the launch traced here: 68.4 us
  starting transfers between devices  32.3 us (46%)
  Pallas kernels  22 us (32%)
  waiting for transfers between devices  13 us (19%)
  between operations  0.91 us (1%)
    ppermute x13, starting transfers between devices, exchanged(): lax.ppermute(x, axis, [(i, i ^ distance) for i in range(lax.axis_size(axi...  19.6 us
    all_to_all x2, starting transfers between devices, body(): lax.all_to_all(sent.reshape(SEQ, SEQ, SIDE), SEQ_AXES, 0, 0, tiled=True)  12.7 us
    ppermute x13, waiting for transfers between devices, exchanged(): lax.ppermute(x, axis, [(i, i ^ distance) for i in range(lax.axis_size(axi...  11.4 us
    pallas_call x1, Pallas kernels, run_filter(): call(functools.partial(filter_kernel, place), HALF // STEP, [spec((32, ST...  8.15 us
    pallas_call x1, Pallas kernels, run_backward(): call(functools.partial(backward_kernel, place), 1, [held] * 6 + [spec((OR...  4.08 us
    pallas_call x1, Pallas kernels, run_send(): call(functools.partial(send_kernel, place), 1, [whole] * 5, [spec((1024,...  2.99 us
    pallas_call x1, Pallas kernels, run_convolve(): call(convolve_kernel, 1, [spec((1024, 256)), spec((512, 256)), spec((SIDE...  2.11 us
    pallas_call x1, Pallas kernels, run_correlate(): call(functools.partial(correlate_kernel, place), 1, [spec((1024, SIDE)),...  2.01 us
  transfers between devices with their start and end apart: 15, of which 9 were waited for; matrix products, arithmetic and copies ran while one was open for 0% of the time, Pallas kernels for 18%

profile of v6, /device:TPU:32, one launch (start us, length us, event | category | flops | bytes accessed | tf_op | source)
XLA Modules:
  0.0 68.4 jit_solution(14354016746616918369)
XLA Ops:
  0.6 3.0 %shard_map.214 = (f32[1024,128]{1,0:T(8,128)}, bf16[32,8192]{1,0:T(8,128)(2,1)}) custom-call(bf16[512,128]{1,0:T(8,128)(2,1)} %query.3, bf16[512,128]{1,0:T(8,128)(2,1)} %key.3, bf16[512,128]{1,0:T(8,128)(2,1)} %value.3, bf16[512,128]{1,0:T(8,128)(2,1)} %grad.3, bf16[32,16384]{1,0:T(8,128)(2,1)} %constant.12.clone.table), custom_call_target="tpu_custom_call" | custom-call | flops 1 | bytes 1 | tf_op jit(solution)/shard_map/pallas_call | solution.py:411
  3.6 7.3 %all-to-all-start = ((f32[32,32,128]{2,1,0:T(8,128)}), f32[32,32,128]{2,1,0:T(8,128)S(1)}, u32[]{:S(2)}, u32[]{:S(2)}) async-start(f32[32,32,128]{2,1,0:T(8,128)} %bitcast), calls=%async_computation | async-start | bytes 1048576 | tf_op jit(solution)/shard_map/all_to_all | solution.py:509
  11.0 0.0 copy-start.6
  11.0 0.0 copy-start.7
  11.0 0.0 copy-start.8
  11.0 0.0 copy-start.9
  11.0 0.0 copy-start.10
  11.0 0.0 copy-start.11
  11.1 8.2 %shard_map.215 = (bf16[256,8192]{1,0:T(8,128)(2,1)}, f32[128,8192]{1,0:T(8,128)}, f32[256,128]{1,0:T(8,128)S(1)}, f32[256,128]{1,0:T(8,128)S(1)}) custom-call(bf16[32,8192]{1,0:T(8,128)(2,1)} %get-tuple-element.37.features, f32[16,64]{1,0:T(8,128)} %filter_in.1, f32[64,64]{1,0:T(8,128)} %filter_mid.3, f32[64,128]{1,0:T(8,128)} %filter_out.3), custom_call_target="tpu_custom_call" | custom-call | flops 4000000000 | bytes 10485760 | tf_op jit(solution)/shard_map/pallas_call | solution.py:420
  19.2 0.3 collective-permute-start
  19.5 1.1 %collective-permute-done.shaped_other.other = f32[256,128]{1,0:T(8,128)S(1)} collective-permute-done((f32[256,128]{1,0:T(8,128)S(1)}, f32[256,128]{1,0:T(8,128)S(1)}, u32[]{:S(2)}, u32[]{:S(2)}) %collective-permute-start) | collective-permute-done | bytes 131104 | tf_op jit(solution)/shard_map/ppermute | solution.py:495
  20.6 1.6 %all-to-all-done = f32[32,32,128]{2,1,0:T(8,128)S(1)} async-done(((f32[32,32,128]{2,1,0:T(8,128)}), f32[32,32,128]{2,1,0:T(8,128)S(1)}, u32[]{:S(2)}, u32[]{:S(2)}) %all-to-all-start) | async-done | bytes 524320 | tf_op jit(solution)/shard_map/all_to_all | solution.py:509
  22.2 0.0 copy-done.6
  22.2 0.0 copy-done.7
  22.2 0.0 copy-done.8
  22.2 0.0 copy-done.9
  22.2 0.0 copy-done.10
  22.2 0.0 copy-done.11
  22.2 0.0 copy-start.5
  22.2 0.0 copy-start.12
  22.2 0.0 copy-start.13
  22.2 2.0 %shard_map.216 = (f32[1024,256]{1,0:T(8,128)S(1)}, f32[512,128]{1,0:T(8,128)S(1)}, f32[512,128]{1,0:T(8,128)S(1)}, f32[16,128]{1,0:T(8,128)S(1)}) custom-call(f32[1024,128]{1,0:T(8,128)S(1)} %bitcast.9, f32[256,128]{1,0:T(8,128)S(1)} %get-tuple-element.41.shaped_mine.mine, f32[256,128]{1,0:T(8,128)S(1)} %collective-permute-done.shaped_other.other, ...), custom_call_target="tpu_custom_call" | custom-call | flops 2000000000 | bytes 4194304 | tf_op jit(solution)/shard_map/pallas_call | solution.py:445
  24.2 0.8 %collective-permute-start.1 = (f32[512,128]{1,0:T(8,128)S(1)}, f32[512,128]{1,0:T(8,128)S(1)}, u32[]{:S(2)}, u32[]{:S(2)}) collective-permute-start(f32[512,128]{1,0:T(8,128)S(1)} %get-tuple-element.45), channel_id=1, source_target_pairs={{0,8},{8,0},{1,9},{9,1},{2,10},{10,2},{3,11},{11,3},{4,12},{12,4},... | collective-permute-start | bytes 786440 | tf_op jit(solution)/shard_map/ppermute | solution.py:495
  25.0 0.8 %shard_map.217.spectrum = f32[512,256]{1,0:T(8,128)S(1)} custom-call(f32[256,128]{1,0:T(8,128)S(1)} %get-tuple-element.41.shaped_mine.mine, f32[256,128]{1,0:T(8,128)S(1)} %collective-permute-done.shaped_other.other, f32[1,128]{1,0:T(1,128)S(1)} %bitcast.12, bf16[256,384]{1,0:T(8,128)(2,1)S(1)} %copy-done.10, bf16[768,256]{1,0:T(8,128)(2,1)S(1)} %copy-done.8, ...), custom_call_target="tpu_custom_call" | custom-call | flops 1000000000 | bytes 1048576 | tf_op jit(solution)/shard_map/pallas_call | solution.py:433
  25.9 0.3 collective-permute-done.1.other
  26.2 0.0 copy-done.5
  26.2 0.0 copy-done.12
  26.2 0.0 copy-done.13
  26.2 4.1 %shard_map.218 = f32[112,128]{1,0:T(8,128)S(1)} custom-call(bf16[32,8192]{1,0:T(8,128)(2,1)S(1)} %copy-done.5, bf16[256,8192]{1,0:T(8,128)(2,1)S(1)} %copy-done.12, f32[128,8192]{1,0:T(8,128)S(1)} %copy-done.13, f32[512,128]{1,0:T(8,128)S(1)} %get-tuple-element.44.mine, f32[512,128]{1,0:T(8,128)S(1)} %collective-permute-done.1.other, ...), custom_call_target="tpu_custom_call" | custom-call | flops 4000000000 | bytes 10485760 | tf_op jit(solution)/shard_map/pallas_call | solution.py:470
  30.3 0.4 collective-permute-start.2
  30.7 0.9 %collective-permute-done.2 = f32[112,128]{1,0:T(8,128)S(1)} collective-permute-done((f32[112,128]{1,0:T(8,128)S(1)}, f32[112,128]{1,0:T(8,128)S(1)}, u32[]{:S(2)}, u32[]{:S(2)}) %collective-permute-start.2) | collective-permute-done | bytes 57376 | tf_op jit(solution)/shard_map/ppermute | solution.py:495
  31.6 0.0 copy-start
  31.7 0.0 copy-start.1
  31.7 0.0 copy-start.2
  31.7 0.0 copy-start.3
  31.7 0.0 copy-start.4
  31.7 3.4 %collective-permute-start.4 = (f32[40,128]{1,0:T(8,128)S(1)}, f32[40,128]{1,0:T(8,128)S(1)}, u32[]{:S(2)}, u32[]{:S(2)}) collective-permute-start(f32[40,128]{1,0:T(8,128)S(1)} %slice.8), channel_id=1, source_target_pairs={{0,2},{1,3},{2,0},{3,1},{4,6},{5,7},{6,4},{7,5},{8,10},{9,11},{10,... | collective-permute-start | bytes 61448 | tf_op jit(solution)/shard_map/ppermute | solution.py:495
  35.1 0.0 collective-permute-start.5
  35.1 1.6 %collective-permute-start.3 = (f32[40,128]{1,0:T(8,128)S(1)}, f32[40,128]{1,0:T(8,128)S(1)}, u32[]{:S(2)}, u32[]{:S(2)}) collective-permute-start(f32[40,128]{1,0:T(8,128)S(1)} %slice.8), channel_id=1, source_target_pairs={{0,1},{1,0},{2,3},{3,2},{4,5},{5,4},{6,7},{7,6},{8,9},{9,8},{10,11... | collective-permute-start | bytes 61448 | tf_op jit(solution)/shard_map/ppermute | solution.py:495
  36.7 2.1 %shard_map.219 = f32[1024,128]{1,0:T(8,128)} custom-call(f32[1024,256]{1,0:T(8,128)S(1)} %get-tuple-element.49.spectra, f32[512,256]{1,0:T(8,128)S(1)} %shard_map.217.spectrum, f32[128,256]{1,0:T(8,128)S(1)} %copy-done.11, bf16[768,256]{1,0:T(8,128)(2,1)S(1)} %copy-done.7, bf16[128,768]{1,0:T(8,128)(2,1)S(1)} %copy-done.9), custom_call_target="tpu_custom_call" | custom-call | flops 2000000000 | bytes 3145728 | tf_op jit(solution)/shard_map/pallas_call | solution.py:458
  38.8 5.4 %all-to-all-start.1 = ((f32[32,32,128]{2,1,0:T(8,128)}), f32[32,32,128]{2,1,0:T(8,128)S(1)}, u32[]{:S(2)}, u32[]{:S(2)}) async-start(f32[32,32,128]{2,1,0:T(8,128)} %bitcast.3), calls=%async_computation.1 | async-start | bytes 1048576 | tf_op jit(solution)/shard_map/all_to_all | solution.py:518
  44.2 0.0 collective-permute-done.4
  44.2 0.0 collective-permute-done.5
  44.2 0.0 collective-permute-done.3
  44.2 4.3 %collective-permute-start.6 = (f32[40,128]{1,0:T(8,128)S(1)}, f32[40,128]{1,0:T(8,128)S(1)}, u32[]{:S(2)}, u32[]{:S(2)}) collective-permute-start(f32[40,128]{1,0:T(8,128)S(1)} %add_add_fusion.2), channel_id=1, source_target_pairs={{0,6},{1,7},{2,4},{3,5},{4,2},{5,3},{6,0},{7,1},{8,14},{9,15},{10,... | collective-permute-start | bytes 61448 | tf_op jit(solution)/shard_map/ppermute | solution.py:495
  48.6 1.8 %collective-permute-done.6 = f32[40,128]{1,0:T(8,128)S(1)} collective-permute-done((f32[40,128]{1,0:T(8,128)S(1)}, f32[40,128]{1,0:T(8,128)S(1)}, u32[]{:S(2)}, u32[]{:S(2)}) %collective-permute-start.6) | collective-permute-done | bytes 20512 | tf_op jit(solution)/shard_map/ppermute | solution.py:495
  50.4 3.4 %collective-permute-start.8 = (f32[112,128]{1,0:T(8,128)S(1)}, f32[112,128]{1,0:T(8,128)S(1)}, u32[]{:S(2)}, u32[]{:S(2)}) collective-permute-start(f32[112,128]{1,0:T(8,128)S(1)} %pad_maximum_fusion), channel_id=1, source_target_pairs={{0,128},{64,192},{128,0},{192,64},{1,129},{65,193},{129,1},{193,65... | collective-permute-start | bytes 172040 | tf_op jit(solution)/shard_map/ppermute | solution.py:495
  53.8 1.2 %collective-permute-start.9 = (f32[112,128]{1,0:T(8,128)S(1)}, f32[112,128]{1,0:T(8,128)S(1)}, u32[]{:S(2)}, u32[]{:S(2)}) collective-permute-start(f32[112,128]{1,0:T(8,128)S(1)} %pad_maximum_fusion), channel_id=1, source_target_pairs={{0,192},{64,128},{128,64},{192,0},{1,193},{65,129},{129,65},{193,1... | collective-permute-start | bytes 172040 | tf_op jit(solution)/shard_map/ppermute | solution.py:495
  55.0 0.0 collective-permute-start.7
  55.0 1.2 %collective-permute-done.8 = f32[112,128]{1,0:T(8,128)S(1)} collective-permute-done((f32[112,128]{1,0:T(8,128)S(1)}, f32[112,128]{1,0:T(8,128)S(1)}, u32[]{:S(2)}, u32[]{:S(2)}) %collective-permute-start.8) | collective-permute-done | bytes 57376 | tf_op jit(solution)/shard_map/ppermute | solution.py:495
  56.2 3.0 %collective-permute-done.9 = f32[112,128]{1,0:T(8,128)S(1)} collective-permute-done((f32[112,128]{1,0:T(8,128)S(1)}, f32[112,128]{1,0:T(8,128)S(1)}, u32[]{:S(2)}, u32[]{:S(2)}) %collective-permute-start.9) | collective-permute-done | bytes 57376 | tf_op jit(solution)/shard_map/ppermute | solution.py:495
  59.2 0.0 collective-permute-done.7
  59.2 0.0 all-to-all-done.1
  59.2 3.1 %collective-permute-start.11 = (f32[112,128]{1,0:T(8,128)S(1)}, f32[112,128]{1,0:T(8,128)S(1)}, u32[]{:S(2)}, u32[]{:S(2)}) collective-permute-start(f32[112,128]{1,0:T(8,128)S(1)} %add_add_fusion.1), channel_id=1, source_target_pairs={{0,32},{16,48},{32,0},{48,16},{1,33},{17,49},{33,1},{49,17},{2,34}... | collective-permute-start | bytes 172040 | tf_op jit(solution)/shard_map/ppermute | solution.py:495
  62.3 1.2 %collective-permute-start.12 = (f32[112,128]{1,0:T(8,128)S(1)}, f32[112,128]{1,0:T(8,128)S(1)}, u32[]{:S(2)}, u32[]{:S(2)}) collective-permute-start(f32[112,128]{1,0:T(8,128)S(1)} %add_add_fusion.1), channel_id=1, source_target_pairs={{0,48},{16,32},{32,16},{48,0},{1,49},{17,33},{33,17},{49,1},{2,50}... | collective-permute-start | bytes 172040 | tf_op jit(solution)/shard_map/ppermute | solution.py:495
  63.4 0.0 collective-permute-start.10
  63.4 0.0 copy-done
  63.4 0.0 copy-done.1
  63.5 0.0 copy-done.2
  63.5 1.2 %shard_map.220 = (bf16[512,128]{1,0:T(8,128)(2,1)}, bf16[512,128]{1,0:T(8,128)(2,1)}, bf16[512,128]{1,0:T(8,128)(2,1)}, bf16[512,128]{1,0:T(8,128)(2,1)}) custom-call(bf16[512,128]{1,0:T(8,128)(2,1)S(1)} %copy-done, bf16[512,128]{1,0:T(8,128)(2,1)S(1)} %copy-done.1, bf16[512,128]{1,0:T(8,128)(2,1)S(1)} %copy-done.2, bf16[512,128]{1,0:T(8,128)(2,1)S(1)} %copy-done.3, ...), custom_call_target="tpu_custom_call" | custom-call | flops 1 | bytes 1 | tf_op jit(solution)/shard_map/pallas_call | solution.py:483
  64.6 0.6 collective-permute-done.11
  65.2 2.4 %collective-permute-done.12 = f32[112,128]{1,0:T(8,128)S(1)} collective-permute-done((f32[112,128]{1,0:T(8,128)S(1)}, f32[112,128]{1,0:T(8,128)S(1)}, u32[]{:S(2)}, u32[]{:S(2)}) %collective-permute-start.12) | collective-permute-done | bytes 57376 | tf_op jit(solution)/shard_map/ppermute | solution.py:495
  67.7 0.0 collective-permute-done.10
  67.7 0.7 %shard_map.221 = (f32[16,64]{1,0:T(8,128)}, f32[64,64]{1,0:T(8,128)}, f32[64,128]{1,0:T(8,128)}, f32[1,128]{1,0:T(1,128)}, f32[1,128]{1,0:T(1,128)}) custom-call(f32[112,128]{1,0:T(8,128)S(1)} %add_add_fusion.total), custom_call_target="tpu_custom_call" | custom-call | flops 1 | bytes 1 | tf_op jit(solution)/shard_map/pallas_call | solution.py:489
  (10 shorter events, 0.1 us)
Async XLA Ops:
  3.6 18.5 %all-to-all-start = ((f32[32,32,128]{2,1,0:T(8,128)}), f32[32,32,128]{2,1,0:T(8,128)S(1)}, u32[]{:S(2)}, u32[]{:S(2)}) async-start(f32[32,32,128]{2,1,0:T(8,128)} %bitcast), calls=%async_computation | async-start | bytes 1048576 | tf_op jit(solution)/shard_map/all_to_all | solution.py:509
  11.0 11.2 %copy-start.6 = (f32[128]{0:T(128)S(1)}, f32[128]{0:T(128)}, u32[]{:S(2)}) copy-start(f32[128]{0:T(128)} %param.22) | copy-start | bytes 1540
  11.0 11.2 %copy-start.7 = (bf16[768,256]{1,0:T(8,128)(2,1)S(1)}, bf16[768,256]{1,0:T(8,128)(2,1)}, u32[]{:S(2)}) copy-start(bf16[768,256]{1,0:T(8,128)(2,1)} %constant.16.clone.second_inv) | copy-start | bytes 1179652
  11.0 11.2 %copy-start.8 = (bf16[768,256]{1,0:T(8,128)(2,1)S(1)}, bf16[768,256]{1,0:T(8,128)(2,1)}, u32[]{:S(2)}) copy-start(bf16[768,256]{1,0:T(8,128)(2,1)} %constant.14.clone.second_fwd) | copy-start | bytes 1179652
  11.0 11.2 %copy-start.9 = (bf16[128,768]{1,0:T(8,128)(2,1)S(1)}, bf16[128,768]{1,0:T(8,128)(2,1)}, u32[]{:S(2)}) copy-start(bf16[128,768]{1,0:T(8,128)(2,1)} %constant.17.clone.first_inv) | copy-start | bytes 589828
  11.0 11.2 %copy-start.10 = (bf16[256,384]{1,0:T(8,128)(2,1)S(1)}, bf16[256,384]{1,0:T(8,128)(2,1)}, u32[]{:S(2)}) copy-start(bf16[256,384]{1,0:T(8,128)(2,1)} %constant.13.clone.first_fwd) | copy-start | bytes 589828
  11.0 11.2 %copy-start.11 = (f32[128,256]{1,0:T(8,128)S(1)}, f32[128,256]{1,0:T(8,128)}, u32[]{:S(2)}) copy-start(f32[128,256]{1,0:T(8,128)} %constant.15.clone.twiddle) | copy-start | bytes 393220
  19.2 1.3 %collective-permute-start = (f32[256,128]{1,0:T(8,128)S(1)}, f32[256,128]{1,0:T(8,128)S(1)}, u32[]{:S(2)}, u32[]{:S(2)}) collective-permute-start(f32[256,128]{1,0:T(8,128)S(1)} %get-tuple-element.42), channel_id=1, source_target_pairs={{0,8},{8,0},{1,9},{9,1},{2,10},{10,2},{3,11},{11,3},{4,12},{12,4},... | collective-permute-start | bytes 393224 | tf_op jit(solution)/shard_map/ppermute | solution.py:495
  22.2 4.0 %copy-start.5 = (bf16[32,8192]{1,0:T(8,128)(2,1)S(1)}, bf16[32,8192]{1,0:T(8,128)(2,1)}, u32[]{:S(2)}) copy-start(bf16[32,8192]{1,0:T(8,128)(2,1)} %get-tuple-element.37.features) | copy-start | bytes 1572868
  22.2 4.0 %copy-start.12 = (bf16[256,8192]{1,0:T(8,128)(2,1)S(1)}, bf16[256,8192]{1,0:T(8,128)(2,1)}, u32[]{:S(2)}) copy-start(bf16[256,8192]{1,0:T(8,128)(2,1)} %get-tuple-element.38.hidden) | copy-start | bytes 12582916
  22.2 4.0 %copy-start.13 = (f32[128,8192]{1,0:T(8,128)S(1)}, f32[128,8192]{1,0:T(8,128)}, u32[]{:S(2)}) copy-start(f32[128,8192]{1,0:T(8,128)} %get-tuple-element.39.cosines) | copy-start | bytes 12582916
  24.2 2.0 %collective-permute-start.1 = (f32[512,128]{1,0:T(8,128)S(1)}, f32[512,128]{1,0:T(8,128)S(1)}, u32[]{:S(2)}, u32[]{:S(2)}) collective-permute-start(f32[512,128]{1,0:T(8,128)S(1)} %get-tuple-element.45), channel_id=1, source_target_pairs={{0,8},{8,0},{1,9},{9,1},{2,10},{10,2},{3,11},{11,3},{4,12},{12,4},... | collective-permute-start | bytes 786440 | tf_op jit(solution)/shard_map/ppermute | solution.py:495
  30.3 1.3 %collective-permute-start.2 = (f32[112,128]{1,0:T(8,128)S(1)}, f32[112,128]{1,0:T(8,128)S(1)}, u32[]{:S(2)}, u32[]{:S(2)}) collective-permute-start(f32[112,128]{1,0:T(8,128)S(1)} %shard_map.218), channel_id=1, source_target_pairs={{0,8},{8,0},{1,9},{9,1},{2,10},{10,2},{3,11},{11,3},{4,12},{12,4},... | collective-permute-start | bytes 172040 | tf_op jit(solution)/shard_map/ppermute | solution.py:495
  31.6 31.8 %copy-start = (bf16[512,128]{1,0:T(8,128)(2,1)S(1)}, bf16[512,128]{1,0:T(8,128)(2,1)}, u32[]{:S(2)}) copy-start(bf16[512,128]{1,0:T(8,128)(2,1)} %query.3) | copy-start | bytes 393220
  31.7 31.8 %copy-start.1 = (bf16[512,128]{1,0:T(8,128)(2,1)S(1)}, bf16[512,128]{1,0:T(8,128)(2,1)}, u32[]{:S(2)}) copy-start(bf16[512,128]{1,0:T(8,128)(2,1)} %key.3) | copy-start | bytes 393220
  31.7 31.8 %copy-start.2 = (bf16[512,128]{1,0:T(8,128)(2,1)S(1)}, bf16[512,128]{1,0:T(8,128)(2,1)}, u32[]{:S(2)}) copy-start(bf16[512,128]{1,0:T(8,128)(2,1)} %value.3) | copy-start | bytes 393220
  31.7 31.8 %copy-start.3 = (bf16[512,128]{1,0:T(8,128)(2,1)S(1)}, bf16[512,128]{1,0:T(8,128)(2,1)}, u32[]{:S(2)}) copy-start(bf16[512,128]{1,0:T(8,128)(2,1)} %grad.3) | copy-start | bytes 393220
  31.7 31.8 %copy-start.4 = (f32[128]{0:T(128)S(1)}, f32[128]{0:T(128)}, u32[]{:S(2)}) copy-start(f32[128]{0:T(128)} %param.23) | copy-start | bytes 1540
  31.7 12.5 %collective-permute-start.4 = (f32[40,128]{1,0:T(8,128)S(1)}, f32[40,128]{1,0:T(8,128)S(1)}, u32[]{:S(2)}, u32[]{:S(2)}) collective-permute-start(f32[40,128]{1,0:T(8,128)S(1)} %slice.8), channel_id=1, source_target_pairs={{0,2},{1,3},{2,0},{3,1},{4,6},{5,7},{6,4},{7,5},{8,10},{9,11},{10,... | collective-permute-start | bytes 61448 | tf_op jit(solution)/shard_map/ppermute | solution.py:495
  35.1 9.1 %collective-permute-start.5 = (f32[40,128]{1,0:T(8,128)S(1)}, f32[40,128]{1,0:T(8,128)S(1)}, u32[]{:S(2)}, u32[]{:S(2)}) collective-permute-start(f32[40,128]{1,0:T(8,128)S(1)} %slice.8), channel_id=1, source_target_pairs={{0,3},{1,2},{2,1},{3,0},{4,7},{5,6},{6,5},{7,4},{8,11},{9,10},{10,... | collective-permute-start | bytes 61448 | tf_op jit(solution)/shard_map/ppermute | solution.py:495
  35.1 9.1 %collective-permute-start.3 = (f32[40,128]{1,0:T(8,128)S(1)}, f32[40,128]{1,0:T(8,128)S(1)}, u32[]{:S(2)}, u32[]{:S(2)}) collective-permute-start(f32[40,128]{1,0:T(8,128)S(1)} %slice.8), channel_id=1, source_target_pairs={{0,1},{1,0},{2,3},{3,2},{4,5},{5,4},{6,7},{7,6},{8,9},{9,8},{10,11... | collective-permute-start | bytes 61448 | tf_op jit(solution)/shard_map/ppermute | solution.py:495
  38.8 20.4 %all-to-all-start.1 = ((f32[32,32,128]{2,1,0:T(8,128)}), f32[32,32,128]{2,1,0:T(8,128)S(1)}, u32[]{:S(2)}, u32[]{:S(2)}) async-start(f32[32,32,128]{2,1,0:T(8,128)} %bitcast.3), calls=%async_computation.1 | async-start | bytes 1048576 | tf_op jit(solution)/shard_map/all_to_all | solution.py:518
  44.2 6.2 %collective-permute-start.6 = (f32[40,128]{1,0:T(8,128)S(1)}, f32[40,128]{1,0:T(8,128)S(1)}, u32[]{:S(2)}, u32[]{:S(2)}) collective-permute-start(f32[40,128]{1,0:T(8,128)S(1)} %add_add_fusion.2), channel_id=1, source_target_pairs={{0,6},{1,7},{2,4},{3,5},{4,2},{5,3},{6,0},{7,1},{8,14},{9,15},{10,... | collective-permute-start | bytes 61448 | tf_op jit(solution)/shard_map/ppermute | solution.py:495
  50.4 5.8 %collective-permute-start.8 = (f32[112,128]{1,0:T(8,128)S(1)}, f32[112,128]{1,0:T(8,128)S(1)}, u32[]{:S(2)}, u32[]{:S(2)}) collective-permute-start(f32[112,128]{1,0:T(8,128)S(1)} %pad_maximum_fusion), channel_id=1, source_target_pairs={{0,128},{64,192},{128,0},{192,64},{1,129},{65,193},{129,1},{193,65... | collective-permute-start | bytes 172040 | tf_op jit(solution)/shard_map/ppermute | solution.py:495
  53.8 5.4 %collective-permute-start.9 = (f32[112,128]{1,0:T(8,128)S(1)}, f32[112,128]{1,0:T(8,128)S(1)}, u32[]{:S(2)}, u32[]{:S(2)}) collective-permute-start(f32[112,128]{1,0:T(8,128)S(1)} %pad_maximum_fusion), channel_id=1, source_target_pairs={{0,192},{64,128},{128,64},{192,0},{1,193},{65,129},{129,65},{193,1... | collective-permute-start | bytes 172040 | tf_op jit(solution)/shard_map/ppermute | solution.py:495
  55.0 4.2 %collective-permute-start.7 = (f32[112,128]{1,0:T(8,128)S(1)}, f32[112,128]{1,0:T(8,128)S(1)}, u32[]{:S(2)}, u32[]{:S(2)}) collective-permute-start(f32[112,128]{1,0:T(8,128)S(1)} %pad_maximum_fusion), channel_id=1, source_target_pairs={{0,64},{64,0},{128,192},{192,128},{1,65},{65,1},{129,193},{193,129... | collective-permute-start | bytes 172040 | tf_op jit(solution)/shard_map/ppermute | solution.py:495
  59.2 6.0 %collective-permute-start.11 = (f32[112,128]{1,0:T(8,128)S(1)}, f32[112,128]{1,0:T(8,128)S(1)}, u32[]{:S(2)}, u32[]{:S(2)}) collective-permute-start(f32[112,128]{1,0:T(8,128)S(1)} %add_add_fusion.1), channel_id=1, source_target_pairs={{0,32},{16,48},{32,0},{48,16},{1,33},{17,49},{33,1},{49,17},{2,34}... | collective-permute-start | bytes 172040 | tf_op jit(solution)/shard_map/ppermute | solution.py:495
  62.3 5.4 %collective-permute-start.12 = (f32[112,128]{1,0:T(8,128)S(1)}, f32[112,128]{1,0:T(8,128)S(1)}, u32[]{:S(2)}, u32[]{:S(2)}) collective-permute-start(f32[112,128]{1,0:T(8,128)S(1)} %add_add_fusion.1), channel_id=1, source_target_pairs={{0,48},{16,32},{32,16},{48,0},{1,49},{17,33},{33,17},{49,1},{2,50}... | collective-permute-start | bytes 172040 | tf_op jit(solution)/shard_map/ppermute | solution.py:495
  63.4 4.2 %collective-permute-start.10 = (f32[112,128]{1,0:T(8,128)S(1)}, f32[112,128]{1,0:T(8,128)S(1)}, u32[]{:S(2)}, u32[]{:S(2)}) collective-permute-start(f32[112,128]{1,0:T(8,128)S(1)} %add_add_fusion.1), channel_id=1, source_target_pairs={{0,16},{16,0},{32,48},{48,32},{1,17},{17,1},{33,49},{49,33},{2,18}... | collective-permute-start | bytes 172040 | tf_op jit(solution)/shard_map/ppermute | solution.py:495

commit v7 on v6

--- a/solution.py
+++ b/solution.py
@@ -515,10 +515,11 @@
     grads = run_backward(features, hidden, mine, exchanged(theirs, "core", 1), sums, filter_mid, filter_out)
     grads, spectra = lax.optimization_barrier((grads, spectra))
     sent = run_convolve(spectra, spectrum)
+    other = exchanged(grads, "core", 1)
+    other, sent = lax.optimization_barrier((other, sent))
+    grads = grads + other
     field = lax.all_to_all(sent.reshape(SEQ, SEQ, SIDE), SEQ_AXES, 0, 0, tiled=True).reshape(1024, SIDE)
-    grads = group_sum(grads, "core", (1,))
     shared = group_sum(grads[:40], "chan", (1, 2, 3))
-    shared, sent = lax.optimization_barrier((shared, sent))
     shared = group_sum(shared, "chan", (6,))
     grads = jnp.concatenate([shared, grads[40:]])
     grads = group_sum(grads, "x", (1, 2, 3))

time: 69.8 us -> 68.7 us (0.984)
  waiting for transfers between devices: 13 us -> 12.1 us
    ppermute x13, waiting for transfers between devices: 11.4 us -> 10.5 us  [exchanged(): lax.ppermute(x, axis, [(i, i ^ distance) for i in range(lax.axis_size(axi...]
  transfers between devices with their start and end apart: 15 -> 15, of which waited for: 9 -> 8; matrix products, arithmetic and copies ran while one was open for 0% -> 0% of each run, Pallas kernels for 18% -> 18%
where the time goes in v7:
time: 68.7 us; the launch traced here: 67.3 us
  starting transfers between devices  32.1 us (47%)
  Pallas kernels  22 us (32%)
  waiting for transfers between devices  12.1 us (18%)
  between operations  0.91 us (1%)
    ppermute x13, starting transfers between devices, exchanged(): lax.ppermute(x, axis, [(i, i ^ distance) for i in range(lax.axis_size(axi...  19.6 us
    all_to_all x2, starting transfers between devices, body(): lax.all_to_all(sent.reshape(SEQ, SEQ, SIDE), SEQ_AXES, 0, 0, tiled=True)  12.6 us
    ppermute x13, waiting for transfers between devices, exchanged(): lax.ppermute(x, axis, [(i, i ^ distance) for i in range(lax.axis_size(axi...  10.5 us
    pallas_call x1, Pallas kernels, run_filter(): call(functools.partial(filter_kernel, place), HALF // STEP, [spec((32, ST...  8.15 us
    pallas_call x1, Pallas kernels, run_backward(): call(functools.partial(backward_kernel, place), 1, [held] * 6 + [spec((OR...  4.08 us
    pallas_call x1, Pallas kernels, run_send(): call(functools.partial(send_kernel, place), 1, [whole] * 5, [spec((1024,...  2.99 us
    pallas_call x1, Pallas kernels, run_convolve(): call(convolve_kernel, 1, [spec((1024, 256)), spec((512, 256)), spec((SIDE...  2.11 us
    pallas_call x1, Pallas kernels, run_correlate(): call(functools.partial(correlate_kernel, place), 1, [spec((1024, SIDE)),...  2.01 us
  transfers between devices with their start and end apart: 15, of which 8 were waited for; matrix products, arithmetic and copies ran while one was open for 0% of the time, Pallas kernels for 18%

profile of v7, /device:TPU:32, one launch (start us, length us, event | category | flops | bytes accessed | tf_op | source)
XLA Modules:
  0.0 67.3 jit_solution(8499105227313593362)
XLA Ops:
  0.6 3.0 %shard_map.214 = (f32[1024,128]{1,0:T(8,128)}, bf16[32,8192]{1,0:T(8,128)(2,1)}) custom-call(bf16[512,128]{1,0:T(8,128)(2,1)} %query.3, bf16[512,128]{1,0:T(8,128)(2,1)} %key.3, bf16[512,128]{1,0:T(8,128)(2,1)} %value.3, bf16[512,128]{1,0:T(8,128)(2,1)} %grad.3, bf16[32,16384]{1,0:T(8,128)(2,1)} %constant.12.clone.table), custom_call_target="tpu_custom_call" | custom-call | flops 1 | bytes 1 | tf_op jit(solution)/shard_map/pallas_call | solution.py:411
  3.6 7.3 %all-to-all-start = ((f32[32,32,128]{2,1,0:T(8,128)}), f32[32,32,128]{2,1,0:T(8,128)S(1)}, u32[]{:S(2)}, u32[]{:S(2)}) async-start(f32[32,32,128]{2,1,0:T(8,128)} %bitcast), calls=%async_computation | async-start | bytes 1048576 | tf_op jit(solution)/shard_map/all_to_all | solution.py:509
  11.0 0.0 copy-start.6
  11.0 0.0 copy-start.7
  11.0 0.0 copy-start.8
  11.0 0.0 copy-start.9
  11.0 0.0 copy-start.10
  11.0 0.0 copy-start.11
  11.1 8.2 %shard_map.215 = (bf16[256,8192]{1,0:T(8,128)(2,1)}, f32[128,8192]{1,0:T(8,128)}, f32[256,128]{1,0:T(8,128)S(1)}, f32[256,128]{1,0:T(8,128)S(1)}) custom-call(bf16[32,8192]{1,0:T(8,128)(2,1)} %get-tuple-element.38.features, f32[16,64]{1,0:T(8,128)} %filter_in.1, f32[64,64]{1,0:T(8,128)} %filter_mid.3, f32[64,128]{1,0:T(8,128)} %filter_out.3), custom_call_target="tpu_custom_call" | custom-call | flops 4000000000 | bytes 10485760 | tf_op jit(solution)/shard_map/pallas_call | solution.py:420
  19.2 0.3 collective-permute-start
  19.5 1.1 %collective-permute-done.shaped_other.other = f32[256,128]{1,0:T(8,128)S(1)} collective-permute-done((f32[256,128]{1,0:T(8,128)S(1)}, f32[256,128]{1,0:T(8,128)S(1)}, u32[]{:S(2)}, u32[]{:S(2)}) %collective-permute-start) | collective-permute-done | bytes 131104 | tf_op jit(solution)/shard_map/ppermute | solution.py:495
  20.6 1.6 %all-to-all-done = f32[32,32,128]{2,1,0:T(8,128)S(1)} async-done(((f32[32,32,128]{2,1,0:T(8,128)}), f32[32,32,128]{2,1,0:T(8,128)S(1)}, u32[]{:S(2)}, u32[]{:S(2)}) %all-to-all-start) | async-done | bytes 524320 | tf_op jit(solution)/shard_map/all_to_all | solution.py:509
  22.2 0.0 copy-done.6
  22.2 0.0 copy-done.7
  22.2 0.0 copy-done.8
  22.2 0.0 copy-done.9
  22.2 0.0 copy-done.10
  22.2 0.0 copy-done.11
  22.2 0.0 copy-start.5
  22.2 0.0 copy-start.12
  22.2 0.0 copy-start.13
  22.2 2.0 %shard_map.216 = (f32[1024,256]{1,0:T(8,128)S(1)}, f32[512,128]{1,0:T(8,128)S(1)}, f32[512,128]{1,0:T(8,128)S(1)}, f32[16,128]{1,0:T(8,128)S(1)}) custom-call(f32[1024,128]{1,0:T(8,128)S(1)} %bitcast.9, f32[256,128]{1,0:T(8,128)S(1)} %get-tuple-element.42.shaped_mine.mine, f32[256,128]{1,0:T(8,128)S(1)} %collective-permute-done.shaped_other.other, ...), custom_call_target="tpu_custom_call" | custom-call | flops 2000000000 | bytes 4194304 | tf_op jit(solution)/shard_map/pallas_call | solution.py:445
  24.2 0.8 %collective-permute-start.1 = (f32[512,128]{1,0:T(8,128)S(1)}, f32[512,128]{1,0:T(8,128)S(1)}, u32[]{:S(2)}, u32[]{:S(2)}) collective-permute-start(f32[512,128]{1,0:T(8,128)S(1)} %get-tuple-element.46), channel_id=1, source_target_pairs={{0,8},{8,0},{1,9},{9,1},{2,10},{10,2},{3,11},{11,3},{4,12},{12,4},... | collective-permute-start | bytes 786440 | tf_op jit(solution)/shard_map/ppermute | solution.py:495
  25.0 0.8 %shard_map.217.spectrum = f32[512,256]{1,0:T(8,128)S(1)} custom-call(f32[256,128]{1,0:T(8,128)S(1)} %get-tuple-element.42.shaped_mine.mine, f32[256,128]{1,0:T(8,128)S(1)} %collective-permute-done.shaped_other.other, f32[1,128]{1,0:T(1,128)S(1)} %bitcast.12, bf16[256,384]{1,0:T(8,128)(2,1)S(1)} %copy-done.10, bf16[768,256]{1,0:T(8,128)(2,1)S(1)} %copy-done.8, ...), custom_call_target="tpu_custom_call" | custom-call | flops 1000000000 | bytes 1048576 | tf_op jit(solution)/shard_map/pallas_call | solution.py:433
  25.9 0.3 collective-permute-done.1.other
  26.2 0.0 copy-done.5
  26.2 0.0 copy-done.12
  26.2 0.0 copy-done.13
  26.2 4.1 %shard_map.218 = f32[112,128]{1,0:T(8,128)S(1)} custom-call(bf16[32,8192]{1,0:T(8,128)(2,1)S(1)} %copy-done.5, bf16[256,8192]{1,0:T(8,128)(2,1)S(1)} %copy-done.12, f32[128,8192]{1,0:T(8,128)S(1)} %copy-done.13, f32[512,128]{1,0:T(8,128)S(1)} %get-tuple-element.45.mine, f32[512,128]{1,0:T(8,128)S(1)} %collective-permute-done.1.other, ...), custom_call_target="tpu_custom_call" | custom-call | flops 4000000000 | bytes 10485760 | tf_op jit(solution)/shard_map/pallas_call | solution.py:470
  30.3 0.0 copy-start.2
  30.3 0.0 copy-start.3
  30.3 0.0 copy-start.4
  30.3 0.5 collective-permute-start.2
  30.8 2.1 %shard_map.219 = f32[1024,128]{1,0:T(8,128)} custom-call(f32[1024,256]{1,0:T(8,128)S(1)} %get-tuple-element.50.spectra, f32[512,256]{1,0:T(8,128)S(1)} %shard_map.217.spectrum, f32[128,256]{1,0:T(8,128)S(1)} %copy-done.11, bf16[768,256]{1,0:T(8,128)(2,1)S(1)} %copy-done.7, bf16[128,768]{1,0:T(8,128)(2,1)S(1)} %copy-done.9), custom_call_target="tpu_custom_call" | custom-call | flops 2000000000 | bytes 3145728 | tf_op jit(solution)/shard_map/pallas_call | solution.py:458
  32.9 0.0 collective-permute-done.2
  32.9 3.4 %collective-permute-start.4 = (f32[40,128]{1,0:T(8,128)S(1)}, f32[40,128]{1,0:T(8,128)S(1)}, u32[]{:S(2)}, u32[]{:S(2)}) collective-permute-start(f32[40,128]{1,0:T(8,128)S(1)} %slice.8), channel_id=1, source_target_pairs={{0,2},{1,3},{2,0},{3,1},{4,6},{5,7},{6,4},{7,5},{8,10},{9,11},{10,... | collective-permute-start | bytes 61448 | tf_op jit(solution)/shard_map/ppermute | solution.py:495
  36.3 0.0 collective-permute-start.5
  36.3 1.6 %collective-permute-start.3 = (f32[40,128]{1,0:T(8,128)S(1)}, f32[40,128]{1,0:T(8,128)S(1)}, u32[]{:S(2)}, u32[]{:S(2)}) collective-permute-start(f32[40,128]{1,0:T(8,128)S(1)} %slice.8), channel_id=1, source_target_pairs={{0,1},{1,0},{2,3},{3,2},{4,5},{5,4},{6,7},{7,6},{8,9},{9,8},{10,11... | collective-permute-start | bytes 61448 | tf_op jit(solution)/shard_map/ppermute | solution.py:495
  37.9 5.2 %all-to-all-start.1 = ((f32[32,32,128]{2,1,0:T(8,128)}), f32[32,32,128]{2,1,0:T(8,128)S(1)}, u32[]{:S(2)}, u32[]{:S(2)}) async-start(f32[32,32,128]{2,1,0:T(8,128)} %bitcast.3), calls=%async_computation.1 | async-start | bytes 1048576 | tf_op jit(solution)/shard_map/all_to_all | solution.py:521
  43.1 0.0 collective-permute-done.4
  43.1 0.0 collective-permute-done.5
  43.1 0.0 collective-permute-done.3
  43.2 4.3 %collective-permute-start.6 = (f32[40,128]{1,0:T(8,128)S(1)}, f32[40,128]{1,0:T(8,128)S(1)}, u32[]{:S(2)}, u32[]{:S(2)}) collective-permute-start(f32[40,128]{1,0:T(8,128)S(1)} %add_add_fusion.2), channel_id=1, source_target_pairs={{0,6},{1,7},{2,4},{3,5},{4,2},{5,3},{6,0},{7,1},{8,14},{9,15},{10,... | collective-permute-start | bytes 61448 | tf_op jit(solution)/shard_map/ppermute | solution.py:495
  47.5 1.8 %collective-permute-done.6 = f32[40,128]{1,0:T(8,128)S(1)} collective-permute-done((f32[40,128]{1,0:T(8,128)S(1)}, f32[40,128]{1,0:T(8,128)S(1)}, u32[]{:S(2)}, u32[]{:S(2)}) %collective-permute-start.6) | collective-permute-done | bytes 20512 | tf_op jit(solution)/shard_map/ppermute | solution.py:495
  49.3 3.4 %collective-permute-start.8 = (f32[112,128]{1,0:T(8,128)S(1)}, f32[112,128]{1,0:T(8,128)S(1)}, u32[]{:S(2)}, u32[]{:S(2)}) collective-permute-start(f32[112,128]{1,0:T(8,128)S(1)} %pad_maximum_fusion), channel_id=1, source_target_pairs={{0,128},{64,192},{128,0},{192,64},{1,129},{65,193},{129,1},{193,65... | collective-permute-start | bytes 172040 | tf_op jit(solution)/shard_map/ppermute | solution.py:495
  52.7 1.2 %collective-permute-start.9 = (f32[112,128]{1,0:T(8,128)S(1)}, f32[112,128]{1,0:T(8,128)S(1)}, u32[]{:S(2)}, u32[]{:S(2)}) collective-permute-start(f32[112,128]{1,0:T(8,128)S(1)} %pad_maximum_fusion), channel_id=1, source_target_pairs={{0,192},{64,128},{128,64},{192,0},{1,193},{65,129},{129,65},{193,1... | collective-permute-start | bytes 172040 | tf_op jit(solution)/shard_map/ppermute | solution.py:495
  53.9 0.0 collective-permute-start.7
  53.9 1.2 %collective-permute-done.8 = f32[112,128]{1,0:T(8,128)S(1)} collective-permute-done((f32[112,128]{1,0:T(8,128)S(1)}, f32[112,128]{1,0:T(8,128)S(1)}, u32[]{:S(2)}, u32[]{:S(2)}) %collective-permute-start.8) | collective-permute-done | bytes 57376 | tf_op jit(solution)/shard_map/ppermute | solution.py:495
  55.1 3.0 %collective-permute-done.9 = f32[112,128]{1,0:T(8,128)S(1)} collective-permute-done((f32[112,128]{1,0:T(8,128)S(1)}, f32[112,128]{1,0:T(8,128)S(1)}, u32[]{:S(2)}, u32[]{:S(2)}) %collective-permute-start.9) | collective-permute-done | bytes 57376 | tf_op jit(solution)/shard_map/ppermute | solution.py:495
  58.1 0.0 collective-permute-done.7
  58.1 0.0 all-to-all-done.1
  58.1 3.1 %collective-permute-start.11 = (f32[112,128]{1,0:T(8,128)S(1)}, f32[112,128]{1,0:T(8,128)S(1)}, u32[]{:S(2)}, u32[]{:S(2)}) collective-permute-start(f32[112,128]{1,0:T(8,128)S(1)} %add_add_fusion.1), channel_id=1, source_target_pairs={{0,32},{16,48},{32,0},{48,16},{1,33},{17,49},{33,1},{49,17},{2,34}... | collective-permute-start | bytes 172040 | tf_op jit(solution)/shard_map/ppermute | solution.py:495
  61.2 1.2 %collective-permute-start.12 = (f32[112,128]{1,0:T(8,128)S(1)}, f32[112,128]{1,0:T(8,128)S(1)}, u32[]{:S(2)}, u32[]{:S(2)}) collective-permute-start(f32[112,128]{1,0:T(8,128)S(1)} %add_add_fusion.1), channel_id=1, source_target_pairs={{0,48},{16,32},{32,16},{48,0},{1,49},{17,33},{33,17},{49,1},{2,50}... | collective-permute-start | bytes 172040 | tf_op jit(solution)/shard_map/ppermute | solution.py:495
  62.4 0.0 collective-permute-start.10
  62.4 0.0 copy-done
  62.4 0.0 copy-done.1
  62.4 0.0 copy-done.2
  62.4 0.0 copy-done.3
  62.4 0.0 copy-done.4
  62.4 1.2 %shard_map.220 = (bf16[512,128]{1,0:T(8,128)(2,1)}, bf16[512,128]{1,0:T(8,128)(2,1)}, bf16[512,128]{1,0:T(8,128)(2,1)}, bf16[512,128]{1,0:T(8,128)(2,1)}) custom-call(bf16[512,128]{1,0:T(8,128)(2,1)S(1)} %copy-done, bf16[512,128]{1,0:T(8,128)(2,1)S(1)} %copy-done.1, bf16[512,128]{1,0:T(8,128)(2,1)S(1)} %copy-done.2, bf16[512,128]{1,0:T(8,128)(2,1)S(1)} %copy-done.3, ...), custom_call_target="tpu_custom_call" | custom-call | flops 1 | bytes 1 | tf_op jit(solution)/shard_map/pallas_call | solution.py:483
  63.6 0.6 collective-permute-done.11
  64.2 2.4 %collective-permute-done.12 = f32[112,128]{1,0:T(8,128)S(1)} collective-permute-done((f32[112,128]{1,0:T(8,128)S(1)}, f32[112,128]{1,0:T(8,128)S(1)}, u32[]{:S(2)}, u32[]{:S(2)}) %collective-permute-start.12) | collective-permute-done | bytes 57376 | tf_op jit(solution)/shard_map/ppermute | solution.py:495
  66.6 0.0 collective-permute-done.10
  66.6 0.7 %shard_map.221 = (f32[16,64]{1,0:T(8,128)}, f32[64,64]{1,0:T(8,128)}, f32[64,128]{1,0:T(8,128)}, f32[1,128]{1,0:T(1,128)}, f32[1,128]{1,0:T(1,128)}) custom-call(f32[112,128]{1,0:T(8,128)S(1)} %add_add_fusion.total), custom_call_target="tpu_custom_call" | custom-call | flops 1 | bytes 1 | tf_op jit(solution)/shard_map/pallas_call | solution.py:489
  (10 shorter events, 0.1 us)
Async XLA Ops:
  3.6 18.5 %all-to-all-start = ((f32[32,32,128]{2,1,0:T(8,128)}), f32[32,32,128]{2,1,0:T(8,128)S(1)}, u32[]{:S(2)}, u32[]{:S(2)}) async-start(f32[32,32,128]{2,1,0:T(8,128)} %bitcast), calls=%async_computation | async-start | bytes 1048576 | tf_op jit(solution)/shard_map/all_to_all | solution.py:509
  11.0 11.2 %copy-start.6 = (f32[128]{0:T(128)S(1)}, f32[128]{0:T(128)}, u32[]{:S(2)}) copy-start(f32[128]{0:T(128)} %param.22) | copy-start | bytes 1540
  11.0 11.2 %copy-start.7 = (bf16[768,256]{1,0:T(8,128)(2,1)S(1)}, bf16[768,256]{1,0:T(8,128)(2,1)}, u32[]{:S(2)}) copy-start(bf16[768,256]{1,0:T(8,128)(2,1)} %constant.16.clone.second_inv) | copy-start | bytes 1179652
  11.0 11.2 %copy-start.8 = (bf16[768,256]{1,0:T(8,128)(2,1)S(1)}, bf16[768,256]{1,0:T(8,128)(2,1)}, u32[]{:S(2)}) copy-start(bf16[768,256]{1,0:T(8,128)(2,1)} %constant.14.clone.second_fwd) | copy-start | bytes 1179652
  11.0 11.2 %copy-start.9 = (bf16[128,768]{1,0:T(8,128)(2,1)S(1)}, bf16[128,768]{1,0:T(8,128)(2,1)}, u32[]{:S(2)}) copy-start(bf16[128,768]{1,0:T(8,128)(2,1)} %constant.17.clone.first_inv) | copy-start | bytes 589828
  11.0 11.2 %copy-start.10 = (bf16[256,384]{1,0:T(8,128)(2,1)S(1)}, bf16[256,384]{1,0:T(8,128)(2,1)}, u32[]{:S(2)}) copy-start(bf16[256,384]{1,0:T(8,128)(2,1)} %constant.13.clone.first_fwd) | copy-start | bytes 589828
  11.0 11.2 %copy-start.11 = (f32[128,256]{1,0:T(8,128)S(1)}, f32[128,256]{1,0:T(8,128)}, u32[]{:S(2)}) copy-start(f32[128,256]{1,0:T(8,128)} %constant.15.clone.twiddle) | copy-start | bytes 393220
  19.2 1.3 %collective-permute-start = (f32[256,128]{1,0:T(8,128)S(1)}, f32[256,128]{1,0:T(8,128)S(1)}, u32[]{:S(2)}, u32[]{:S(2)}) collective-permute-start(f32[256,128]{1,0:T(8,128)S(1)} %get-tuple-element.43), channel_id=1, source_target_pairs={{0,8},{8,0},{1,9},{9,1},{2,10},{10,2},{3,11},{11,3},{4,12},{12,4},... | collective-permute-start | bytes 393224 | tf_op jit(solution)/shard_map/ppermute | solution.py:495
  22.2 4.0 %copy-start.5 = (bf16[32,8192]{1,0:T(8,128)(2,1)S(1)}, bf16[32,8192]{1,0:T(8,128)(2,1)}, u32[]{:S(2)}) copy-start(bf16[32,8192]{1,0:T(8,128)(2,1)} %get-tuple-element.38.features) | copy-start | bytes 1572868
  22.2 4.0 %copy-start.12 = (bf16[256,8192]{1,0:T(8,128)(2,1)S(1)}, bf16[256,8192]{1,0:T(8,128)(2,1)}, u32[]{:S(2)}) copy-start(bf16[256,8192]{1,0:T(8,128)(2,1)} %get-tuple-element.39.hidden) | copy-start | bytes 12582916
  22.2 4.0 %copy-start.13 = (f32[128,8192]{1,0:T(8,128)S(1)}, f32[128,8192]{1,0:T(8,128)}, u32[]{:S(2)}) copy-start(f32[128,8192]{1,0:T(8,128)} %get-tuple-element.40.cosines) | copy-start | bytes 12582916
  24.2 2.0 %collective-permute-start.1 = (f32[512,128]{1,0:T(8,128)S(1)}, f32[512,128]{1,0:T(8,128)S(1)}, u32[]{:S(2)}, u32[]{:S(2)}) collective-permute-start(f32[512,128]{1,0:T(8,128)S(1)} %get-tuple-element.46), channel_id=1, source_target_pairs={{0,8},{8,0},{1,9},{9,1},{2,10},{10,2},{3,11},{11,3},{4,12},{12,4},... | collective-permute-start | bytes 786440 | tf_op jit(solution)/shard_map/ppermute | solution.py:495
  30.3 32.1 %copy-start = (bf16[512,128]{1,0:T(8,128)(2,1)S(1)}, bf16[512,128]{1,0:T(8,128)(2,1)}, u32[]{:S(2)}) copy-start(bf16[512,128]{1,0:T(8,128)(2,1)} %query.3) | copy-start | bytes 393220
  30.3 32.1 %copy-start.1 = (bf16[512,128]{1,0:T(8,128)(2,1)S(1)}, bf16[512,128]{1,0:T(8,128)(2,1)}, u32[]{:S(2)}) copy-start(bf16[512,128]{1,0:T(8,128)(2,1)} %key.3) | copy-start | bytes 393220
  30.3 32.1 %copy-start.2 = (bf16[512,128]{1,0:T(8,128)(2,1)S(1)}, bf16[512,128]{1,0:T(8,128)(2,1)}, u32[]{:S(2)}) copy-start(bf16[512,128]{1,0:T(8,128)(2,1)} %value.3) | copy-start | bytes 393220
  30.3 32.1 %copy-start.3 = (bf16[512,128]{1,0:T(8,128)(2,1)S(1)}, bf16[512,128]{1,0:T(8,128)(2,1)}, u32[]{:S(2)}) copy-start(bf16[512,128]{1,0:T(8,128)(2,1)} %grad.3) | copy-start | bytes 393220
  30.3 32.1 %copy-start.4 = (f32[128]{0:T(128)S(1)}, f32[128]{0:T(128)}, u32[]{:S(2)}) copy-start(f32[128]{0:T(128)} %param.23) | copy-start | bytes 1540
  30.3 2.6 %collective-permute-start.2 = (f32[112,128]{1,0:T(8,128)S(1)}, f32[112,128]{1,0:T(8,128)S(1)}, u32[]{:S(2)}, u32[]{:S(2)}) collective-permute-start(f32[112,128]{1,0:T(8,128)S(1)} %shard_map.218), channel_id=1, source_target_pairs={{0,8},{8,0},{1,9},{9,1},{2,10},{10,2},{3,11},{11,3},{4,12},{12,4},... | collective-permute-start | bytes 172040 | tf_op jit(solution)/shard_map/ppermute | solution.py:495
  32.9 10.2 %collective-permute-start.4 = (f32[40,128]{1,0:T(8,128)S(1)}, f32[40,128]{1,0:T(8,128)S(1)}, u32[]{:S(2)}, u32[]{:S(2)}) collective-permute-start(f32[40,128]{1,0:T(8,128)S(1)} %slice.8), channel_id=1, source_target_pairs={{0,2},{1,3},{2,0},{3,1},{4,6},{5,7},{6,4},{7,5},{8,10},{9,11},{10,... | collective-permute-start | bytes 61448 | tf_op jit(solution)/shard_map/ppermute | solution.py:495
  36.3 6.8 %collective-permute-start.5 = (f32[40,128]{1,0:T(8,128)S(1)}, f32[40,128]{1,0:T(8,128)S(1)}, u32[]{:S(2)}, u32[]{:S(2)}) collective-permute-start(f32[40,128]{1,0:T(8,128)S(1)} %slice.8), channel_id=1, source_target_pairs={{0,3},{1,2},{2,1},{3,0},{4,7},{5,6},{6,5},{7,4},{8,11},{9,10},{10,... | collective-permute-start | bytes 61448 | tf_op jit(solution)/shard_map/ppermute | solution.py:495
  36.3 6.8 %collective-permute-start.3 = (f32[40,128]{1,0:T(8,128)S(1)}, f32[40,128]{1,0:T(8,128)S(1)}, u32[]{:S(2)}, u32[]{:S(2)}) collective-permute-start(f32[40,128]{1,0:T(8,128)S(1)} %slice.8), channel_id=1, source_target_pairs={{0,1},{1,0},{2,3},{3,2},{4,5},{5,4},{6,7},{7,6},{8,9},{9,8},{10,11... | collective-permute-start | bytes 61448 | tf_op jit(solution)/shard_map/ppermute | solution.py:495
  37.9 20.3 %all-to-all-start.1 = ((f32[32,32,128]{2,1,0:T(8,128)}), f32[32,32,128]{2,1,0:T(8,128)S(1)}, u32[]{:S(2)}, u32[]{:S(2)}) async-start(f32[32,32,128]{2,1,0:T(8,128)} %bitcast.3), calls=%async_computation.1 | async-start | bytes 1048576 | tf_op jit(solution)/shard_map/all_to_all | solution.py:521
  43.2 6.2 %collective-permute-start.6 = (f32[40,128]{1,0:T(8,128)S(1)}, f32[40,128]{1,0:T(8,128)S(1)}, u32[]{:S(2)}, u32[]{:S(2)}) collective-permute-start(f32[40,128]{1,0:T(8,128)S(1)} %add_add_fusion.2), channel_id=1, source_target_pairs={{0,6},{1,7},{2,4},{3,5},{4,2},{5,3},{6,0},{7,1},{8,14},{9,15},{10,... | collective-permute-start | bytes 61448 | tf_op jit(solution)/shard_map/ppermute | solution.py:495
  49.3 5.8 %collective-permute-start.8 = (f32[112,128]{1,0:T(8,128)S(1)}, f32[112,128]{1,0:T(8,128)S(1)}, u32[]{:S(2)}, u32[]{:S(2)}) collective-permute-start(f32[112,128]{1,0:T(8,128)S(1)} %pad_maximum_fusion), channel_id=1, source_target_pairs={{0,128},{64,192},{128,0},{192,64},{1,129},{65,193},{129,1},{193,65... | collective-permute-start | bytes 172040 | tf_op jit(solution)/shard_map/ppermute | solution.py:495
  52.7 5.4 %collective-permute-start.9 = (f32[112,128]{1,0:T(8,128)S(1)}, f32[112,128]{1,0:T(8,128)S(1)}, u32[]{:S(2)}, u32[]{:S(2)}) collective-permute-start(f32[112,128]{1,0:T(8,128)S(1)} %pad_maximum_fusion), channel_id=1, source_target_pairs={{0,192},{64,128},{128,64},{192,0},{1,193},{65,129},{129,65},{193,1... | collective-permute-start | bytes 172040 | tf_op jit(solution)/shard_map/ppermute | solution.py:495
  53.9 4.2 %collective-permute-start.7 = (f32[112,128]{1,0:T(8,128)S(1)}, f32[112,128]{1,0:T(8,128)S(1)}, u32[]{:S(2)}, u32[]{:S(2)}) collective-permute-start(f32[112,128]{1,0:T(8,128)S(1)} %pad_maximum_fusion), channel_id=1, source_target_pairs={{0,64},{64,0},{128,192},{192,128},{1,65},{65,1},{129,193},{193,129... | collective-permute-start | bytes 172040 | tf_op jit(solution)/shard_map/ppermute | solution.py:495
  58.1 6.0 %collective-permute-start.11 = (f32[112,128]{1,0:T(8,128)S(1)}, f32[112,128]{1,0:T(8,128)S(1)}, u32[]{:S(2)}, u32[]{:S(2)}) collective-permute-start(f32[112,128]{1,0:T(8,128)S(1)} %add_add_fusion.1), channel_id=1, source_target_pairs={{0,32},{16,48},{32,0},{48,16},{1,33},{17,49},{33,1},{49,17},{2,34}... | collective-permute-start | bytes 172040 | tf_op jit(solution)/shard_map/ppermute | solution.py:495
  61.2 5.4 %collective-permute-start.12 = (f32[112,128]{1,0:T(8,128)S(1)}, f32[112,128]{1,0:T(8,128)S(1)}, u32[]{:S(2)}, u32[]{:S(2)}) collective-permute-start(f32[112,128]{1,0:T(8,128)S(1)} %add_add_fusion.1), channel_id=1, source_target_pairs={{0,48},{16,32},{32,16},{48,0},{1,49},{17,33},{33,17},{49,1},{2,50}... | collective-permute-start | bytes 172040 | tf_op jit(solution)/shard_map/ppermute | solution.py:495
  62.4 4.2 %collective-permute-start.10 = (f32[112,128]{1,0:T(8,128)S(1)}, f32[112,128]{1,0:T(8,128)S(1)}, u32[]{:S(2)}, u32[]{:S(2)}) collective-permute-start(f32[112,128]{1,0:T(8,128)S(1)} %add_add_fusion.1), channel_id=1, source_target_pairs={{0,16},{16,0},{32,48},{48,32},{1,17},{17,1},{33,49},{49,33},{2,18}... | collective-permute-start | bytes 172040 | tf_op jit(solution)/shard_map/ppermute | solution.py:495

commit v8 on v7

--- a/solution.py
+++ b/solution.py
@@ -170,18 +170,11 @@
     )
 
 
-def send_kernel(place, query, key, value, grad, table, sent, features, held, half_held, sems):
-    half = pl.ds(pl.multiple_of(HALF * (place() % 2), HALF), HALF)
-    features_in = pltpu.make_async_copy(table.at[:, half], half_held, sems.at[4])
-    features_out = pltpu.make_async_copy(half_held, features, sems.at[5])
+def send_kernel(query, key, value, grad, sent, held, sems):
     copies = [pltpu.make_async_copy(x, held.at[k], sems.at[k]) for k, x in enumerate((key, value, grad, query))]
     for copy in copies:
         copy.start()
-    features_in.start()
     for offset, first, second in ((0, 0, 1), (OWN, 2, 3)):
-        if offset:
-            features_in.wait()
-            features_out.start()
         copies[first].wait()
         copies[second].wait()
         for h in range(ROWS // SIDE):
@@ -189,7 +182,6 @@
             block = (held[first, rows, :].astype(F32) * held[second, rows, :].astype(F32)).T
             for c in range(OWN):
                 sent[pl.ds(8 * h + offset + c, SEQ, stride=SEQ), :] = block[SEQ * c : SEQ * (c + 1), :]
-    features_out.wait()
 
 
 def receive_kernel(query, key, value, grad, skip, field, output, grad_query, grad_key, grad_value):
@@ -352,7 +344,11 @@
     return jnp.where(lane == place - place % 2 + row // OWN + SEQ * (row % OWN), 1.0, 0.0).astype(F32)
 
 
-def backward_kernel(place, features, hidden, cosines, mine, other, sums, filter_mid, filter_out, grads, d2, d1, shaped):
+def backward_kernel(place, table, hidden, cosines, mine, other, sums, filter_mid, filter_out, grads, d2, d1, shaped,
+                    features, sem):
+    half = pl.ds(pl.multiple_of(HALF * (place() % 2), HALF), HALF)
+    features_copy = pltpu.make_async_copy(table.at[:, half], features, sem)
+    features_copy.start()
     weight3 = picked(filter_out, pair_channels(place())).astype(BF16)
     weight3 = jnp.concatenate([weight3[:64], weight3[:64], weight3[64:]], axis=1)
     weight2 = weight_left(filter_mid[...], 1)
@@ -372,6 +368,7 @@
         d1[:, piece] = jnp.concatenate(
             halves(dot(weight2, jnp.concatenate([rows, rows[:64]])) * cosines[pl.ds(0, 64), piece])
         )
+    features_copy.wait()
     left = jnp.concatenate([hidden[...], d1[...]])
     right = jnp.concatenate([d2[...], shaped[...], features[...]])
     total = dot_nt(left, right)
@@ -406,13 +403,11 @@
     return lax.axis_index(SEQ_AXES)
 
 
-def run_send(query, key, value, grad, place=seq_place, **kw):
-    whole = pl.BlockSpec(memory_space=pl.ANY)
+def run_send(query, key, value, grad, **kw):
     return call(
-        functools.partial(send_kernel, place), 1, [whole] * 5, [spec((1024, SIDE)), whole],
-        [out((1024, SIDE)), pltpu.HBM((32, HALF), BF16)],
-        scratch=[pltpu.VMEM((4, ROWS, SIDE), BF16), pltpu.VMEM((32, HALF), BF16), pltpu.SemaphoreType.DMA((6,))], **kw,
-    )(*[in_hbm(x) for x in (query, key, value, grad, jnp.asarray(feature_table()))])
+        send_kernel, 1, [pl.BlockSpec(memory_space=pltpu.HBM)] * 4, spec((1024, SIDE)), out((1024, SIDE)),
+        scratch=[pltpu.VMEM((4, ROWS, SIDE), BF16), pltpu.SemaphoreType.DMA((4,))], **kw,
+    )(*[in_hbm(x) for x in (query, key, value, grad)])
 
 
 def run_filter(features, filter_in, filter_mid, filter_out, place=seq_place, **kw):
@@ -420,7 +415,7 @@
     return call(
         functools.partial(filter_kernel, place),
         HALF // STEP,
-        [spec((32, STEP), wide), spec((16, ORDER)), spec((ORDER, ORDER)), spec((ORDER, SIDE))],
+        [spec((32, STEP), lambda i: (0, i + HALF // STEP * (place() % 2))), spec((16, ORDER)), spec((ORDER, ORDER)), spec((ORDER, SIDE))],
         [spec((256, STEP), wide), spec((SIDE, STEP), wide)] + [spec((256, SIDE))] * 2,
         [pltpu.HBM((256, HALF), BF16), pltpu.HBM((SIDE, HALF), F32), out((256, SIDE)), out((256, SIDE))],
         scratch=[pltpu.VMEM((512, SIDE), F32)],
@@ -470,12 +465,13 @@
     return call(
         functools.partial(backward_kernel, place),
         1,
-        [held] * 6 + [spec((ORDER, ORDER)), spec((ORDER, SIDE))],
+        [pl.BlockSpec(memory_space=pl.ANY)] + [held] * 5 + [spec((ORDER, ORDER)), spec((ORDER, SIDE))],
         spec((112, SIDE)),
         out((112, SIDE)),
-        scratch=[pltpu.VMEM((SIDE, HALF), BF16)] * 2 + [pltpu.VMEM((16, HALF), BF16)],
+        scratch=[pltpu.VMEM((SIDE, HALF), BF16)] * 2 + [pltpu.VMEM((16, HALF), BF16), pltpu.VMEM((32, HALF), BF16),
+                                                        pltpu.SemaphoreType.DMA],
         flops=4 * 10**9, nbytes=10 * MIB, **kw,
-    )(features, *hidden, mine, other, sums, in_hbm(filter_mid), in_hbm(filter_out))
+    )(in_hbm(features), *hidden, mine, other, sums, in_hbm(filter_mid), in_hbm(filter_out))
 
 
 def run_receive(query, key, value, grad, skip, field, **kw):
@@ -505,7 +501,8 @@
 def body(query, key, value, grad, filter_in, filter_mid, filter_out, decay_rate, skip_gain):
     decay = decay_rate.reshape(1, SIDE)
     skip = skip_gain.reshape(1, SIDE)
-    sent, features = run_send(query, key, value, grad)
+    features = jnp.asarray(feature_table())
+    sent = run_send(query, key, value, grad)
     field = lax.all_to_all(sent.reshape(SEQ, SEQ, SIDE), SEQ_AXES, 0, 0, tiled=True).reshape(1024, SIDE)
     *hidden, mine, theirs = run_filter(features, filter_in, filter_mid, filter_out)
     other = exchanged(theirs, "core", 1)

time: 68.7 us -> 68.5 us (level)
  the two profiles are of different devices: /device:TPU:32 before, /device:TPU:6 now
where the time goes in v8:
time: 68.5 us; the launch traced here: 68.1 us
  starting transfers between devices  34.5 us (50%)
  Pallas kernels  21.7 us (32%)
  waiting for transfers between devices  10.8 us (16%)
  between operations  0.92 us (1%)
    ppermute x13, starting transfers between devices, exchanged(): lax.ppermute(x, axis, [(i, i ^ distance) for i in range(lax.axis_size(axi...  19.5 us
    all_to_all x2, starting transfers between devices, body(): lax.all_to_all(sent.reshape(SEQ, SEQ, SIDE), SEQ_AXES, 0, 0, tiled=True)  15 us
    ppermute x13, waiting for transfers between devices, exchanged(): lax.ppermute(x, axis, [(i, i ^ distance) for i in range(lax.axis_size(axi...  10.8 us
    pallas_call x1, Pallas kernels, run_filter(): call(functools.partial(filter_kernel, place), HALF // STEP, [spec((32, ST...  8.28 us
    pallas_call x1, Pallas kernels, run_backward(): call(functools.partial(backward_kernel, place), 1, [pl.BlockSpec(memory_s...  4.35 us
    pallas_call x1, Pallas kernels, run_send(): call(send_kernel, 1, [pl.BlockSpec(memory_space=pltpu.HBM)] * 4, spec((10...  2.33 us
    pallas_call x1, Pallas kernels, run_convolve(): call(convolve_kernel, 1, [spec((1024, 256)), spec((512, 256)), spec((SIDE...  2.11 us
    pallas_call x1, Pallas kernels, run_correlate(): call(functools.partial(correlate_kernel, place), 1, [spec((1024, SIDE)),...  2.01 us
  transfers between devices with their start and end apart: 15, of which 8 were waited for; matrix products, arithmetic and copies ran while one was open for 0% of the time, Pallas kernels for 18%

profile of v8, /device:TPU:6, one launch (start us, length us, event | category | flops | bytes accessed | tf_op | source)
XLA Modules:
  0.0 68.1 jit_solution(13210821920746986077)
XLA Ops:
  0.6 2.3 %shard_map.215 = f32[1024,128]{1,0:T(8,128)} custom-call(bf16[512,128]{1,0:T(8,128)(2,1)} %query.3, bf16[512,128]{1,0:T(8,128)(2,1)} %key.3, bf16[512,128]{1,0:T(8,128)(2,1)} %value.3, bf16[512,128]{1,0:T(8,128)(2,1)} %grad.3), custom_call_target="tpu_custom_call" | custom-call | flops 1 | bytes 1 | tf_op jit(solution)/shard_map/pallas_call | solution.py:407
  3.0 7.6 %all-to-all-start = ((f32[32,32,128]{2,1,0:T(8,128)}), f32[32,32,128]{2,1,0:T(8,128)S(1)}, u32[]{:S(2)}, u32[]{:S(2)}) async-start(f32[32,32,128]{2,1,0:T(8,128)} %bitcast), calls=%async_computation | async-start | bytes 1048576 | tf_op jit(solution)/shard_map/all_to_all | solution.py:506
  10.6 0.0 copy-start.5
  10.6 0.0 copy-start.6
  10.6 0.0 copy-start.7
  10.6 0.0 copy-start.8
  10.7 0.0 copy-start.9
  10.7 0.0 copy-start.10
  10.7 8.3 %shard_map.214 = (bf16[256,8192]{1,0:T(8,128)(2,1)}, f32[128,8192]{1,0:T(8,128)}, f32[256,128]{1,0:T(8,128)S(1)}, f32[256,128]{1,0:T(8,128)S(1)}) custom-call(bf16[32,16384]{1,0:T(8,128)(2,1)} %constant.12.clone.features.table, f32[16,64]{1,0:T(8,128)} %filter_in.1, f32[64,64]{1,0:T(8,128)} %filter_mid.3, f32[64,128]{1,0:T(8,128)} %filter_out.3), custom_call_target="tpu_custom_call" | custom-call | flops 4000000000 | bytes 10485760 | tf_op jit(solution)/shard_map/pallas_call | solution.py:415
  19.0 0.1 collective-permute-start
  19.1 1.2 %collective-permute-done.shaped_other.other = f32[256,128]{1,0:T(8,128)S(1)} collective-permute-done((f32[256,128]{1,0:T(8,128)S(1)}, f32[256,128]{1,0:T(8,128)S(1)}, u32[]{:S(2)}, u32[]{:S(2)}) %collective-permute-start) | collective-permute-done | bytes 131104 | tf_op jit(solution)/shard_map/ppermute | solution.py:491
  20.3 0.0 all-to-all-done
  20.3 0.0 copy-done.5
  20.3 0.0 copy-done.6
  20.3 0.0 copy-done.7
  20.3 0.0 copy-done.8
  20.3 0.0 copy-done.9
  20.4 0.0 copy-done.10
  20.4 0.0 copy-start.11
  20.4 0.0 copy-start.12
  20.4 2.0 %shard_map.216 = (f32[1024,256]{1,0:T(8,128)S(1)}, f32[512,128]{1,0:T(8,128)S(1)}, f32[512,128]{1,0:T(8,128)S(1)}, f32[16,128]{1,0:T(8,128)S(1)}) custom-call(f32[1024,128]{1,0:T(8,128)S(1)} %bitcast.9, f32[256,128]{1,0:T(8,128)S(1)} %get-tuple-element.38.shaped_mine.mine, f32[256,128]{1,0:T(8,128)S(1)} %collective-permute-done.shaped_other.other, ...), custom_call_target="tpu_custom_call" | custom-call | flops 2000000000 | bytes 4194304 | tf_op jit(solution)/shard_map/pallas_call | solution.py:440
  22.4 0.2 collective-permute-start.1
  22.6 0.8 %shard_map.217.spectrum = f32[512,256]{1,0:T(8,128)S(1)} custom-call(f32[256,128]{1,0:T(8,128)S(1)} %get-tuple-element.38.shaped_mine.mine, f32[256,128]{1,0:T(8,128)S(1)} %collective-permute-done.shaped_other.other, f32[1,128]{1,0:T(1,128)S(1)} %bitcast.12, bf16[256,384]{1,0:T(8,128)(2,1)S(1)} %copy-done.9, bf16[768,256]{1,0:T(8,128)(2,1)S(1)} %copy-done.7, ...), custom_call_target="tpu_custom_call" | custom-call | flops 1000000000 | bytes 1048576 | tf_op jit(solution)/shard_map/pallas_call | solution.py:428
  23.4 0.6 collective-permute-done.1.other
  24.0 0.0 copy-done.11
  24.0 0.0 copy-done.12
  24.0 4.4 %shard_map.218 = f32[112,128]{1,0:T(8,128)S(1)} custom-call(bf16[32,16384]{1,0:T(8,128)(2,1)} %constant.12.clone.features.table, bf16[256,8192]{1,0:T(8,128)(2,1)S(1)} %copy-done.11, f32[128,8192]{1,0:T(8,128)S(1)} %copy-done.12, f32[512,128]{1,0:T(8,128)S(1)} %get-tuple-element.41.mine, f32[512,128]{1,0:T(8,128)S(1)} %collective-permute-done.1.other, ...), custom_call_target="tpu_custom_call" | custom-call | flops 4000000000 | bytes 10485760 | tf_op jit(solution)/shard_map/pallas_call | solution.py:465
  28.4 0.0 copy-start
  28.4 0.0 copy-start.1
  28.4 0.0 copy-start.2
  28.4 0.0 copy-start.3
  28.4 0.0 copy-start.4
  28.4 0.2 collective-permute-start.2
  28.7 2.1 %shard_map.219 = f32[1024,128]{1,0:T(8,128)} custom-call(f32[1024,256]{1,0:T(8,128)S(1)} %get-tuple-element.46.spectra, f32[512,256]{1,0:T(8,128)S(1)} %shard_map.217.spectrum, f32[128,256]{1,0:T(8,128)S(1)} %copy-done.10, bf16[768,256]{1,0:T(8,128)(2,1)S(1)} %copy-done.6, bf16[128,768]{1,0:T(8,128)(2,1)S(1)} %copy-done.8), custom_call_target="tpu_custom_call" | custom-call | flops 2000000000 | bytes 3145728 | tf_op jit(solution)/shard_map/pallas_call | solution.py:453
  30.8 0.0 collective-permute-done.2
  30.8 3.4 %collective-permute-start.4 = (f32[40,128]{1,0:T(8,128)S(1)}, f32[40,128]{1,0:T(8,128)S(1)}, u32[]{:S(2)}, u32[]{:S(2)}) collective-permute-start(f32[40,128]{1,0:T(8,128)S(1)} %slice.8), channel_id=1, source_target_pairs={{0,2},{1,3},{2,0},{3,1},{4,6},{5,7},{6,4},{7,5},{8,10},{9,11},{10,... | collective-permute-start | bytes 61448 | tf_op jit(solution)/shard_map/ppermute | solution.py:491
  34.2 1.5 %collective-permute-start.5 = (f32[40,128]{1,0:T(8,128)S(1)}, f32[40,128]{1,0:T(8,128)S(1)}, u32[]{:S(2)}, u32[]{:S(2)}) collective-permute-start(f32[40,128]{1,0:T(8,128)S(1)} %slice.8), channel_id=1, source_target_pairs={{0,3},{1,2},{2,1},{3,0},{4,7},{5,6},{6,5},{7,4},{8,11},{9,10},{10,... | collective-permute-start | bytes 61448 | tf_op jit(solution)/shard_map/ppermute | solution.py:491
  35.6 0.5 collective-permute-start.3
  36.1 7.4 %all-to-all-start.1 = ((f32[32,32,128]{2,1,0:T(8,128)}), f32[32,32,128]{2,1,0:T(8,128)S(1)}, u32[]{:S(2)}, u32[]{:S(2)}) async-start(f32[32,32,128]{2,1,0:T(8,128)} %bitcast.3), calls=%async_computation.1 | async-start | bytes 1048576 | tf_op jit(solution)/shard_map/all_to_all | solution.py:518
  43.5 0.0 collective-permute-done.4
  43.5 0.0 collective-permute-done.5
  43.5 0.0 collective-permute-done.3
  43.6 5.8 %collective-permute-start.6 = (f32[40,128]{1,0:T(8,128)S(1)}, f32[40,128]{1,0:T(8,128)S(1)}, u32[]{:S(2)}, u32[]{:S(2)}) collective-permute-start(f32[40,128]{1,0:T(8,128)S(1)} %add_add_fusion.2), channel_id=1, source_target_pairs={{0,6},{1,7},{2,4},{3,5},{4,2},{5,3},{6,0},{7,1},{8,14},{9,15},{10,... | collective-permute-start | bytes 61448 | tf_op jit(solution)/shard_map/ppermute | solution.py:491
  49.3 1.8 %collective-permute-done.6 = f32[40,128]{1,0:T(8,128)S(1)} collective-permute-done((f32[40,128]{1,0:T(8,128)S(1)}, f32[40,128]{1,0:T(8,128)S(1)}, u32[]{:S(2)}, u32[]{:S(2)}) %collective-permute-start.6) | collective-permute-done | bytes 20512 | tf_op jit(solution)/shard_map/ppermute | solution.py:491
  51.1 1.5 %collective-permute-start.8 = (f32[112,128]{1,0:T(8,128)S(1)}, f32[112,128]{1,0:T(8,128)S(1)}, u32[]{:S(2)}, u32[]{:S(2)}) collective-permute-start(f32[112,128]{1,0:T(8,128)S(1)} %pad_maximum_fusion), channel_id=1, source_target_pairs={{0,128},{64,192},{128,0},{192,64},{1,129},{65,193},{129,1},{193,65... | collective-permute-start | bytes 172040 | tf_op jit(solution)/shard_map/ppermute | solution.py:491
  52.6 2.1 %collective-permute-start.9 = (f32[112,128]{1,0:T(8,128)S(1)}, f32[112,128]{1,0:T(8,128)S(1)}, u32[]{:S(2)}, u32[]{:S(2)}) collective-permute-start(f32[112,128]{1,0:T(8,128)S(1)} %pad_maximum_fusion), channel_id=1, source_target_pairs={{0,192},{64,128},{128,64},{192,0},{1,193},{65,129},{129,65},{193,1... | collective-permute-start | bytes 172040 | tf_op jit(solution)/shard_map/ppermute | solution.py:491
  54.7 0.0 collective-permute-start.7
  54.7 2.5 %collective-permute-done.8 = f32[112,128]{1,0:T(8,128)S(1)} collective-permute-done((f32[112,128]{1,0:T(8,128)S(1)}, f32[112,128]{1,0:T(8,128)S(1)}, u32[]{:S(2)}, u32[]{:S(2)}) %collective-permute-start.8) | collective-permute-done | bytes 57376 | tf_op jit(solution)/shard_map/ppermute | solution.py:491
  57.1 0.9 %collective-permute-done.9 = f32[112,128]{1,0:T(8,128)S(1)} collective-permute-done((f32[112,128]{1,0:T(8,128)S(1)}, f32[112,128]{1,0:T(8,128)S(1)}, u32[]{:S(2)}, u32[]{:S(2)}) %collective-permute-start.9) | collective-permute-done | bytes 57376 | tf_op jit(solution)/shard_map/ppermute | solution.py:491
  58.0 0.9 %collective-permute-done.7 = f32[112,128]{1,0:T(8,128)S(1)} collective-permute-done((f32[112,128]{1,0:T(8,128)S(1)}, f32[112,128]{1,0:T(8,128)S(1)}, u32[]{:S(2)}, u32[]{:S(2)}) %collective-permute-start.7) | collective-permute-done | bytes 57376 | tf_op jit(solution)/shard_map/ppermute | solution.py:491
  58.9 0.0 all-to-all-done.1
  58.9 3.1 %collective-permute-start.11 = (f32[112,128]{1,0:T(8,128)S(1)}, f32[112,128]{1,0:T(8,128)S(1)}, u32[]{:S(2)}, u32[]{:S(2)}) collective-permute-start(f32[112,128]{1,0:T(8,128)S(1)} %add_add_fusion.1), channel_id=1, source_target_pairs={{0,32},{16,48},{32,0},{48,16},{1,33},{17,49},{33,1},{49,17},{2,34}... | collective-permute-start | bytes 172040 | tf_op jit(solution)/shard_map/ppermute | solution.py:491
  61.9 1.2 %collective-permute-start.12 = (f32[112,128]{1,0:T(8,128)S(1)}, f32[112,128]{1,0:T(8,128)S(1)}, u32[]{:S(2)}, u32[]{:S(2)}) collective-permute-start(f32[112,128]{1,0:T(8,128)S(1)} %add_add_fusion.1), channel_id=1, source_target_pairs={{0,48},{16,32},{32,16},{48,0},{1,49},{17,33},{33,17},{49,1},{2,50}... | collective-permute-start | bytes 172040 | tf_op jit(solution)/shard_map/ppermute | solution.py:491
  63.1 0.0 collective-permute-start.10
  63.1 0.0 copy-done
  63.1 0.0 copy-done.1
  63.1 0.0 copy-done.2
  63.1 0.0 copy-done.3
  63.1 0.0 copy-done.4
  63.1 1.2 %shard_map.220 = (bf16[512,128]{1,0:T(8,128)(2,1)}, bf16[512,128]{1,0:T(8,128)(2,1)}, bf16[512,128]{1,0:T(8,128)(2,1)}, bf16[512,128]{1,0:T(8,128)(2,1)}) custom-call(bf16[512,128]{1,0:T(8,128)(2,1)S(1)} %copy-done, bf16[512,128]{1,0:T(8,128)(2,1)S(1)} %copy-done.1, bf16[512,128]{1,0:T(8,128)(2,1)S(1)} %copy-done.2, bf16[512,128]{1,0:T(8,128)(2,1)S(1)} %copy-done.3, ...), custom_call_target="tpu_custom_call" | custom-call | flops 1 | bytes 1 | tf_op jit(solution)/shard_map/pallas_call | solution.py:479
  64.3 0.6 collective-permute-done.11
  64.9 2.5 %collective-permute-done.12 = f32[112,128]{1,0:T(8,128)S(1)} collective-permute-done((f32[112,128]{1,0:T(8,128)S(1)}, f32[112,128]{1,0:T(8,128)S(1)}, u32[]{:S(2)}, u32[]{:S(2)}) %collective-permute-start.12) | collective-permute-done | bytes 57376 | tf_op jit(solution)/shard_map/ppermute | solution.py:491
  67.3 0.0 collective-permute-done.10
  67.4 0.7 %shard_map.221 = (f32[16,64]{1,0:T(8,128)}, f32[64,64]{1,0:T(8,128)}, f32[64,128]{1,0:T(8,128)}, f32[1,128]{1,0:T(1,128)}, f32[1,128]{1,0:T(1,128)}) custom-call(f32[112,128]{1,0:T(8,128)S(1)} %add_add_fusion.total), custom_call_target="tpu_custom_call" | custom-call | flops 1 | bytes 1 | tf_op jit(solution)/shard_map/pallas_call | solution.py:485
  (8 shorter events, 0.1 us)
Async XLA Ops:
  3.0 17.3 %all-to-all-start = ((f32[32,32,128]{2,1,0:T(8,128)}), f32[32,32,128]{2,1,0:T(8,128)S(1)}, u32[]{:S(2)}, u32[]{:S(2)}) async-start(f32[32,32,128]{2,1,0:T(8,128)} %bitcast), calls=%async_computation | async-start | bytes 1048576 | tf_op jit(solution)/shard_map/all_to_all | solution.py:506
  10.6 9.7 %copy-start.5 = (f32[128]{0:T(128)S(1)}, f32[128]{0:T(128)}, u32[]{:S(2)}) copy-start(f32[128]{0:T(128)} %param.22) | copy-start | bytes 1540
  10.6 9.7 %copy-start.6 = (bf16[768,256]{1,0:T(8,128)(2,1)S(1)}, bf16[768,256]{1,0:T(8,128)(2,1)}, u32[]{:S(2)}) copy-start(bf16[768,256]{1,0:T(8,128)(2,1)} %constant.16.clone.second_inv) | copy-start | bytes 1179652
  10.6 9.7 %copy-start.7 = (bf16[768,256]{1,0:T(8,128)(2,1)S(1)}, bf16[768,256]{1,0:T(8,128)(2,1)}, u32[]{:S(2)}) copy-start(bf16[768,256]{1,0:T(8,128)(2,1)} %constant.14.clone.second_fwd) | copy-start | bytes 1179652
  10.6 9.7 %copy-start.8 = (bf16[128,768]{1,0:T(8,128)(2,1)S(1)}, bf16[128,768]{1,0:T(8,128)(2,1)}, u32[]{:S(2)}) copy-start(bf16[128,768]{1,0:T(8,128)(2,1)} %constant.17.clone.first_inv) | copy-start | bytes 589828
  10.7 9.7 %copy-start.9 = (bf16[256,384]{1,0:T(8,128)(2,1)S(1)}, bf16[256,384]{1,0:T(8,128)(2,1)}, u32[]{:S(2)}) copy-start(bf16[256,384]{1,0:T(8,128)(2,1)} %constant.13.clone.first_fwd) | copy-start | bytes 589828
  10.7 9.7 %copy-start.10 = (f32[128,256]{1,0:T(8,128)S(1)}, f32[128,256]{1,0:T(8,128)}, u32[]{:S(2)}) copy-start(f32[128,256]{1,0:T(8,128)} %constant.15.clone.twiddle) | copy-start | bytes 393220
  19.0 1.3 %collective-permute-start = (f32[256,128]{1,0:T(8,128)S(1)}, f32[256,128]{1,0:T(8,128)S(1)}, u32[]{:S(2)}, u32[]{:S(2)}) collective-permute-start(f32[256,128]{1,0:T(8,128)S(1)} %get-tuple-element.39), channel_id=1, source_target_pairs={{0,8},{8,0},{1,9},{9,1},{2,10},{10,2},{3,11},{11,3},{4,12},{12,4},... | collective-permute-start | bytes 393224 | tf_op jit(solution)/shard_map/ppermute | solution.py:491
  20.4 3.7 %copy-start.11 = (bf16[256,8192]{1,0:T(8,128)(2,1)S(1)}, bf16[256,8192]{1,0:T(8,128)(2,1)}, u32[]{:S(2)}) copy-start(bf16[256,8192]{1,0:T(8,128)(2,1)} %get-tuple-element.36.hidden) | copy-start | bytes 12582916
  20.4 3.7 %copy-start.12 = (f32[128,8192]{1,0:T(8,128)S(1)}, f32[128,8192]{1,0:T(8,128)}, u32[]{:S(2)}) copy-start(f32[128,8192]{1,0:T(8,128)} %get-tuple-element.37.cosines) | copy-start | bytes 12582916
  22.4 1.6 %collective-permute-start.1 = (f32[512,128]{1,0:T(8,128)S(1)}, f32[512,128]{1,0:T(8,128)S(1)}, u32[]{:S(2)}, u32[]{:S(2)}) collective-permute-start(f32[512,128]{1,0:T(8,128)S(1)} %get-tuple-element.42), channel_id=1, source_target_pairs={{0,8},{8,0},{1,9},{9,1},{2,10},{10,2},{3,11},{11,3},{4,12},{12,4},... | collective-permute-start | bytes 786440 | tf_op jit(solution)/shard_map/ppermute | solution.py:491
  28.4 34.7 %copy-start = (bf16[512,128]{1,0:T(8,128)(2,1)S(1)}, bf16[512,128]{1,0:T(8,128)(2,1)}, u32[]{:S(2)}) copy-start(bf16[512,128]{1,0:T(8,128)(2,1)} %query.3) | copy-start | bytes 393220
  28.4 34.7 %copy-start.1 = (bf16[512,128]{1,0:T(8,128)(2,1)S(1)}, bf16[512,128]{1,0:T(8,128)(2,1)}, u32[]{:S(2)}) copy-start(bf16[512,128]{1,0:T(8,128)(2,1)} %key.3) | copy-start | bytes 393220
  28.4 34.7 %copy-start.2 = (bf16[512,128]{1,0:T(8,128)(2,1)S(1)}, bf16[512,128]{1,0:T(8,128)(2,1)}, u32[]{:S(2)}) copy-start(bf16[512,128]{1,0:T(8,128)(2,1)} %value.3) | copy-start | bytes 393220
  28.4 34.7 %copy-start.3 = (bf16[512,128]{1,0:T(8,128)(2,1)S(1)}, bf16[512,128]{1,0:T(8,128)(2,1)}, u32[]{:S(2)}) copy-start(bf16[512,128]{1,0:T(8,128)(2,1)} %grad.3) | copy-start | bytes 393220
  28.4 34.7 %copy-start.4 = (f32[128]{0:T(128)S(1)}, f32[128]{0:T(128)}, u32[]{:S(2)}) copy-start(f32[128]{0:T(128)} %param.23) | copy-start | bytes 1540
  28.4 2.4 %collective-permute-start.2 = (f32[112,128]{1,0:T(8,128)S(1)}, f32[112,128]{1,0:T(8,128)S(1)}, u32[]{:S(2)}, u32[]{:S(2)}) collective-permute-start(f32[112,128]{1,0:T(8,128)S(1)} %shard_map.218), channel_id=1, source_target_pairs={{0,8},{8,0},{1,9},{9,1},{2,10},{10,2},{3,11},{11,3},{4,12},{12,4},... | collective-permute-start | bytes 172040 | tf_op jit(solution)/shard_map/ppermute | solution.py:491
  30.8 12.7 %collective-permute-start.4 = (f32[40,128]{1,0:T(8,128)S(1)}, f32[40,128]{1,0:T(8,128)S(1)}, u32[]{:S(2)}, u32[]{:S(2)}) collective-permute-start(f32[40,128]{1,0:T(8,128)S(1)} %slice.8), channel_id=1, source_target_pairs={{0,2},{1,3},{2,0},{3,1},{4,6},{5,7},{6,4},{7,5},{8,10},{9,11},{10,... | collective-permute-start | bytes 61448 | tf_op jit(solution)/shard_map/ppermute | solution.py:491
  34.2 9.3 %collective-permute-start.5 = (f32[40,128]{1,0:T(8,128)S(1)}, f32[40,128]{1,0:T(8,128)S(1)}, u32[]{:S(2)}, u32[]{:S(2)}) collective-permute-start(f32[40,128]{1,0:T(8,128)S(1)} %slice.8), channel_id=1, source_target_pairs={{0,3},{1,2},{2,1},{3,0},{4,7},{5,6},{6,5},{7,4},{8,11},{9,10},{10,... | collective-permute-start | bytes 61448 | tf_op jit(solution)/shard_map/ppermute | solution.py:491
  35.6 7.9 %collective-permute-start.3 = (f32[40,128]{1,0:T(8,128)S(1)}, f32[40,128]{1,0:T(8,128)S(1)}, u32[]{:S(2)}, u32[]{:S(2)}) collective-permute-start(f32[40,128]{1,0:T(8,128)S(1)} %slice.8), channel_id=1, source_target_pairs={{0,1},{1,0},{2,3},{3,2},{4,5},{5,4},{6,7},{7,6},{8,9},{9,8},{10,11... | collective-permute-start | bytes 61448 | tf_op jit(solution)/shard_map/ppermute | solution.py:491
  36.1 22.8 %all-to-all-start.1 = ((f32[32,32,128]{2,1,0:T(8,128)}), f32[32,32,128]{2,1,0:T(8,128)S(1)}, u32[]{:S(2)}, u32[]{:S(2)}) async-start(f32[32,32,128]{2,1,0:T(8,128)} %bitcast.3), calls=%async_computation.1 | async-start | bytes 1048576 | tf_op jit(solution)/shard_map/all_to_all | solution.py:518
  43.6 7.5 %collective-permute-start.6 = (f32[40,128]{1,0:T(8,128)S(1)}, f32[40,128]{1,0:T(8,128)S(1)}, u32[]{:S(2)}, u32[]{:S(2)}) collective-permute-start(f32[40,128]{1,0:T(8,128)S(1)} %add_add_fusion.2), channel_id=1, source_target_pairs={{0,6},{1,7},{2,4},{3,5},{4,2},{5,3},{6,0},{7,1},{8,14},{9,15},{10,... | collective-permute-start | bytes 61448 | tf_op jit(solution)/shard_map/ppermute | solution.py:491
  51.1 6.0 %collective-permute-start.8 = (f32[112,128]{1,0:T(8,128)S(1)}, f32[112,128]{1,0:T(8,128)S(1)}, u32[]{:S(2)}, u32[]{:S(2)}) collective-permute-start(f32[112,128]{1,0:T(8,128)S(1)} %pad_maximum_fusion), channel_id=1, source_target_pairs={{0,128},{64,192},{128,0},{192,64},{1,129},{65,193},{129,1},{193,65... | collective-permute-start | bytes 172040 | tf_op jit(solution)/shard_map/ppermute | solution.py:491
  52.6 5.4 %collective-permute-start.9 = (f32[112,128]{1,0:T(8,128)S(1)}, f32[112,128]{1,0:T(8,128)S(1)}, u32[]{:S(2)}, u32[]{:S(2)}) collective-permute-start(f32[112,128]{1,0:T(8,128)S(1)} %pad_maximum_fusion), channel_id=1, source_target_pairs={{0,192},{64,128},{128,64},{192,0},{1,193},{65,129},{129,65},{193,1... | collective-permute-start | bytes 172040 | tf_op jit(solution)/shard_map/ppermute | solution.py:491
  54.7 4.2 %collective-permute-start.7 = (f32[112,128]{1,0:T(8,128)S(1)}, f32[112,128]{1,0:T(8,128)S(1)}, u32[]{:S(2)}, u32[]{:S(2)}) collective-permute-start(f32[112,128]{1,0:T(8,128)S(1)} %pad_maximum_fusion), channel_id=1, source_target_pairs={{0,64},{64,0},{128,192},{192,128},{1,65},{65,1},{129,193},{193,129... | collective-permute-start | bytes 172040 | tf_op jit(solution)/shard_map/ppermute | solution.py:491
  58.9 6.0 %collective-permute-start.11 = (f32[112,128]{1,0:T(8,128)S(1)}, f32[112,128]{1,0:T(8,128)S(1)}, u32[]{:S(2)}, u32[]{:S(2)}) collective-permute-start(f32[112,128]{1,0:T(8,128)S(1)} %add_add_fusion.1), channel_id=1, source_target_pairs={{0,32},{16,48},{32,0},{48,16},{1,33},{17,49},{33,1},{49,17},{2,34}... | collective-permute-start | bytes 172040 | tf_op jit(solution)/shard_map/ppermute | solution.py:491
  61.9 5.4 %collective-permute-start.12 = (f32[112,128]{1,0:T(8,128)S(1)}, f32[112,128]{1,0:T(8,128)S(1)}, u32[]{:S(2)}, u32[]{:S(2)}) collective-permute-start(f32[112,128]{1,0:T(8,128)S(1)} %add_add_fusion.1), channel_id=1, source_target_pairs={{0,48},{16,32},{32,16},{48,0},{1,49},{17,33},{33,17},{49,1},{2,50}... | collective-permute-start | bytes 172040 | tf_op jit(solution)/shard_map/ppermute | solution.py:491
  63.1 4.2 %collective-permute-start.10 = (f32[112,128]{1,0:T(8,128)S(1)}, f32[112,128]{1,0:T(8,128)S(1)}, u32[]{:S(2)}, u32[]{:S(2)}) collective-permute-start(f32[112,128]{1,0:T(8,128)S(1)} %add_add_fusion.1), channel_id=1, source_target_pairs={{0,16},{16,0},{32,48},{48,32},{1,17},{17,1},{33,49},{49,33},{2,18}... | collective-permute-start | bytes 172040 | tf_op jit(solution)/shard_map/ppermute | solution.py:491
